TPU v7x, 32 devices: a whole 2x2x4 slice. The times are simulated.
32 devices in a mesh: batch: 16 (over z, x, core), tensor: 2 (over y).
Axes of the slice: x: 2, y: 2, z: 4, core: 2. Of those that a mesh axis runs over, the one named last changes fastest.
Arguments:
- inputs: bfloat16 [32, 1024, 1024], P(('batch', 'tensor')), may hold values from -6 to 6
- counts: int32 [16], P('batch'), may hold values from 1 to 2, as said below
- ln1_gain: bfloat16 [1024], replicated, may hold values from 0.099609375 to 1.8984375
- ln1_bias: bfloat16 [1024], replicated, may hold values from -1.1953125 to 1.1953125
- log_dt: float32 [1024], P('tensor'), may hold values from -6.9 to -2.3
- log_a: float32 [1024, 32], P('tensor'), may hold values from -1 to 1
- freq: float32 [1024, 32], P('tensor'), may hold values from 0 to 100
- c_real: float32 [1024, 32], P('tensor'), may hold values from -3 to 3
- c_imag: float32 [1024, 32], P('tensor'), may hold values from -3 to 3
- skip_gain: float32 [1024], P('tensor'), may hold values from -4 to 4
- w_value: bfloat16 [1024, 1024], P(None, 'tensor'), may hold values from -0.375 to 0.375
- w_gate: bfloat16 [1024, 1024], P(None, 'tensor'), may hold values from -0.1875 to 0.1875
- ln2_gain: bfloat16 [1024], replicated, may hold values from 0.099609375 to 1.8984375
- ln2_bias: bfloat16 [1024], replicated, may hold values from -1.1953125 to 1.1953125
- w_in: bfloat16 [1024, 4096], P(None, 'tensor'), may hold values from -0.1875 to 0.1875
- w_out: bfloat16 [4096, 1024], P('tensor'), may hold values from -0.125 to 0.125
- cotangent: bfloat16 [32, 1024, 1024], P(('batch', 'tensor')), may hold values from -6 to 6
Outputs:
- output: bfloat16 [32, 1024, 1024], P(('batch', 'tensor'))
- input_grad: bfloat16 [32, 1024, 1024], P(('batch', 'tensor'))
- ln1_gain_grad: float32 [1024], P('tensor')
- ln1_bias_grad: float32 [1024], P('tensor')
- log_dt_grad: float32 [1024], P('tensor')
- log_a_grad: float32 [1024, 32], P('tensor')
- freq_grad: float32 [1024, 32], P('tensor')
- c_real_grad: float32 [1024, 32], P('tensor')
- c_imag_grad: float32 [1024, 32], P('tensor')
- skip_grad: float32 [1024], P('tensor')
- w_value_grad: float32 [1024, 1024], P(None, 'tensor')
- w_gate_grad: float32 [1024, 1024], P(None, 'tensor')
- ln2_gain_grad: float32 [1024], P('tensor')
- ln2_bias_grad: float32 [1024], P('tensor')
- w_in_grad: float32 [1024, 4096], P(None, 'tensor')
- w_out_grad: float32 [4096, 1024], P('tensor')
Inputs may be any that keep to these rules, and one draw needn't show every extreme that they name: Slot t of batch shard b (sequence b * 2 + t) is used when t < counts[b]; some shard uses all 2 slots and some only one.
All inputs are finite; a program needn't handle non-finite values.
Results may differ from a plain program's by a relative error of at most 0.013.
Values may be sent and summed in bfloat16 or wider, within the bound.
A program may use at most 256 MiB of HBM per device.

v0:
```python
import jax
import jax.numpy as jnp
from jax import lax
from jax.sharding import PartitionSpec as P

norm_eps = 1e-05


def kernel_of(log_dt, log_a, freq, c_real, c_imag, length):
    channels, modes = log_a.shape
    group_size = min(4, modes)
    group_count = modes // group_size
    time_step = jnp.exp(log_dt)[:, None]
    positions = jnp.arange(length).astype(jnp.float32)

    def stacked(values):
        return values.reshape(channels, group_count, group_size).transpose(1, 0, 2)

    def add_group(running, pieces):
        rate_part, turn_part, real_part, imag_part = pieces
        decay_rate = time_step * rate_part
        decayed = jnp.exp(-decay_rate[:, :, None] * positions)
        angles = (time_step * turn_part)[:, :, None] * positions
        summands = decayed * (
            real_part[:, :, None] * jnp.cos(angles) - imag_part[:, :, None] * jnp.sin(angles)
        )
        return (running + jnp.sum(summands, axis=1), None)

    start_value = jnp.zeros((channels, length), jnp.float32)
    running, _ = lax.scan(
        jax.checkpoint(add_group),
        start_value,
        (stacked(jnp.exp(log_a)), stacked(freq), stacked(c_real), stacked(c_imag)),
    )
    return 2.0 * time_step * running


def causal_conv(signal, kernel):
    length = signal.shape[1]
    flipped = kernel.T[::-1][:, None, :]
    return lax.conv_general_dilated(
        signal,
        flipped,
        (1,),
        [(length - 1, 0)],
        dimension_numbers=("NHC", "HIO", "NHC"),
        feature_group_count=signal.shape[2],
    )


def rounded(values):
    return lax.optimization_barrier(values.astype(jnp.bfloat16)).astype(jnp.float32)


def norm_forward(values, norm_gain, norm_bias):
    center = values - jnp.mean(values, axis=-1, keepdims=True)
    inv_std = lax.rsqrt(jnp.mean(center * center, axis=-1, keepdims=True) + norm_eps)
    standard = center * inv_std
    return (standard * norm_gain + norm_bias, standard, inv_std)


def norm_backward(incoming, standard, inv_std, norm_gain):
    scaled = incoming * norm_gain
    value_grad = inv_std * (
        scaled
        - jnp.mean(scaled, axis=-1, keepdims=True)
        - standard * jnp.mean(scaled * standard, axis=-1, keepdims=True)
    )
    return (value_grad, jnp.sum(incoming * standard, axis=0), jnp.sum(incoming, axis=0))


def matmul(left, right):
    return jnp.dot(left, right, preferred_element_type=jnp.float32)


def contract_rows(left, right):
    return lax.dot_general(
        left, right, (((0,), (0,)), ((), ())), preferred_element_type=jnp.float32
    )


def contract_cols(left, right):
    return lax.dot_general(
        left, right, (((1,), (1,)), ((), ())), preferred_element_type=jnp.float32
    )


def shards(
    inputs,
    counts,
    ln1_gain,
    ln1_bias,
    log_dt,
    log_a,
    freq,
    c_real,
    c_imag,
    skip_gain,
    w_value,
    w_gate,
    ln2_gain,
    ln2_bias,
    w_in,
    w_out,
    cotangent,
):
    seqs_here, length, model_width = inputs.shape
    row_count = seqs_here * length
    used_flag = (lax.axis_index("tensor") < counts[0]).astype(jnp.float32)
    source = inputs.reshape(row_count, model_width).astype(jnp.float32)
    gain_first = ln1_gain.astype(jnp.float32)
    bias_first = ln1_bias.astype(jnp.float32)
    gain_second = ln2_gain.astype(jnp.float32)
    bias_second = ln2_bias.astype(jnp.float32)
    params = (
        lax.all_gather(log_dt, "tensor", axis=0, tiled=True),
        lax.all_gather(log_a, "tensor", axis=0, tiled=True),
        lax.all_gather(freq, "tensor", axis=0, tiled=True),
        lax.all_gather(c_real, "tensor", axis=0, tiled=True),
        lax.all_gather(c_imag, "tensor", axis=0, tiled=True),
        lax.all_gather(skip_gain, "tensor", axis=0, tiled=True),
    )
    direct = params[5]
    normed1_full, standard1, inv_std1 = norm_forward(source, gain_first, bias_first)
    normed1 = rounded(normed1_full)
    kernel, kernel_back = jax.vjp(
        lambda a, b, c, d, e: kernel_of(a, b, c, d, e, length),
        params[0],
        params[1],
        params[2],
        params[3],
        params[4],
    )
    kernel_low = rounded(kernel)
    normed_seqs = normed1.reshape(seqs_here, length, model_width)
    conv_out, conv_back = jax.vjp(causal_conv, normed_seqs, kernel_low)
    mixed = conv_out.reshape(row_count, model_width) + direct * normed1
    activated, gelu_back = jax.vjp(jax.nn.gelu, mixed)
    act_low = activated.astype(jnp.bfloat16)
    act_all = lax.all_gather(act_low, "tensor", axis=0, tiled=True)
    both_w = jnp.concatenate([w_value, w_gate], axis=1)
    both_proj = matmul(act_all, both_w)
    half_cols = both_proj.shape[1] // 2
    value_proj = both_proj[:, :half_cols]
    gate_proj = both_proj[:, half_cols:]
    gate_sig = jax.nn.sigmoid(gate_proj)
    glu_low = (value_proj * gate_sig).astype(jnp.bfloat16)
    glu_rows = lax.all_to_all(glu_low, "tensor", split_axis=0, concat_axis=1, tiled=True)
    residual = source + glu_rows.astype(jnp.float32)
    normed2_full, standard2, inv_std2 = norm_forward(residual, gain_second, bias_second)
    normed2 = normed2_full.astype(jnp.bfloat16)
    normed_all = lax.all_gather(normed2, "tensor", axis=0, tiled=True)
    pre_act = matmul(normed_all, w_in)
    hidden_full, gelu_second_back = jax.vjp(jax.nn.gelu, pre_act)
    hidden = hidden_full.astype(jnp.bfloat16)
    ffn_out = lax.psum_scatter(
        matmul(
            lax.slice_in_dim(hidden, 0, row_count * lax.axis_size("tensor"), axis=0), w_out
        ).astype(jnp.bfloat16),
        "tensor",
        scatter_dimension=0,
        tiled=True,
    ).astype(jnp.float32)
    output = (used_flag * (residual + ffn_out)).astype(jnp.bfloat16).reshape(inputs.shape)
    grad_out = used_flag * cotangent.reshape(row_count, model_width).astype(jnp.float32)
    grad_low = grad_out.astype(jnp.bfloat16)
    grad_all = lax.all_gather(grad_low, "tensor", axis=0, tiled=True)
    grad_hidden = contract_cols(grad_all, w_out)
    out_grad = contract_rows(hidden, grad_all)
    grad_pre = gelu_second_back(grad_hidden)[0].astype(jnp.bfloat16)
    in_grad = contract_rows(normed_all, grad_pre)
    grad_normed2 = lax.psum_scatter(
        contract_cols(
            lax.slice_in_dim(grad_pre, 0, row_count * lax.axis_size("tensor"), axis=0), w_in
        ),
        "tensor",
        scatter_dimension=0,
        tiled=True,
    )
    grad_resid_part, gain_second_grad, bias_second_grad = norm_backward(
        grad_normed2, standard2, inv_std2, gain_second
    )
    grad_residual = grad_out + grad_resid_part
    grad_glu_rows = grad_residual.astype(jnp.bfloat16)
    grad_glu = lax.all_to_all(grad_glu_rows, "tensor", split_axis=1, concat_axis=0, tiled=True)
    grad_glu_full = grad_glu.astype(jnp.float32)
    grad_value = (grad_glu_full * gate_sig).astype(jnp.bfloat16)
    grad_gate = (grad_glu_full * value_proj * gate_sig * (1.0 - gate_sig)).astype(jnp.bfloat16)
    grad_both = jnp.concatenate([grad_value, grad_gate], axis=1)
    both_grad = contract_rows(act_all, grad_both)
    value_grad = both_grad[:, :half_cols]
    gate_grad = both_grad[:, half_cols:]
    grad_act = lax.psum_scatter(
        contract_cols(
            lax.slice_in_dim(grad_both, 0, row_count * lax.axis_size("tensor"), axis=0), both_w
        ),
        "tensor",
        scatter_dimension=0,
        tiled=True,
    )
    grad_mixed = gelu_back(grad_act)[0]
    grad_conv = rounded(grad_mixed)
    conv_grads = conv_back(grad_conv.reshape(seqs_here, length, model_width))
    grad_normed1 = conv_grads[0].reshape(row_count, model_width) + direct * grad_mixed
    skip_grad = jnp.sum(grad_mixed * normed1, axis=0)
    kernel_grads = kernel_back(conv_grads[1])
    grad_source, gain_first_grad, bias_first_grad = norm_backward(
        grad_normed1, standard1, inv_std1, gain_first
    )
    input_grad = (grad_residual + grad_source).astype(jnp.bfloat16).reshape(inputs.shape)
    shares = (
        lax.psum_scatter(
            kernel_grads[0].astype(jnp.bfloat16), "tensor", scatter_dimension=0, tiled=True
        ).astype(jnp.float32),
        lax.psum_scatter(
            kernel_grads[1].astype(jnp.bfloat16), "tensor", scatter_dimension=0, tiled=True
        ).astype(jnp.float32),
        lax.psum_scatter(
            kernel_grads[2].astype(jnp.bfloat16), "tensor", scatter_dimension=0, tiled=True
        ).astype(jnp.float32),
        lax.psum_scatter(
            kernel_grads[3].astype(jnp.bfloat16), "tensor", scatter_dimension=0, tiled=True
        ).astype(jnp.float32),
        lax.psum_scatter(
            kernel_grads[4].astype(jnp.bfloat16), "tensor", scatter_dimension=0, tiled=True
        ).astype(jnp.float32),
        lax.psum_scatter(
            skip_grad.astype(jnp.bfloat16), "tensor", scatter_dimension=0, tiled=True
        ).astype(jnp.float32),
        lax.psum_scatter(
            gain_first_grad.astype(jnp.bfloat16), "tensor", scatter_dimension=0, tiled=True
        ).astype(jnp.float32),
        lax.psum_scatter(
            bias_first_grad.astype(jnp.bfloat16), "tensor", scatter_dimension=0, tiled=True
        ).astype(jnp.float32),
        lax.psum_scatter(
            gain_second_grad.astype(jnp.bfloat16), "tensor", scatter_dimension=0, tiled=True
        ).astype(jnp.float32),
        lax.psum_scatter(
            bias_second_grad.astype(jnp.bfloat16), "tensor", scatter_dimension=0, tiled=True
        ).astype(jnp.float32),
    )
    value_share, gate_share, in_share, out_share = (value_grad, gate_grad, in_grad, out_grad)
    totals = lax.psum(
        (
            shares[0],
            shares[1],
            shares[2],
            shares[3],
            shares[4],
            shares[5],
            shares[6],
            shares[7],
            shares[8],
            shares[9],
            value_share,
            gate_share,
            in_share,
            out_share,
        ),
        "batch",
    )
    return (
        output,
        input_grad,
        totals[6],
        totals[7],
        totals[0],
        totals[1],
        totals[2],
        totals[3],
        totals[4],
        totals[5],
        totals[10],
        totals[11],
        totals[8],
        totals[9],
        totals[12],
        totals[13],
    )


def solution(mesh):
    in_specs = (
        P(("batch", "tensor"), None, None),
        P("batch"),
        P(),
        P(),
        P("tensor"),
        P("tensor", None),
        P("tensor", None),
        P("tensor", None),
        P("tensor", None),
        P("tensor"),
        P(None, "tensor"),
        P(None, "tensor"),
        P(),
        P(),
        P(None, "tensor"),
        P("tensor", None),
        P(("batch", "tensor"), None, None),
    )
    out_specs = (
        P(("batch", "tensor"), None, None),
        P(("batch", "tensor"), None, None),
        P("tensor"),
        P("tensor"),
        P("tensor"),
        P("tensor", None),
        P("tensor", None),
        P("tensor", None),
        P("tensor", None),
        P("tensor"),
        P(None, "tensor"),
        P(None, "tensor"),
        P("tensor"),
        P("tensor"),
        P(None, "tensor"),
        P("tensor", None),
    )
    return jax.shard_map(shards, mesh=mesh, in_specs=in_specs, out_specs=out_specs, check_vma=False)
```

profile of v0, /device:TPU:0, one launch (start us, length us, event | category | flops | bytes accessed | tf_op | source)
XLA Modules:
  0.0 6791.5 jit_solution(3656420200459139322)
XLA Ops:
  47.5 544.4 %while.39 = (s32[]{:T(128)}, f32[1024,1024]{1,0:T(8,128)}, f32[1024,1]{0,1:T(1,128)S(1)}, f32[8,1024,4]{1,2,0:T(4,128)S(1)}, f32[8,1024,4]{1,2,0:T(4,128)S(1)}, ...) while((s32[]{:T(128)}, f32[1024,1024]{1,0:T(8,128)}, ...), condition=%wide.region_4.5_spmd.clone.clone, body=%wide.region_2.4_spmd.clone.clone.sunk | while | flops 30422016 | bytes 50540716 | solution.py:30
  47.7 64.4 fusion.120
  115.7 64.4 fusion.120
  183.8 64.4 fusion.120
  251.8 64.4 fusion.120
  319.8 64.4 fusion.120
  387.9 64.4 fusion.120
  455.9 64.4 fusion.120
  523.9 64.4 fusion.120
  601.8 30.5 rev.7
  632.3 845.0 %fusion.73 = f32[1,1024,1024]{2,0,1:T(1,128)S(1)} fusion(bf16[1024,1,1024]{2,0,1:T(8,128)(2,1)} %bitcast.218, bf16[1,1024,1024]{2,1,0:T(8,128)(2,1)S(1)} %bitcast.206), kind=kOutput, calls=%fused_computation.115 | convolution fusion | flops 1074790400 | bytes 8388608 | tf_op jit(solution)/shard_map/jvp()/conv_general_dilated | solution.py:41
  1488.9 50.5 all-gather.6.cloned.1.call-done
  1555.3 48.1 all-to-all-done
  1636.2 43.5 all-gather.8.cloned.1.call-done
  1679.7 28.9 fusion.37
  1739.6 83.1 %reduce-scatter.10.cloned.1.call-done = f32[1024,1024]{1,0:T(8,128)} async-done(((f32[2048,1024]{1,0:T(8,128)}), f32[1024,1024]{1,0:T(8,128)}) %reduce-scatter.10.cloned.1.call-update) | async-done | bytes 4194320 | tf_op jit(solution)/shard_map/reduce_scatter | solution.py:172
  1827.7 51.6 reduce-scatter.8.cloned.1.call-done
  1886.1 27.9 all_to_all.26
  1946.5 81.5 %reduce-scatter.12.cloned.1.call-done = f32[1024,1024]{1,0:T(8,128)} async-done(((f32[2048,1024]{1,0:T(8,128)}), f32[1024,1024]{1,0:T(8,128)}) %reduce-scatter.12.cloned.1.call-update) | async-done | bytes 4194320 | tf_op jit(solution)/shard_map/reduce_scatter | solution.py:193
  2036.6 3226.7 %fusion.75 = f32[1024,1,1024]{2,1,0:T(1,128)S(1)} fusion(bf16[1,1024,1024]{2,1,0:T(8,128)(2,1)S(1)} %bitcast.216, bf16[1,1024,1024]{2,1,0:T(8,128)(2,1)S(1)} %bitcast.207), kind=kOutput, calls=%fused_computation.132 | convolution fusion | flops 1074790400 | bytes 8388608 | tf_op jit(solution)/shard_map/transpose(jvp())/conv_general_dilated | solution.py:41
  5266.3 32.7 rev.8
  5311.2 722.8 %while.38 = (s32[]{:T(128)}, f32[1024,1]{0,1:T(1,128)S(1)}, f32[1024,1024]{1,0:T(8,128)}, f32[8,1024,4]{1,2,0:T(4,128)S(1)}, bf16[8,1024,4]{1,2,0:T(4,128)(2,1)S...) while((s32[]{:T(128)}, f32[1024,1]{0,1:T(1,128)S(1)}, ...), condition=%wide.region_28.29_spmd.clone, body=%wide.region_21.28_spmd.clone.sunk | while | flops 96499712 | bytes 4718787 | solution.py:30
  5314.1 87.3 %fusion.116 = (bf16[1024,4]{0,1:T(4,128)(2,1)S(1)}, bf16[1024,4]{0,1:T(4,128)(2,1)S(1)}, f32[1024,4]{0,1:T(4,128)S(1)}, f32[1024,4]{0,1:T(4,128)S(1)}) fusion(f32[1024,4]{0,1:T(4,128)S(1)} %get-tuple-element.742, f32[1024,1024]{1,0:T(8,128)} %get-tuple-element.828, f32[1024]{0:T(1024)S(1)} %iota_convert_fusion.4, ...), kind=kLoop, calls=%fused_computation.18.clone.1 | loop fusion | flops 96452608 | bytes 4313088 | tf_op jit(solution)/shard_map/transpose(jvp())/while/body/eval_jaxpr/checkpoint/reduce_sum | solution.py:25
  5404.5 87.3 %fusion.116 = (bf16[1024,4]{0,1:T(4,128)(2,1)S(1)}, bf16[1024,4]{0,1:T(4,128)(2,1)S(1)}, f32[1024,4]{0,1:T(4,128)S(1)}, f32[1024,4]{0,1:T(4,128)S(1)}) fusion(f32[1024,4]{0,1:T(4,128)S(1)} %get-tuple-element.742, f32[1024,1024]{1,0:T(8,128)} %get-tuple-element.828, f32[1024]{0:T(1024)S(1)} %iota_convert_fusion.4, ...), kind=kLoop, calls=%fused_computation.18.clone.1 | loop fusion | flops 96452608 | bytes 4313088 | tf_op jit(solution)/shard_map/transpose(jvp())/while/body/eval_jaxpr/checkpoint/reduce_sum | solution.py:25
  5494.8 87.3 %fusion.116 = (bf16[1024,4]{0,1:T(4,128)(2,1)S(1)}, bf16[1024,4]{0,1:T(4,128)(2,1)S(1)}, f32[1024,4]{0,1:T(4,128)S(1)}, f32[1024,4]{0,1:T(4,128)S(1)}) fusion(f32[1024,4]{0,1:T(4,128)S(1)} %get-tuple-element.742, f32[1024,1024]{1,0:T(8,128)} %get-tuple-element.828, f32[1024]{0:T(1024)S(1)} %iota_convert_fusion.4, ...), kind=kLoop, calls=%fused_computation.18.clone.1 | loop fusion | flops 96452608 | bytes 4313088 | tf_op jit(solution)/shard_map/transpose(jvp())/while/body/eval_jaxpr/checkpoint/reduce_sum | solution.py:25
  5585.2 87.3 %fusion.116 = (bf16[1024,4]{0,1:T(4,128)(2,1)S(1)}, bf16[1024,4]{0,1:T(4,128)(2,1)S(1)}, f32[1024,4]{0,1:T(4,128)S(1)}, f32[1024,4]{0,1:T(4,128)S(1)}) fusion(f32[1024,4]{0,1:T(4,128)S(1)} %get-tuple-element.742, f32[1024,1024]{1,0:T(8,128)} %get-tuple-element.828, f32[1024]{0:T(1024)S(1)} %iota_convert_fusion.4, ...), kind=kLoop, calls=%fused_computation.18.clone.1 | loop fusion | flops 96452608 | bytes 4313088 | tf_op jit(solution)/shard_map/transpose(jvp())/while/body/eval_jaxpr/checkpoint/reduce_sum | solution.py:25
  5675.5 87.3 %fusion.116 = (bf16[1024,4]{0,1:T(4,128)(2,1)S(1)}, bf16[1024,4]{0,1:T(4,128)(2,1)S(1)}, f32[1024,4]{0,1:T(4,128)S(1)}, f32[1024,4]{0,1:T(4,128)S(1)}) fusion(f32[1024,4]{0,1:T(4,128)S(1)} %get-tuple-element.742, f32[1024,1024]{1,0:T(8,128)} %get-tuple-element.828, f32[1024]{0:T(1024)S(1)} %iota_convert_fusion.4, ...), kind=kLoop, calls=%fused_computation.18.clone.1 | loop fusion | flops 96452608 | bytes 4313088 | tf_op jit(solution)/shard_map/transpose(jvp())/while/body/eval_jaxpr/checkpoint/reduce_sum | solution.py:25
  5765.9 87.3 %fusion.116 = (bf16[1024,4]{0,1:T(4,128)(2,1)S(1)}, bf16[1024,4]{0,1:T(4,128)(2,1)S(1)}, f32[1024,4]{0,1:T(4,128)S(1)}, f32[1024,4]{0,1:T(4,128)S(1)}) fusion(f32[1024,4]{0,1:T(4,128)S(1)} %get-tuple-element.742, f32[1024,1024]{1,0:T(8,128)} %get-tuple-element.828, f32[1024]{0:T(1024)S(1)} %iota_convert_fusion.4, ...), kind=kLoop, calls=%fused_computation.18.clone.1 | loop fusion | flops 96452608 | bytes 4313088 | tf_op jit(solution)/shard_map/transpose(jvp())/while/body/eval_jaxpr/checkpoint/reduce_sum | solution.py:25
  5856.3 87.3 %fusion.116 = (bf16[1024,4]{0,1:T(4,128)(2,1)S(1)}, bf16[1024,4]{0,1:T(4,128)(2,1)S(1)}, f32[1024,4]{0,1:T(4,128)S(1)}, f32[1024,4]{0,1:T(4,128)S(1)}) fusion(f32[1024,4]{0,1:T(4,128)S(1)} %get-tuple-element.742, f32[1024,1024]{1,0:T(8,128)} %get-tuple-element.828, f32[1024]{0:T(1024)S(1)} %iota_convert_fusion.4, ...), kind=kLoop, calls=%fused_computation.18.clone.1 | loop fusion | flops 96452608 | bytes 4313088 | tf_op jit(solution)/shard_map/transpose(jvp())/while/body/eval_jaxpr/checkpoint/reduce_sum | solution.py:25
  5946.6 87.3 %fusion.116 = (bf16[1024,4]{0,1:T(4,128)(2,1)S(1)}, bf16[1024,4]{0,1:T(4,128)(2,1)S(1)}, f32[1024,4]{0,1:T(4,128)S(1)}, f32[1024,4]{0,1:T(4,128)S(1)}) fusion(f32[1024,4]{0,1:T(4,128)S(1)} %get-tuple-element.742, f32[1024,1024]{1,0:T(8,128)} %get-tuple-element.828, f32[1024]{0:T(1024)S(1)} %iota_convert_fusion.4, ...), kind=kLoop, calls=%fused_computation.18.clone.1 | loop fusion | flops 96452608 | bytes 4313088 | tf_op jit(solution)/shard_map/transpose(jvp())/while/body/eval_jaxpr/checkpoint/reduce_sum | solution.py:25
  6068.0 620.2 %fusion.71 = f32[1,1024,1024]{2,0,1:T(1,128)S(1)} fusion(bf16[1024,1024,1]{1,0,2:T(8,128)(2,1)} %bitcast.219, bf16[1,1024,1024]{2,1,0:T(8,128)(2,1)} %bitcast.217), kind=kOutput, calls=%fused_computation.113 | convolution fusion | flops 1074790400 | bytes 8388608 | tf_op jit(solution)/shard_map/transpose(jvp())/conv_general_dilated | solution.py:41
  6705.7 63.7 all-reduce.13
  (365 shorter events, 326.8 us)
Async XLA Ops:
  7.2 1532.2 %all-gather.6.cloned.1.call-start = ((), (), s32[]{:S(2)}) async-start(), calls=%async_computation.9 | async-start | bytes 6291456 | tf_op jit(solution)/shard_map/all_gather | solution.py:140
  14.3 583.2 %copy-start.41 = (f32[1024]{0:T(1024)}, f32[1024]{0:T(1024)S(1)}, u32[]{:S(2)}) copy-start(f32[1024]{0:T(1024)S(1)} %broadcast_multiply_fusion.2) | copy-start | bytes 12292
  47.7 64.4 copy-start
  115.7 64.4 copy-start
  183.8 64.4 copy-start
  251.8 64.4 copy-start
  319.8 64.4 copy-start
  387.8 64.4 copy-start
  455.9 64.4 copy-start
  523.9 64.4 copy-start
  632.3 846.9 %copy-start.30 = (f32[2,1,512]{2,1,0:T(1,128)S(1)}, f32[2,1,512]{2,1,0:T(1,128)}, u32[]{:S(2)}) copy-start(f32[2,1,512]{2,1,0:T(1,128)} %all-gather.1) | copy-start | bytes 12292
  1482.2 138.6 %all-gather.10.cloned.1.call-start = ((), (), s32[]{:S(2)}) async-start(), calls=%async_computation.12 | async-start | bytes 6291456 | tf_op jit(solution)/shard_map/all_gather | solution.py:167
  1551.2 52.2 all-to-all-start
  1555.2 124.5 %all-gather.8.cloned.1.call-start = ((), (), s32[]{:S(2)}) async-start(), calls=%async_computation.10 | async-start | bytes 6291456 | tf_op jit(solution)/shard_map/all_gather | solution.py:152
  1610.2 212.5 %reduce-scatter.10.cloned.1.call-start = ((), (), s32[]{:S(2)}) async-start(), calls=%async_computation.13 | async-start | bytes 12582912 | tf_op jit(solution)/shard_map/reduce_scatter | solution.py:172
  1723.3 156.0 %reduce-scatter.8.cloned.1.call-start = ((), (), s32[]{:S(2)}) async-start(), calls=%async_computation.11 | async-start | bytes 6291456 | tf_op jit(solution)/shard_map/reduce_scatter | solution.py:156
  1739.5 139.8 %copy-start.12 = (bf16[1,1024,1024]{2,1,0:T(8,128)(2,1)S(1)}, bf16[1,1024,1024]{2,1,0:T(8,128)(2,1)}, u32[]{:S(2)}) copy-start(bf16[1,1024,1024]{2,1,0:T(8,128)(2,1)} %param.37) | copy-start | bytes 6291460
  1739.5 288.5 %reduce-scatter.12.cloned.1.call-start = ((), (), s32[]{:S(2)}) async-start(), calls=%async_computation.14 | async-start | bytes 12582912 | tf_op jit(solution)/shard_map/reduce_scatter | solution.py:193
  1928.7 4776.9 %reduce-scatter.18.cloned.1.call-start = ((), (), s32[]{:S(2)}) async-start(), calls=%async_computation.17 | async-start | bytes 98304 | tf_op jit(solution)/shard_map/reduce_scatter | solution.py:221
  1928.8 99.3 %copy-start.10 = (bf16[1024,1024]{1,0:T(8,128)(2,1)S(1)}, bf16[1024,1024]{1,0:T(8,128)(2,1)}, u32[]{:S(2)}) copy-start(bf16[1024,1024]{1,0:T(8,128)(2,1)} %fusion.47) | copy-start | bytes 6291460
  1928.8 99.2 %copy-start.31 = (f32[2,1,512]{2,1,0:T(1,128)S(1)}, f32[2,1,512]{2,1,0:T(1,128)}, u32[]{:S(2)}) copy-start(f32[2,1,512]{2,1,0:T(1,128)} %all-gather.1) | copy-start | bytes 12292
  2036.6 3226.7 %copy-start.14 = (bf16[1024,1024]{1,0:T(8,128)(2,1)}, bf16[1024,1024]{1,0:T(8,128)(2,1)S(1)}, u32[]{:S(2)}) copy-start(bf16[1024,1024]{1,0:T(8,128)(2,1)S(1)} %convert_element_type.218) | copy-start | bytes 6291460
  6034.7 670.9 %reduce-scatter.20.cloned.1.call-start = ((), (), s32[]{:S(2)}) async-start(), calls=%async_computation.18 | async-start | bytes 98304 | tf_op jit(solution)/shard_map/reduce_scatter | solution.py:224
  6050.4 655.2 %reduce-scatter.16.cloned.1.call-start = ((), (), s32[]{:S(2)}) async-start(), calls=%async_computation.16 | async-start | bytes 98304 | tf_op jit(solution)/shard_map/reduce_scatter | solution.py:218
  6060.6 645.0 %reduce-scatter.14.cloned.1.call-start = ((), (), s32[]{:S(2)}) async-start(), calls=%async_computation.15 | async-start | bytes 98304 | tf_op jit(solution)/shard_map/reduce_scatter | solution.py:215
  6061.3 708.0 %all-reduce.12.cloned.1.call-start = ((), (), s32[]{:S(2)}) async-start(), calls=%async_computation.19 | async-start | bytes 41943040 | tf_op jit(solution)/shard_map/psum | solution.py:244
  6068.0 620.3 %copy-start.5 = (bf16[1,1024,1024]{2,1,0:T(8,128)(2,1)S(1)}, bf16[1,1024,1024]{2,1,0:T(8,128)(2,1)}, u32[]{:S(2)}) copy-start(bf16[1,1024,1024]{2,1,0:T(8,128)(2,1)} %param.21) | copy-start | bytes 6291460
  6068.0 620.2 %copy-start.7 = (f32[1024,1024]{1,0:T(8,128)S(1)}, f32[1024,1024]{1,0:T(8,128)}, u32[]{:S(2)}) copy-start(f32[1024,1024]{1,0:T(8,128)} %copy-done.6) | copy-start | bytes 12582916
  6068.0 620.2 %copy-start.29 = (f32[1024]{0:T(1024)S(1)}, f32[1024]{0:T(1024)}, u32[]{:S(2)}) copy-start(f32[1024]{0:T(1024)} %copy-done.28) | copy-start | bytes 12292
  6068.0 620.2 %copy-start.32 = (f32[2,1,512]{2,1,0:T(1,128)S(1)}, f32[2,1,512]{2,1,0:T(1,128)}, u32[]{:S(2)}) copy-start(f32[2,1,512]{2,1,0:T(1,128)} %all-gather.1) | copy-start | bytes 12292
  6068.0 620.2 %copy-start.38 = (f32[1024]{0:T(1024)S(1)}, f32[1024]{0:T(1024)}, u32[]{:S(2)}) copy-start(f32[1024]{0:T(1024)} %copy-done.37) | copy-start | bytes 12292
  6068.0 620.2 %copy-start.40 = (f32[1024]{0:T(1024)S(1)}, f32[1024]{0:T(1024)}, u32[]{:S(2)}) copy-start(f32[1024]{0:T(1024)} %copy-done.39) | copy-start | bytes 12292
  (45 other events, 438.8 us)
Sparse Core Ops, SparseCore 0:
  1482.3 57.0 all-gather.5
  1541.5 79.2 all-gather.9
  1622.9 56.7 all-gather.7
  1723.4 99.2 reduce-scatter.9
  1825.0 54.3 reduce-scatter.7
  1928.8 99.2 reduce-scatter.11
  6034.8 9.8 reduce-scatter.17
  6050.5 9.8 reduce-scatter.19
  6063.3 9.8 reduce-scatter.15
  6075.9 9.8 reduce-scatter.13
  6091.8 364.6 all-reduce.11
where the time goes:
time: 6790 us
  matrix products  4820 us (71%)
  other arithmetic  1290 us (19%)
  waiting for transfers between devices  369 us (5%)
  local copies, waits for them, and re-layouts  154 us (2%)
  blocking collectives  130 us (2%)
    conv_general_dilated x3, matrix products, causal_conv(): lax.conv_general_dilated(signal, flipped, (1,), [(length - 1, 0)], dimens...  4690 us
    reduce_sum x8, other arithmetic, add_group(): imag_part[:, :, None] * jnp.sin(angles)  698 us
    reduce_sum x8, other arithmetic, add_group(): return (running + jnp.sum(summands, axis=1), None)  515 us
  transfers between devices with their start and end apart: 12, of which 7 were waited for; matrix products, arithmetic and copies ran while one was open for 11% of the time, Pallas kernels for 0%

commit v1 on v0

v1 whole, which is shorter than its diff:
```python
import numpy as np, ml_dtypes, jax, jax.numpy as jnp
from jax import lax
from jax.experimental import pallas as pl
from jax.experimental.pallas import tpu as pltpu
from jax.sharding import PartitionSpec as P

VMEM_LIMIT = 56 * 1024 * 1024
F32, BF16 = jnp.float32, jnp.bfloat16
LANES = 128
Q = 32


def transform_table(length):
    f = np.arange(length, dtype=np.int64)[:, None]
    t = np.arange(length, dtype=np.int64)[None, :]
    turn = ((4 * f + 1) * t) % (4 * length)
    angle = turn * (2.0 * np.pi / (4 * length))
    return np.concatenate([np.cos(angle), -np.sin(angle)], axis=0)


def cmul(a, b):
    return a[0] * b[0] - a[1] * b[1], a[0] * b[1] + a[1] * b[0]


def fill_powers(base_r, base_i, out_r, out_i, tmp, scale=None):
    modes = base_r.shape[0]
    p1 = (base_r, base_i)
    p2 = cmul(p1, p1)
    p4 = cmul(p2, p2)
    p8 = cmul(p4, p4)
    p16 = cmul(p8, p8)
    for i, p in enumerate((p1, p2, p4, p8, p16)):
        tmp[2 * i] = p[0]
        tmp[2 * i + 1] = p[1]
    if scale is not None:
        tmp[10] = scale[0]
        tmp[11] = scale[1]
    row = lax.broadcasted_iota(jnp.int32, (8, LANES), 0)
    one = jnp.ones((8, LANES), F32)
    zero = jnp.zeros((8, LANES), F32)

    def mode(n, carry):
        def at(i):
            return (
                jnp.broadcast_to(tmp[2 * i, pl.ds(n, 1), :], (8, LANES)),
                jnp.broadcast_to(tmp[2 * i + 1, pl.ds(n, 1), :], (8, LANES)),
            )

        p = (one, zero) if scale is None else at(5)
        for bit in range(3):
            q = cmul(p, at(bit))
            on = (row & (1 << bit)) != 0
            p = (jnp.where(on, q[0], p[0]), jnp.where(on, q[1], p[1]))
        parts = [p, cmul(p, at(3))]
        p16_here = at(4)
        parts += [cmul(parts[0], p16_here), cmul(parts[1], p16_here)]
        for j, part in enumerate(parts):
            out_r[n, 8 * j : 8 * j + 8, :] = part[0]
            out_i[n, 8 * j : 8 * j + 8, :] = part[1]
        return carry

    lax.fori_loop(0, modes, mode, 0)


def kernel_body(z_ref, k_ref, zr, zi, wr, wi, tmp):
    fill_powers(z_ref[0], z_ref[1], zr, zi, tmp)
    fill_powers(z_ref[2], z_ref[3], wr, wi, tmp, (z_ref[4], z_ref[5]))
    modes = z_ref.shape[1]
    step = 4
    blocks = k_ref.shape[0] // Q

    def rows(i, carry):
        d = i * step
        acc = [jnp.zeros((Q, LANES), F32) for _ in range(step)]
        for n in range(modes):
            a, b = zr[n], zi[n]
            for u in range(step):
                acc[u] = acc[u] + (
                    wr[n, pl.ds(d + u, 1), :] * a - wi[n, pl.ds(d + u, 1), :] * b
                )
        for u in range(step):
            k_ref[pl.ds(pl.multiple_of((d + u) * Q, Q), Q), :] = acc[u].astype(BF16)
        return carry

    lax.fori_loop(0, blocks // step, rows, 0)


def make_kernel(z, length):
    modes, channels = z.shape[1:]
    return pl.pallas_call(
        kernel_body,
        grid=(channels // LANES,),
        in_specs=[pl.BlockSpec((6, modes, LANES), lambda i: (0, 0, i))],
        out_specs=pl.BlockSpec((length, LANES), lambda i: (0, i)),
        out_shape=jax.ShapeDtypeStruct((length, channels), BF16),
        scratch_shapes=[pltpu.VMEM((modes, Q, LANES), F32)] * 4
        + [pltpu.VMEM((12, modes, LANES), F32)],
        compiler_params=pltpu.CompilerParams(vmem_limit_bytes=VMEM_LIMIT),
        name="make_kernel",
    )(z)


def moments_body(z_ref, g_ref, out_ref, zr, zi, wr, wi, tmp, gl):
    fill_powers(z_ref[0], z_ref[1], zr, zi, tmp)
    fill_powers(z_ref[2], z_ref[3], wr, wi, tmp)
    modes = z_ref.shape[1]
    blocks = g_ref.shape[0] // Q

    def weigh(i, carry):
        at = pl.ds(pl.multiple_of(i * Q, Q), Q)
        pos = (lax.broadcasted_iota(jnp.int32, (Q, LANES), 0) + i * Q).astype(F32)
        gl[at, :] = g_ref[at, :] * pos
        return carry

    lax.fori_loop(0, blocks, weigh, 0)
    pair = 2

    def mode(i, carry):
        n = i * pair
        sums = [[jnp.zeros((Q, LANES), F32) for _ in range(4)] for _ in range(pair)]
        for d in range(blocks):
            g = g_ref[d * Q : (d + 1) * Q, :]
            h = gl[d * Q : (d + 1) * Q, :]
            for u in range(pair):
                a = wr[n + u, d : d + 1, :]
                b = wi[n + u, d : d + 1, :]
                s = sums[u]
                s[0] = s[0] + g * a
                s[1] = s[1] + g * b
                s[2] = s[2] + h * a
                s[3] = s[3] + h * b
        for u in range(pair):
            s = sums[u]
            z = (zr[n + u], zi[n + u])
            first = cmul(z, (s[0], s[1]))
            second = cmul(z, (s[2], s[3]))
            for j, v in enumerate(first + second):
                out_ref[j, pl.ds(n + u, 1), :] = jnp.sum(v, axis=0, keepdims=True)
        return carry

    lax.fori_loop(0, modes // pair, mode, 0)


def make_moments(z, g):
    modes, channels = z.shape[1:]
    length = g.shape[0]
    return pl.pallas_call(
        moments_body,
        grid=(channels // LANES,),
        in_specs=[
            pl.BlockSpec((4, modes, LANES), lambda i: (0, 0, i)),
            pl.BlockSpec((length, LANES), lambda i: (0, i)),
        ],
        out_specs=pl.BlockSpec((4, modes, LANES), lambda i: (0, 0, i)),
        out_shape=jax.ShapeDtypeStruct((4, modes, channels), F32),
        scratch_shapes=[pltpu.VMEM((modes, Q, LANES), F32)] * 4
        + [pltpu.VMEM((12, modes, LANES), F32), pltpu.VMEM((length, LANES), F32)],
        compiler_params=pltpu.CompilerParams(vmem_limit_bytes=VMEM_LIMIT),
        name="make_moments",
    )(z, g)


GELU_A = 0.7978845608028654
GELU_B = 0.044715


def gelu(v):
    return 0.5 * v * (1.0 + jnp.tanh(GELU_A * (v + GELU_B * (v * v * v))))


def gelu_slope(v):
    sq = v * v
    th = jnp.tanh(GELU_A * (v + GELU_B * (sq * v)))
    return 0.5 * (1.0 + th) + 0.5 * v * (1.0 - th * th) * (GELU_A + (3.0 * GELU_A * GELU_B) * sq)


def dot(a, b):
    return jnp.dot(a, b, preferred_element_type=F32)


FT = 512
TT = 256


def conv_body(x_ref, k_ref, skip_ref, fwd_ref, inv_ref, mixed_ref, act_ref, xs_ref, ks_ref, ys):
    n = x_ref.shape[0]
    x = x_ref[...]
    k = k_ref[...]
    for i in range(n // FT):
        re = pl.ds(i * FT, FT)
        im = pl.ds(n + i * FT, FT)
        xr, xi = dot(fwd_ref[re, :], x), dot(fwd_ref[im, :], x)
        kr, ki = dot(fwd_ref[re, :], k), dot(fwd_ref[im, :], k)
        xs_ref[re, :] = xr.astype(BF16)
        xs_ref[im, :] = xi.astype(BF16)
        ks_ref[re, :] = kr.astype(BF16)
        ks_ref[im, :] = ki.astype(BF16)
        ys[re, :] = (xr * kr - xi * ki).astype(BF16)
        ys[im, :] = (xr * ki + xi * kr).astype(BF16)
    y = ys[...]
    for i in range(n // TT):
        at = pl.ds(i * TT, TT)
        mixed = dot(inv_ref[at, :], y) + skip_ref[...] * x_ref[at, :].astype(F32)
        mixed_ref[at, :] = mixed
        act_ref[at, :] = gelu(mixed).astype(BF16)


CB = 256


def conv_forward(x, k, skip, fwd, inv):
    n, channels = x.shape
    col = lambda rows: pl.BlockSpec((rows, CB), lambda i: (0, i))
    whole = lambda a: pl.BlockSpec(a.shape, lambda i: (0, 0), pipeline_mode=pl.Buffered(1))
    return pl.pallas_call(
        conv_body,
        grid=(channels // CB,),
        in_specs=[col(n), col(n), col(1), whole(fwd), whole(inv)],
        out_specs=[col(n), col(n), col(2 * n), col(2 * n)],
        out_shape=[
            jax.ShapeDtypeStruct((n, channels), F32),
            jax.ShapeDtypeStruct((n, channels), BF16),
            jax.ShapeDtypeStruct((2 * n, channels), BF16),
            jax.ShapeDtypeStruct((2 * n, channels), BF16),
        ],
        scratch_shapes=[pltpu.VMEM((2 * n, CB), BF16)],
        compiler_params=pltpu.CompilerParams(vmem_limit_bytes=VMEM_LIMIT),
        name="conv_forward",
    )(x, k, skip, fwd, inv)


def back_body(
    ga_ref, mixed_ref, x_ref, xs_ref, ks_ref, skip_ref, fwd_ref, inv_ref,
    gn_ref, gk_ref, sg_ref, gm, gy, ax, ak,
):
    n = x_ref.shape[0]
    total = jnp.zeros((1, CB), F32)
    for i in range(n // TT):
        at = pl.ds(i * TT, TT)
        v = ga_ref[at, :] * gelu_slope(mixed_ref[at, :])
        gm[at, :] = v
        gy[at, :] = v.astype(BF16)
        total += jnp.sum(v * x_ref[at, :].astype(F32), axis=0, keepdims=True)
    sg_ref[...] = total
    g = gy[...]
    for i in range(n // FT):
        re = pl.ds(i * FT, FT)
        im = pl.ds(n + i * FT, FT)
        gr, gi = dot(fwd_ref[re, :], g), dot(fwd_ref[im, :], g)
        for src, dst in ((ks_ref, ax), (xs_ref, ak)):
            a, b = src[re, :].astype(F32), src[im, :].astype(F32)
            dst[re, :] = (a * gr + b * gi).astype(BF16)
            dst[im, :] = (a * gi - b * gr).astype(BF16)
    yx = ax[...]
    yk = ak[...]
    for i in range(n // TT):
        at = pl.ds(i * TT, TT)
        gk_ref[at, :] = dot(inv_ref[at, :], yk)
        gn_ref[at, :] = dot(inv_ref[at, :], yx) + skip_ref[...] * gm[at, :]


def conv_backward(ga, mixed, x, xs, ks, skip, fwd, inv):
    n, channels = x.shape
    col = lambda rows: pl.BlockSpec((rows, CB), lambda i: (0, i))
    whole = lambda a: pl.BlockSpec(a.shape, lambda i: (0, 0), pipeline_mode=pl.Buffered(1))
    return pl.pallas_call(
        back_body,
        grid=(channels // CB,),
        in_specs=[col(n), col(n), col(n), col(2 * n), col(2 * n), col(1), whole(fwd), whole(inv)],
        out_specs=[col(n), col(n), col(1)],
        out_shape=[
            jax.ShapeDtypeStruct((n, channels), F32),
            jax.ShapeDtypeStruct((n, channels), F32),
            jax.ShapeDtypeStruct((1, channels), F32),
        ],
        scratch_shapes=[pltpu.VMEM((n, CB), F32), pltpu.VMEM((n, CB), BF16)]
        + [pltpu.VMEM((2 * n, CB), BF16)] * 2,
        compiler_params=pltpu.CompilerParams(vmem_limit_bytes=VMEM_LIMIT),
        name="conv_backward",
    )(ga, mixed, x, xs, ks, skip, fwd, inv)


def modes_of(log_dt, log_a, freq, c_real, c_imag):
    dt = jnp.exp(log_dt)[None, :]
    rate = dt * jnp.exp(log_a)
    turn = dt * freq
    rho, rho_q = jnp.exp(-rate), jnp.exp(-float(Q) * rate)
    return jnp.stack(
        [
            rho * jnp.cos(turn), rho * jnp.sin(turn),
            rho_q * jnp.cos(Q * turn), rho_q * jnp.sin(Q * turn),
            2.0 * dt * c_real, 2.0 * dt * c_imag,
        ]
    )
norm_eps = 1e-05


def norm_forward(values, norm_gain, norm_bias):
    center = values - jnp.mean(values, axis=-1, keepdims=True)
    inv_std = lax.rsqrt(jnp.mean(center * center, axis=-1, keepdims=True) + norm_eps)
    standard = center * inv_std
    return (standard * norm_gain + norm_bias, standard, inv_std)


def norm_backward(incoming, standard, inv_std, norm_gain):
    scaled = incoming * norm_gain
    value_grad = inv_std * (
        scaled
        - jnp.mean(scaled, axis=-1, keepdims=True)
        - standard * jnp.mean(scaled * standard, axis=-1, keepdims=True)
    )
    return (value_grad, jnp.sum(incoming * standard, axis=0), jnp.sum(incoming, axis=0))


def contract_rows(left, right):
    return lax.dot_general(left, right, (((0,), (0,)), ((), ())), preferred_element_type=F32)


def contract_cols(left, right):
    return lax.dot_general(left, right, (((1,), (1,)), ((), ())), preferred_element_type=F32)


SWAP = ((0, 1), (1, 0))


def over_core(values):
    return lax.ppermute(values, "core", SWAP)


def over_tensor(values):
    return lax.ppermute(values, "tensor", SWAP)


def ordered(index, mine, other, axis):
    first = jnp.where(index == 0, mine, other)
    second = jnp.where(index == 0, other, mine)
    return jnp.concatenate([first, second], axis=axis)


def part(values, index, axis):
    half = values.shape[axis] // 2
    return lax.dynamic_slice_in_dim(values, index * half, half, axis)


def fetch(weight, axis):
    core = lax.axis_index("core")
    direct = over_tensor(part(weight, core, axis))
    return direct, over_core(direct)


def reduce_parts(own, direct, via, axis):
    core = lax.axis_index("core")
    there = direct + over_core(via.astype(BF16)).astype(F32)
    from_core = over_core(part(own, 1 - core, axis).astype(BF16)).astype(F32)
    from_tensor = over_tensor(there.astype(BF16)).astype(F32)
    here = part(own, core, axis) + from_core + from_tensor
    total = lax.psum(here.astype(BF16), "pair")
    return ordered(core, total, over_core(total), axis).astype(F32)


def shards(
    inputs, counts, ln1_gain, ln1_bias, log_dt, log_a, freq, c_real, c_imag, skip_gain,
    w_value, w_gate, ln2_gain, ln2_bias, w_in, w_out, cotangent,
):
    _, length, width = inputs.shape
    core, side = lax.axis_index("core"), lax.axis_index("tensor")
    used_flag = (side < counts[0]).astype(F32)
    source = inputs.reshape(length, width).astype(F32)
    gain_first, bias_first = ln1_gain.astype(F32), ln1_bias.astype(F32)
    gain_second, bias_second = ln2_gain.astype(F32), ln2_bias.astype(F32)
    table = transform_table(length)
    fwd = jnp.asarray(table.astype(ml_dtypes.bfloat16))
    inv = jnp.asarray(np.ascontiguousarray((table.T / length).astype(ml_dtypes.bfloat16)))

    modes = log_a.shape[1]
    local = jnp.concatenate(
        [log_a.T, freq.T, c_real.T, c_imag.T, log_dt[None], skip_gain[None]], axis=0
    )
    params = ordered(side, local, over_tensor(local), 1)
    log_a_all, freq_all, real_all, imag_all = (params[i * modes : (i + 1) * modes] for i in range(4))
    log_dt_all, skip = params[4 * modes], params[4 * modes + 1 : 4 * modes + 2]

    value_parts, gate_parts = fetch(w_value, 1), fetch(w_gate, 1)
    in_parts, out_parts = (w_in,) + fetch(w_in, 1), (w_out,) + fetch(w_out, 0)
    value_w = ordered(side, w_value, ordered(core, *value_parts, 1), 1)
    gate_w = ordered(side, w_gate, ordered(core, *gate_parts, 1), 1)

    normed1_full, standard1, inv_std1 = norm_forward(source, gain_first, bias_first)
    normed1 = normed1_full.astype(BF16)
    z = modes_of(log_dt_all, log_a_all, freq_all, real_all, imag_all)
    kernel = make_kernel(z, length)
    mixed, act, spectrum, kernel_spectrum = conv_forward(normed1, kernel, skip, fwd, inv)

    value_proj = dot(act, value_w)
    gate_sig = jax.nn.sigmoid(dot(act, gate_w))
    residual = source + (value_proj * gate_sig).astype(BF16).astype(F32)
    normed2_full, standard2, inv_std2 = norm_forward(residual, gain_second, bias_second)
    normed2 = normed2_full.astype(BF16)
    grad_low = (used_flag * cotangent.reshape(length, width).astype(F32)).astype(BF16)
    grad_out = grad_low.astype(F32)
    ffn_out = 0.0
    grad_normed2 = 0.0
    in_grads, out_grads = [], []
    for w_i, w_o in zip(in_parts, out_parts):
        pre_act = dot(normed2, w_i)
        hidden = gelu(pre_act).astype(BF16)
        slope = gelu_slope(pre_act).astype(BF16)
        ffn_out = ffn_out + dot(hidden, w_o)
        out_grads.append(contract_rows(hidden, grad_low))
        grad_pre = (contract_cols(grad_low, w_o) * slope.astype(F32)).astype(BF16)
        in_grads.append(contract_rows(normed2, grad_pre))
        grad_normed2 = grad_normed2 + contract_cols(grad_pre, w_i)
    output = (used_flag * (residual + ffn_out)).astype(BF16).reshape(inputs.shape)
    out_total = reduce_parts(*out_grads, 0)
    in_total = reduce_parts(*in_grads, 1)

    grad_resid_part, gain_second_grad, bias_second_grad = norm_backward(
        grad_normed2, standard2, inv_std2, gain_second
    )
    grad_residual = grad_out + grad_resid_part
    grad_glu = grad_residual.astype(BF16).astype(F32)
    grad_value = (grad_glu * gate_sig).astype(BF16)
    grad_gate = (grad_glu * value_proj * gate_sig * (1.0 - gate_sig)).astype(BF16)
    grad_act = contract_cols(grad_value, value_w) + contract_cols(grad_gate, gate_w)

    def glu_total(grad):
        other = part(grad, 1 - side, 1)
        return reduce_parts(part(grad, side, 1), part(other, core, 1), part(other, 1 - core, 1), 1)

    value_total = glu_total(contract_rows(act, grad_value))
    gate_total = glu_total(contract_rows(act, grad_gate))

    grad_normed1, grad_kernel, skip_grad = conv_backward(
        grad_act, mixed, normed1, spectrum, kernel_spectrum, skip, fwd, inv
    )
    moments = make_moments(z[:4], grad_kernel)
    grad_source, gain_first_grad, bias_first_grad = norm_backward(
        grad_normed1, standard1, inv_std1, gain_first
    )
    input_grad = (grad_residual + grad_source).astype(BF16).reshape(inputs.shape)

    scale = 2.0 * jnp.exp(log_dt_all)[None, :]
    real_grad, imag_grad = scale * moments[0], -scale * moments[1]
    slope_r = scale * (real_all * moments[2] - imag_all * moments[3])
    slope_i = scale * (real_all * moments[3] + imag_all * moments[2])
    dt = jnp.exp(log_dt_all)[None, :]
    log_a_grad = -dt * jnp.exp(log_a_all) * slope_r
    freq_grad = -dt * slope_i
    log_dt_grad = jnp.sum(
        real_all * real_grad + imag_all * imag_grad + log_a_grad + freq_all * freq_grad,
        axis=0, keepdims=True,
    )
    small = jnp.concatenate(
        [log_a_grad, freq_grad, real_grad, imag_grad, log_dt_grad, skip_grad]
        + [g[None] for g in (gain_first_grad, bias_first_grad, gain_second_grad, bias_second_grad)],
        axis=0,
    )
    mine = part(small, side, 1) + over_tensor(part(small, 1 - side, 1))
    small = lax.psum(mine, ("pair", "core"))
    rows = small[4 * modes :]
    return (
        output,
        input_grad,
        rows[2],
        rows[3],
        rows[0],
        small[:modes].T,
        small[modes : 2 * modes].T,
        small[2 * modes : 3 * modes].T,
        small[3 * modes : 4 * modes].T,
        rows[1],
        value_total,
        gate_total,
        rows[4],
        rows[5],
        in_total,
        out_total,
    )


def solution(mesh):
    devices = mesh.devices
    cores = jax.sharding.Mesh(
        devices.reshape(devices.shape[0] // 2, 2, devices.shape[1]), ("pair", "core", "tensor")
    )
    batch, every = ("pair", "core"), ("pair", "core", "tensor")
    in_specs = (
        P(every, None, None), P(batch), P(), P(), P("tensor"), P("tensor", None), P("tensor", None),
        P("tensor", None), P("tensor", None), P("tensor"), P(None, "tensor"), P(None, "tensor"),
        P(), P(), P(None, "tensor"), P("tensor", None), P(every, None, None),
    )
    out_specs = (
        P(every, None, None), P(every, None, None), P("tensor"), P("tensor"), P("tensor"),
        P("tensor", None), P("tensor", None), P("tensor", None), P("tensor", None), P("tensor"),
        P(None, "tensor"), P(None, "tensor"), P("tensor"), P("tensor"), P(None, "tensor"),
        P("tensor", None),
    )
    return jax.shard_map(shards, mesh=cores, in_specs=in_specs, out_specs=out_specs, check_vma=False)
```

time: 6790 us -> 661 us (0.10)
  matrix products: 4820 us -> 134 us
  other arithmetic: 1290 us -> 68.6 us
  Pallas kernels: 0 us -> 132 us
  blocking collectives: 130 us -> 0 us
  local copies, waits for them, and re-layouts: 154 us -> 33.4 us
  waiting for transfers between devices: 369 us -> 255 us
    conv_general_dilated x3 -> x0, matrix products: 4690 us -> none  [causal_conv(): lax.conv_general_dilated(signal, flipped, (1,), [(length - 1, 0)], dimens...]
    reduce_sum x25 -> x1, other arithmetic: 1220 us -> 1.28 us  [shards(): jnp.sum(real_all * real_grad + imag_all * imag_grad + log_a_grad + freq_a...]
    reduce_scatter x7 -> x0, waiting for transfers between devices: 216 us -> none  [the longest x1 83.1 us: shards(): lax.psum_scatter(contract_cols(lax.slice_in_dim(grad_pre, 0, row_count *...]
    psum x1 -> x2, waiting for transfers between devices: 0.01 us -> 154 us  [the longest x1 82.1 us: shards(): small = lax.psum(mine, ('pair', 'core'))]
    pallas_call x0 -> x4, Pallas kernels: none -> 132 us  [the longest x1 50.5 us: make_moments(): pl.pallas_call(moments_body, grid=(channels // LANES,), in_specs=[pl.Bloc...]
    all_gather x3 -> x0, waiting for transfers between devices: 104 us -> none  [the longest x1 50.5 us: shards(): act_all = lax.all_gather(act_low, 'tensor', axis=0, tiled=True)]
    ppermute x0 -> x26, waiting for transfers between devices: none -> 101 us  [the longest x10 100 us: over_tensor(): return lax.ppermute(values, 'tensor', SWAP)]
  transfers between devices with their start and end apart: 12 -> 28, of which waited for: 7 -> 5; matrix products, arithmetic and copies ran while one was open for 11% -> 32% of each run, Pallas kernels for 0% -> 20%
where the time goes in v1:
time: 661 us; the launch traced here: 655 us
  waiting for transfers between devices  255 us (39%)
  matrix products  134 us (20%)
  Pallas kernels  132 us (20%)
  other arithmetic  68.6 us (10%)
  local copies, waits for them, and re-layouts  33.4 us (5%)
  between operations  17.4 us (3%)
  starting transfers between devices  14.2 us (2%)
    ppermute x10, waiting for transfers between devices, over_tensor(): return lax.ppermute(values, 'tensor', SWAP)  100 us
    psum x1, waiting for transfers between devices, shards(): small = lax.psum(mine, ('pair', 'core'))  82.1 us
    psum x1, waiting for transfers between devices, reduce_parts(): total = lax.psum(here.astype(BF16), 'pair')  71.9 us
    pallas_call x1, Pallas kernels, make_moments(): pl.pallas_call(moments_body, grid=(channels // LANES,), in_specs=[pl.Bloc...  50.5 us
    dot_general x8, matrix products, contract_cols(): lax.dot_general(left, right, (((1,), (1,)), ((), ())), preferred_element_...  50 us
    dot_general x8, matrix products, dot(): return jnp.dot(a, b, preferred_element_type=F32)  47 us
    dot_general x8, matrix products, contract_rows(): lax.dot_general(left, right, (((0,), (0,)), ((), ())), preferred_element_...  37.4 us
    pallas_call x1, Pallas kernels, make_kernel(): pl.pallas_call(kernel_body, grid=(channels // LANES,), in_specs=[pl.Block...  36.9 us
  transfers between devices with their start and end apart: 28, of which 5 were waited for; matrix products, arithmetic and copies ran while one was open for 32% of the time, Pallas kernels for 20%

profile of v1, /device:TPU:0, one launch (start us, length us, event | category | flops | bytes accessed | tf_op | source)
XLA Modules:
  0.0 655.1 jit_solution(12034126110705773837)
XLA Ops:
  8.1 4.1 concatenate.34
  42.2 36.9 %make_kernel.1.k_ref = bf16[1024,1024]{1,0:T(8,128)(2,1)} custom-call(f32[6,32,1024]{2,1,0:T(8,128)} %copy-done.25), custom_call_target="tpu_custom_call" | custom-call | tf_op jit(solution)/shard_map/make_kernel/pallas_call | solution.py:90
  79.1 20.9 %conv_forward.1 = (f32[1024,1024]{1,0:T(8,128)}, bf16[1024,1024]{1,0:T(8,128)(2,1)}, bf16[2048,1024]{1,0:T(8,128)(2,1)}, bf16[2048,1024]{1,0:T(8,128)(2,1)}) custom-call(bf16[1024,1024]{1,0:T(8,128)(2,1)} %fusion.17.x_ref, bf16[1024,1024]{1,0:T(8,128)(2,1)} %make_kernel.1.k_ref, f32[1,1024]{1,0:T(1,128)} %get-tuple-element.87.skip_ref, ...), custom_call_target="tpu_custom_call" | custom-call | tf_op jit(solution)/shard_map/conv_forward/pallas_call | solution.py:215
  112.0 7.1 %fusion.83 = f32[1024,2048]{1,0:T(8,128)} fusion(bf16[1024,1024]{1,0:T(8,128)(2,1)S(1)} %add_convert_fusion.4, bf16[1024,2048]{1,0:T(8,128)(2,1)S(1)} %copy-done.30), kind=kOutput, calls=%fused_computation.190 | convolution fusion | flops 4294967296 | bytes 14680064 | tf_op jit(solution)/shard_map/dot_general | solution.py:178
  119.1 10.1 %multiply_convert_fusion = bf16[1024,2048]{1,0:T(8,128)(2,1)S(1)} fusion(bf16[2048,1024]{1,0:T(8,128)(2,1)S(1)} %copy-done.32, f32[1024,2048]{1,0:T(8,128)} %fusion.83, bf16[1,1024,1024]{2,1,0:T(8,128)(2,1)S(1)} %copy-done.22, f32[]{:T(128)S(6)} %convert_element_type.196), kind=kOutput, calls=%fused_computation.10 | convolution fusion | flops 4337958912 | bytes 18874372 | tf_op jit(solution)/shard_map/dot_general | solution.py:320
  129.2 4.6 fusion.90
  137.9 8.2 %fusion.54 = f32[2048,1024]{1,0:T(8,128)S(1)} fusion(bf16[1,1024,1024]{2,1,0:T(8,128)(2,1)S(1)} %copy-done.22, f32[]{:T(128)S(6)} %convert_element_type.196, f32[1024,2048]{1,0:T(8,128)} %fusion.83), kind=kOutput, calls=%fused_computation.122 | convolution fusion | flops 4316987392 | bytes 18874372 | tf_op jit(solution)/shard_map/dot_general | solution.py:316
  151.4 8.5 %fusion.86 = f32[1024,1024]{1,0:T(8,128)} fusion(bf16[1024,2048]{1,0:T(8,128)(2,1)} %copy-done.56, bf16[1024,2048]{1,0:T(8,128)(2,1)S(1)} %copy-done.31), kind=kOutput, calls=%fused_computation.193 | convolution fusion | flops 4294967296 | bytes 12582912 | tf_op jit(solution)/shard_map/dot_general | solution.py:320
  160.5 3.9 fusion.84
  164.4 7.3 %multiply_convert_fusion.3 = bf16[1024,1024]{1,0:T(8,128)(2,1)S(1)} fusion(bf16[1024,1024]{1,0:T(8,128)(2,1)} %collective-permute-done.6, f32[1024,1024]{1,0:T(8,128)S(1)} %fusion.84, bf16[1,1024,1024]{2,1,0:T(8,128)(2,1)S(1)} %copy-done.22, f32[]{:T(128)S(6)} %convert_element_type.196), kind=kOutput, calls=%fused_computation.70 | convolution fusion | flops 2170552320 | bytes 10485764 | tf_op jit(solution)/shard_map/dot_general | solution.py:320
  171.8 6.7 %fusion.87 = f32[1024,1024]{1,0:T(8,128)} fusion(bf16[1024,1024]{1,0:T(8,128)(2,1)S(1)} %multiply_convert_fusion.3, bf16[1024,1024]{1,0:T(8,128)(2,1)} %collective-permute-done.5), kind=kOutput, calls=%fused_computation.194 | convolution fusion | flops 2147483648 | bytes 8388608 | tf_op jit(solution)/shard_map/dot_general | solution.py:320
  180.8 4.4 convolution_convert_fusion
  185.3 4.3 multiply_convert_fusion.2
  189.6 3.7 convolution_convert_fusion.1
  193.8 6.3 multiply_reduce_fusion
  214.2 5.5 add_convert_fusion.3
  219.8 6.0 add_convert_fusion.1
  232.4 91.7 %collective-permute-done.12 = bf16[1024,256]{1,0:T(8,128)(2,1)S(1)} collective-permute-done((bf16[1024,256]{1,0:T(8,128)(2,1)S(1)}, bf16[1024,256]{1,0:T(8,128)(2,1)S(1)}, u32[]{:S(2)}, u32[]{:S(2)}) %collective-permute-start.12) | collective-permute-done | bytes 524320 | tf_op jit(solution)/shard_map/ppermute | solution.py:331
  329.1 8.6 %collective-permute-done.16 = bf16[1024,256]{1,0:T(8,128)(2,1)} collective-permute-done((bf16[1024,256]{1,0:T(8,128)(2,1)S(1)}, bf16[1024,256]{1,0:T(8,128)(2,1)}, u32[]{:S(2)}, u32[]{:S(2)}) %collective-permute-start.16) | collective-permute-done | bytes 524320 | tf_op jit(solution)/shard_map/ppermute | solution.py:331
  340.6 6.1 add_convert_fusion.2
  346.7 4.8 add_convert_fusion
  351.6 11.8 %fusion.74 = f32[1024,1024]{1,0:T(8,128)} fusion(bf16[2048,1024]{1,0:T(8,128)(2,1)} %param.34, f32[1024,2048]{1,0:T(8,128)} %fusion.83), kind=kOutput, calls=%fused_computation.187 | convolution fusion | flops 4313841664 | bytes 16777216 | tf_op jit(solution)/shard_map/dot_general | solution.py:178
  363.4 6.4 fusion.73
  372.2 4.3 convolution_add_fusion.ga_ref
  376.5 23.5 %conv_backward.1 = (f32[1024,1024]{1,0:T(8,128)}, f32[1024,1024]{1,0:T(8,128)}, f32[1,1024]{1,0:T(1,128)}) custom-call(f32[1024,1024]{1,0:T(8,128)} %convolution_add_fusion.ga_ref, f32[1024,1024]{1,0:T(8,128)} %get-tuple-element.24.mixed_ref, bf16[1024,1024]{1,0:T(8,128)(2,1)} %fusion.17.x_ref, bf16[2048,1024]{1,0:T(8,128)(2,1)} %get-tuple-element.25.xs_ref, ...), custom_call_target="tpu_custom_call" | custom-call | tf_op jit(solution)/shard_map/conv_backward/pallas_call | solution.py:266
  400.1 50.5 %make_moments.1 = f32[4,32,1024]{2,1,0:T(8,128)} custom-call(f32[4,32,1024]{2,1,0:T(8,128)} %pad_maximum_fusion.8.z_ref, f32[1024,1024]{1,0:T(8,128)} %get-tuple-element.28.g_ref), custom_call_target="tpu_custom_call" | custom-call | tf_op jit(solution)/shard_map/make_moments/pallas_call | solution.py:147
  454.9 10.3 %fusion.46 = bf16[1,1024,1024]{2,1,0:T(8,128)(2,1)} fusion(f32[1024,1024]{1,0:T(8,128)} %fusion.74, f32[1024,1024]{1,0:T(8,128)} %fusion.73, bf16[1024,1024]{1,0:T(8,128)(2,1)} %copy-done.1, bf16[1,1024,1024]{2,1,0:T(8,128)(2,1)S(1)} %copy-done, f32[]{:T(128)S(6)} %convert_element_type.196, bf16[1024,1024]{1,0:T(8,128)(2,1)} %copy-done.55, ...), kind=kOutput, calls=%fused_computation.83 | convolution fusion | flops 2165309440 | bytes 20971524 | tf_op jit(solution)/shard_map/dot_general | solution.py:178
  465.2 71.9 %all-reduce.6.cloned.1.call-done = (bf16[1024,256]{1,0:T(8,128)(2,1)}, bf16[1024,256]{1,0:T(8,128)(2,1)}, bf16[1024,1024]{1,0:T(8,128)(2,1)}, bf16[1024,1024]{1,0:T(8,128)(2,1)}) async-done(((bf16[1024,256]{1,0:T(8,128)(2,1)}, bf16[1024,256]{1,0:T(8,128)(2,1)}, bf16[1024,1024]{1,0:T(8,128)(2,1)}, bf16[1024,1024]{1,0:T(8,128)(2,1)}), (bf16[1024,256]{1,0:T(8,128)(2,1)}, bf16[1024,256]{1,0:T(8,128)(2,1)}, ...) | async-done | bytes 5242896 | tf_op jit(solution)/shard_map/psum | solution.py:357
  538.5 5.4 fusion.48
  544.1 82.1 %all-reduce.4.cloned.1.call-done = f32[134,512]{1,0:T(8,128)} async-done(((f32[134,512]{1,0:T(8,128)}), f32[134,512]{1,0:T(8,128)}) %all-reduce.4.cloned.1.call-update) | async-done | bytes 274448 | tf_op jit(solution)/shard_map/psum | solution.py:459
  636.0 4.4 maximum_convert_fusion
  642.9 4.5 maximum_convert_fusion.1
  (248 shorter events, 102.7 us)
Async XLA Ops:
  8.0 529.1 %all-reduce.6.cloned.1.call-start = ((), (), s32[]{:S(2)}) async-start(), calls=%async_computation.1 | async-start | bytes 10485760 | tf_op jit(solution)/shard_map/psum | solution.py:357
  12.2 21.2 %collective-permute-start = (f32[130,512]{1,0:T(8,128)S(1)}, f32[130,512]{1,0:T(8,128)}, u32[]{:S(2)}, u32[]{:S(2)}) collective-permute-start(f32[130,512]{1,0:T(8,128)S(1)} %concatenate.34), channel_id=1, source_target_pairs={{0,1},{1,0},{2,3},{3,2},{4,5},{5,4},{6,7},{7,6},{8,9},{9,8},{10,11... | collective-permute-start | bytes 798728 | tf_op jit(solution)/shard_map/ppermute | solution.py:331
  17.1 22.3 %collective-permute-start.3 = (bf16[1024,256]{1,0:T(8,128)(2,1)}, bf16[1024,256]{1,0:T(8,128)(2,1)S(1)}, u32[]{:S(2)}, u32[]{:S(2)}) collective-permute-start(bf16[1024,256]{1,0:T(8,128)(2,1)} %constant_dynamic-slice_fusion.3), channel_id=1, source_target_pairs={{0,1},{1,0},{2,3},{3,2},{4,5},{5,4},{6,7},{7,6},{8,9},{9,8},{10,11... | collective-permute-start | bytes 1572872 | tf_op jit(solution)/shard_map/ppermute | solution.py:331
  18.9 81.1 %collective-permute-start.1 = (bf16[1024,256]{1,0:T(8,128)(2,1)}, bf16[1024,256]{1,0:T(8,128)(2,1)S(1)}, u32[]{:S(2)}, u32[]{:S(2)}) collective-permute-start(bf16[1024,256]{1,0:T(8,128)(2,1)} %constant_dynamic-slice_fusion.4), channel_id=1, source_target_pairs={{0,1},{1,0},{2,3},{3,2},{4,5},{5,4},{6,7},{7,6},{8,9},{9,8},{10,11... | collective-permute-start | bytes 1572872 | tf_op jit(solution)/shard_map/ppermute | solution.py:331
  24.2 135.8 %collective-permute-start.6 = (bf16[1024,1024]{1,0:T(8,128)(2,1)}, bf16[1024,1024]{1,0:T(8,128)(2,1)}, u32[]{:S(2)}, u32[]{:S(2)}) collective-permute-start(bf16[1024,1024]{1,0:T(8,128)(2,1)} %constant_dynamic-slice_fusion.1), channel_id=1, source_target_pairs={{0,1},{1,0},{2,3},{3,2},{4,5},{5,4},{6,7},{7,6},{8,9},{9,8},{10,11... | collective-permute-start | bytes 6291464 | tf_op jit(solution)/shard_map/ppermute | solution.py:331
  27.3 133.1 %collective-permute-start.5 = (bf16[1024,1024]{1,0:T(8,128)(2,1)}, bf16[1024,1024]{1,0:T(8,128)(2,1)}, u32[]{:S(2)}, u32[]{:S(2)}) collective-permute-start(bf16[1024,1024]{1,0:T(8,128)(2,1)} %constant_dynamic-slice_fusion.2), channel_id=1, source_target_pairs={{0,1},{1,0},{2,3},{3,2},{4,5},{5,4},{6,7},{7,6},{8,9},{9,8},{10,11... | collective-permute-start | bytes 6291464 | tf_op jit(solution)/shard_map/ppermute | solution.py:331
  39.4 61.2 %collective-permute-start.4 = (bf16[1024,256]{1,0:T(8,128)(2,1)S(1)}, bf16[1024,256]{1,0:T(8,128)(2,1)S(1)}, u32[]{:S(2)}, u32[]{:S(2)}) collective-permute-start(bf16[1024,256]{1,0:T(8,128)(2,1)S(1)} %collective-permute-done.3), channel_id=1, source_target_pairs={{0,2},{2,0},{1,3},{3,1},{4,6},{6,4},{5,7},{7,5},{8,10},{10,8},{9,1... | collective-permute-start | bytes 1572872 | tf_op jit(solution)/shard_map/ppermute | solution.py:327
  100.1 2.1 collective-permute-start.2
  137.8 202.8 %collective-permute-start.18 = (bf16[1024,1024]{1,0:T(8,128)(2,1)}, bf16[1024,1024]{1,0:T(8,128)(2,1)}, u32[]{:S(2)}, u32[]{:S(2)}) collective-permute-start(bf16[1024,1024]{1,0:T(8,128)(2,1)} %dynamic-slice_convert_fusion.1), channel_id=1, source_target_pairs={{0,2},{2,0},{1,3},{3,1},{4,6},{6,4},{5,7},{7,5},{8,10},{10,8},{9,1... | collective-permute-start | bytes 6291464 | tf_op jit(solution)/shard_map/ppermute | solution.py:327
  160.0 25.3 %collective-permute-start.8 = (bf16[1024,1024]{1,0:T(8,128)(2,1)}, bf16[1024,1024]{1,0:T(8,128)(2,1)S(1)}, u32[]{:S(2)}, u32[]{:S(2)}) collective-permute-start(bf16[1024,1024]{1,0:T(8,128)(2,1)} %collective-permute-done.6), channel_id=1, source_target_pairs={{0,2},{2,0},{1,3},{3,1},{4,6},{6,4},{5,7},{7,5},{8,10},{10,8},{9,1... | collective-permute-start | bytes 6291464 | tf_op jit(solution)/shard_map/ppermute | solution.py:327
  160.4 18.1 %collective-permute-start.7 = (bf16[1024,1024]{1,0:T(8,128)(2,1)}, bf16[1024,1024]{1,0:T(8,128)(2,1)S(1)}, u32[]{:S(2)}, u32[]{:S(2)}) collective-permute-start(bf16[1024,1024]{1,0:T(8,128)(2,1)} %collective-permute-done.5), channel_id=1, source_target_pairs={{0,2},{2,0},{1,3},{3,1},{4,6},{6,4},{5,7},{7,5},{8,10},{10,8},{9,1... | collective-permute-start | bytes 6291464 | tf_op jit(solution)/shard_map/ppermute | solution.py:327
  193.3 20.4 %collective-permute-start.19 = (bf16[1024,1024]{1,0:T(8,128)(2,1)}, bf16[1024,1024]{1,0:T(8,128)(2,1)}, u32[]{:S(2)}, u32[]{:S(2)}) collective-permute-start(bf16[1024,1024]{1,0:T(8,128)(2,1)} %convolution_convert_fusion.1), channel_id=1, source_target_pairs={{0,2},{2,0},{1,3},{3,1},{4,6},{6,4},{5,7},{7,5},{8,10},{10,8},{9,1... | collective-permute-start | bytes 6291464 | tf_op jit(solution)/shard_map/ppermute | solution.py:327
  193.8 25.9 %collective-permute-start.23 = (bf16[1024,1024]{1,0:T(8,128)(2,1)}, bf16[1024,1024]{1,0:T(8,128)(2,1)}, u32[]{:S(2)}, u32[]{:S(2)}) collective-permute-start(bf16[1024,1024]{1,0:T(8,128)(2,1)} %convolution_convert_fusion), channel_id=1, source_target_pairs={{0,2},{2,0},{1,3},{3,1},{4,6},{6,4},{5,7},{7,5},{8,10},{10,8},{9,1... | collective-permute-start | bytes 6291464 | tf_op jit(solution)/shard_map/ppermute | solution.py:327
  208.5 11.2 %collective-permute-start.11 = (bf16[1024,256]{1,0:T(8,128)(2,1)S(1)}, bf16[1024,256]{1,0:T(8,128)(2,1)}, u32[]{:S(2)}, u32[]{:S(2)}) collective-permute-start(bf16[1024,256]{1,0:T(8,128)(2,1)S(1)} %get-tuple-element.74), channel_id=1, source_target_pairs={{0,2},{2,0},{1,3},{3,1},{4,6},{6,4},{5,7},{7,5},{8,10},{10,8},{9,1... | collective-permute-start | bytes 1572872 | tf_op jit(solution)/shard_map/ppermute | solution.py:327
  209.0 16.8 %collective-permute-start.10 = (bf16[1024,256]{1,0:T(8,128)(2,1)S(1)}, bf16[1024,256]{1,0:T(8,128)(2,1)}, u32[]{:S(2)}, u32[]{:S(2)}) collective-permute-start(bf16[1024,256]{1,0:T(8,128)(2,1)S(1)} %get-tuple-element.73), channel_id=1, source_target_pairs={{0,2},{2,0},{1,3},{3,1},{4,6},{6,4},{5,7},{7,5},{8,10},{10,8},{9,1... | collective-permute-start | bytes 1572872 | tf_op jit(solution)/shard_map/ppermute | solution.py:327
  213.7 12.6 %collective-permute-start.15 = (bf16[1024,256]{1,0:T(8,128)(2,1)S(1)}, bf16[1024,256]{1,0:T(8,128)(2,1)}, u32[]{:S(2)}, u32[]{:S(2)}) collective-permute-start(bf16[1024,256]{1,0:T(8,128)(2,1)S(1)} %get-tuple-element.72), channel_id=1, source_target_pairs={{0,2},{2,0},{1,3},{3,1},{4,6},{6,4},{5,7},{7,5},{8,10},{10,8},{9,1... | collective-permute-start | bytes 1572872 | tf_op jit(solution)/shard_map/ppermute | solution.py:327
  219.7 10.5 %collective-permute-start.14 = (bf16[1024,256]{1,0:T(8,128)(2,1)}, bf16[1024,256]{1,0:T(8,128)(2,1)}, u32[]{:S(2)}, u32[]{:S(2)}) collective-permute-start(bf16[1024,256]{1,0:T(8,128)(2,1)} %get-tuple-element.71), channel_id=1, source_target_pairs={{0,2},{2,0},{1,3},{3,1},{4,6},{6,4},{5,7},{7,5},{8,10},{10,8},{9,1... | collective-permute-start | bytes 1572872 | tf_op jit(solution)/shard_map/ppermute | solution.py:327
  219.7 120.9 %collective-permute-start.20 = (bf16[1024,1024]{1,0:T(8,128)(2,1)}, bf16[1024,1024]{1,0:T(8,128)(2,1)}, u32[]{:S(2)}, u32[]{:S(2)}) collective-permute-start(bf16[1024,1024]{1,0:T(8,128)(2,1)} %add_convert_fusion.3), channel_id=1, source_target_pairs={{0,1},{1,0},{2,3},{3,2},{4,5},{5,4},{6,7},{7,6},{8,9},{9,8},{10,11... | collective-permute-start | bytes 6291464 | tf_op jit(solution)/shard_map/ppermute | solution.py:331
  225.8 98.6 %copy-start.37 = (f32[1,32,1024]{2,1,0:T(8,128)S(1)}, f32[1,32,1024]{2,1,0:T(8,128)}, u32[]{:S(2)}) copy-start(f32[1,32,1024]{2,1,0:T(8,128)} %get-tuple-element.64) | copy-start | bytes 393220
  225.8 98.6 %copy-start.38 = (f32[1,32,1024]{2,1,0:T(8,128)S(1)}, f32[1,32,1024]{2,1,0:T(8,128)}, u32[]{:S(2)}) copy-start(f32[1,32,1024]{2,1,0:T(8,128)} %get-tuple-element.62) | copy-start | bytes 393220
  225.8 98.6 %copy-start.39 = (f32[1,32,1024]{2,1,0:T(8,128)S(1)}, f32[1,32,1024]{2,1,0:T(8,128)}, u32[]{:S(2)}) copy-start(f32[1,32,1024]{2,1,0:T(8,128)} %get-tuple-element.60) | copy-start | bytes 393220
  225.8 120.9 %collective-permute-start.22 = (bf16[1024,1024]{1,0:T(8,128)(2,1)}, bf16[1024,1024]{1,0:T(8,128)(2,1)}, u32[]{:S(2)}, u32[]{:S(2)}) collective-permute-start(bf16[1024,1024]{1,0:T(8,128)(2,1)} %dynamic-slice_convert_fusion), channel_id=1, source_target_pairs={{0,2},{2,0},{1,3},{3,1},{4,6},{6,4},{5,7},{7,5},{8,10},{10,8},{9,1... | collective-permute-start | bytes 6291464 | tf_op jit(solution)/shard_map/ppermute | solution.py:327
  226.3 120.4 %collective-permute-start.24 = (bf16[1024,1024]{1,0:T(8,128)(2,1)}, bf16[1024,1024]{1,0:T(8,128)(2,1)}, u32[]{:S(2)}, u32[]{:S(2)}) collective-permute-start(bf16[1024,1024]{1,0:T(8,128)(2,1)} %add_convert_fusion.1), channel_id=1, source_target_pairs={{0,1},{1,0},{2,3},{3,2},{4,5},{5,4},{6,7},{7,6},{8,9},{9,8},{10,11... | collective-permute-start | bytes 6291464 | tf_op jit(solution)/shard_map/ppermute | solution.py:331
  230.2 94.0 %collective-permute-start.12 = (bf16[1024,256]{1,0:T(8,128)(2,1)S(1)}, bf16[1024,256]{1,0:T(8,128)(2,1)S(1)}, u32[]{:S(2)}, u32[]{:S(2)}) collective-permute-start(bf16[1024,256]{1,0:T(8,128)(2,1)S(1)} %add_convert_fusion.8), channel_id=1, source_target_pairs={{0,1},{1,0},{2,3},{3,2},{4,5},{5,4},{6,7},{7,6},{8,9},{9,8},{10,11... | collective-permute-start | bytes 1572872 | tf_op jit(solution)/shard_map/ppermute | solution.py:331
  324.1 13.6 %collective-permute-start.16 = (bf16[1024,256]{1,0:T(8,128)(2,1)S(1)}, bf16[1024,256]{1,0:T(8,128)(2,1)}, u32[]{:S(2)}, u32[]{:S(2)}) collective-permute-start(bf16[1024,256]{1,0:T(8,128)(2,1)S(1)} %add_convert_fusion.6), channel_id=1, source_target_pairs={{0,1},{1,0},{2,3},{3,2},{4,5},{5,4},{6,7},{7,6},{8,9},{9,8},{10,11... | collective-permute-start | bytes 1572872 | tf_op jit(solution)/shard_map/ppermute | solution.py:331
  351.6 274.6 %all-reduce.4.cloned.1.call-start = ((), (), s32[]{:S(2)}) async-start(), calls=%async_computation | async-start | bytes 557056 | tf_op jit(solution)/shard_map/psum | solution.py:459
  454.3 82.8 %collective-permute-start.9 = (f32[134,512]{1,0:T(8,128)S(1)}, f32[134,512]{1,0:T(8,128)S(1)}, u32[]{:S(2)}, u32[]{:S(2)}) collective-permute-start(f32[134,512]{1,0:T(8,128)S(1)} %constant_dynamic-slice_fusion), channel_id=1, source_target_pairs={{0,1},{1,0},{2,3},{3,2},{4,5},{5,4},{6,7},{7,6},{8,9},{9,8},{10,11... | collective-permute-start | bytes 823304 | tf_op jit(solution)/shard_map/ppermute | solution.py:331
  537.1 96.7 %collective-permute-start.21 = (bf16[1024,1024]{1,0:T(8,128)(2,1)}, bf16[1024,1024]{1,0:T(8,128)(2,1)}, u32[]{:S(2)}, u32[]{:S(2)}) collective-permute-start(bf16[1024,1024]{1,0:T(8,128)(2,1)} %get-tuple-element.40), channel_id=1, source_target_pairs={{0,2},{2,0},{1,3},{3,1},{4,6},{6,4},{5,7},{7,5},{8,10},{10,8},{9,1... | collective-permute-start | bytes 6291464 | tf_op jit(solution)/shard_map/ppermute | solution.py:327
  537.9 91.5 %copy-start.34 = (bf16[1024,256]{1,0:T(8,128)(2,1)S(1)}, bf16[1024,256]{1,0:T(8,128)(2,1)}, u32[]{:S(2)}) copy-start(bf16[1024,256]{1,0:T(8,128)(2,1)} %get-tuple-element.38) | copy-start | bytes 1572868
  537.9 91.5 %collective-permute-start.13 = (bf16[1024,256]{1,0:T(8,128)(2,1)}, bf16[1024,256]{1,0:T(8,128)(2,1)}, u32[]{:S(2)}, u32[]{:S(2)}) collective-permute-start(bf16[1024,256]{1,0:T(8,128)(2,1)} %get-tuple-element.38), channel_id=1, source_target_pairs={{0,2},{2,0},{1,3},{3,1},{4,6},{6,4},{5,7},{7,5},{8,10},{10,8},{9,1... | collective-permute-start | bytes 1572872 | tf_op jit(solution)/shard_map/ppermute | solution.py:327
  543.9 96.5 %collective-permute-start.25 = (bf16[1024,1024]{1,0:T(8,128)(2,1)}, bf16[1024,1024]{1,0:T(8,128)(2,1)}, u32[]{:S(2)}, u32[]{:S(2)}) collective-permute-start(bf16[1024,1024]{1,0:T(8,128)(2,1)} %get-tuple-element.41), channel_id=1, source_target_pairs={{0,2},{2,0},{1,3},{3,1},{4,6},{6,4},{5,7},{7,5},{8,10},{10,8},{9,1... | collective-permute-start | bytes 6291464 | tf_op jit(solution)/shard_map/ppermute | solution.py:327
  627.8 4.3 collective-permute-start.17
  (61 other events, 1065.7 us)
Sparse Core Ops, SparseCore 0:
  351.7 185.3 all-reduce.5
Sparse Core Ops, SparseCore 1:
  538.0 88.2 all-reduce.3

commit v2 on v1

v2 whole, which is shorter than its diff:
```python
import math

import ml_dtypes
import numpy as np

import jax
import jax.numpy as jnp
from jax import lax
from jax.experimental import pallas as pl
from jax.experimental.pallas import tpu as pltpu
from jax.sharding import PartitionSpec as P

VMEM_LIMIT = 56 * 1024 * 1024
F32, BF16 = jnp.float32, jnp.bfloat16
LANES = 128
MESH = pl.DeviceIdType.MESH
KERNEL_INNER = 64
MOMENT_INNER = 32
CB = 256
DFT_ROWS = 512
TOKEN_ROWS = 256
FFN_TILE = 512
GELU_A = 0.7978845608028654
GELU_B = 0.044715
norm_eps = 1e-05


def params_of(**extra):
    return pltpu.CompilerParams(vmem_limit_bytes=VMEM_LIMIT, **extra)


class CoreExchange:
    def __init__(self, pairs, send, recv):
        self.pairs, self.send, self.recv = pairs, send, recv
        self.other = {"core": 1 - lax.axis_index("core")}

    def greet(self):
        pl.semaphore_signal(
            pltpu.get_barrier_semaphore(), inc=1, device_id=self.other, device_id_type=MESH
        )

    def meet(self):
        pl.semaphore_wait(pltpu.get_barrier_semaphore(), 1)

    def copies(self, slot):
        return [
            pltpu.make_async_remote_copy(
                src_ref=mine.at[slot], dst_ref=theirs.at[slot],
                send_sem=self.send.at[i, slot], recv_sem=self.recv.at[i, slot],
                device_id=self.other, device_id_type=MESH,
            )
            for i, (mine, theirs) in enumerate(self.pairs)
        ]

    def start(self, slot):
        for copy in self.copies(slot):
            copy.start()

    def arrived(self, slot):
        for copy in self.copies(slot):
            copy.wait_recv()

    def sent(self, slots):
        for slot in range(slots):
            for copy in self.copies(slot):
                copy.wait_send()


def exchange_sems(pairs, slots):
    return [pltpu.SemaphoreType.DMA((pairs, slots))] * 2


def transform_table(length):
    f = np.arange(length, dtype=np.int64)[:, None]
    t = np.arange(length, dtype=np.int64)[None, :]
    turn = ((4 * f + 1) * t) % (4 * length)
    angle = turn * (2.0 * np.pi / (4 * length))
    return np.concatenate([np.cos(angle), -np.sin(angle)], axis=0)


def cmul(a, b):
    return a[0] * b[0] - a[1] * b[1], a[0] * b[1] + a[1] * b[0]


def log2_of(count):
    bits = count.bit_length() - 1
    assert 1 << bits == count
    return bits


def fill_powers(base, count, out_r, out_i, tmp, scale=None):
    bits = log2_of(count)
    p = base
    for i in range(bits):
        tmp[2 * i] = p[0]
        tmp[2 * i + 1] = p[1]
        p = cmul(p, p)
    if scale is not None:
        tmp[2 * bits] = scale[0]
        tmp[2 * bits + 1] = scale[1]
    row = lax.broadcasted_iota(jnp.int32, (8, LANES), 0)

    def mode(n, carry):
        def at(i):
            return tuple(
                jnp.broadcast_to(tmp[2 * i + j, pl.ds(n, 1), :], (8, LANES)) for j in range(2)
            )

        if scale is None:
            p = (jnp.ones((8, LANES), F32), jnp.zeros((8, LANES), F32))
        else:
            p = at(bits)
        for bit in range(3):
            q = cmul(p, at(bit))
            on = (row & (1 << bit)) != 0
            p = (jnp.where(on, q[0], p[0]), jnp.where(on, q[1], p[1]))
        parts = [p]
        for bit in range(3, bits):
            w = at(bit)
            parts += [cmul(x, w) for x in parts]
        for j, part in enumerate(parts):
            out_r[n, 8 * j : 8 * j + 8, :] = part[0]
            out_i[n, 8 * j : 8 * j + 8, :] = part[1]
        return carry

    lax.fori_loop(0, base[0].shape[0], mode, 0)
    return p


def split_params(packed_ref, log_dt_ref):
    rows = packed_ref[...].T
    modes = rows.shape[0] // 4
    log_a, freq, c_real, c_imag = (rows[i * modes : (i + 1) * modes] for i in range(4))
    step = jnp.exp(log_dt_ref[...])
    rate = jnp.exp(log_a)
    decay = jnp.exp(-(step * rate))
    turn = step * freq
    return step, rate, freq, c_real, c_imag, (decay * jnp.cos(turn), decay * jnp.sin(turn))


def kernel_body(packed_ref, log_dt_ref, k_ref, zr, zi, wr, wi, tmp):
    step, _, _, c_real, c_imag, z = split_params(packed_ref, log_dt_ref)
    inner = zr.shape[1]
    outer = wr.shape[1]
    z_inner = fill_powers(z, inner, zr, zi, tmp)
    fill_powers(z_inner, outer, wr, wi, tmp, (2.0 * step * c_real, 2.0 * step * c_imag))
    modes = c_real.shape[0]
    group = 2

    def rows(i, carry):
        d = i * group
        acc = [jnp.zeros((inner, LANES), F32) for _ in range(group)]
        for n in range(modes):
            a, b = zr[n], zi[n]
            for u in range(group):
                acc[u] = acc[u] + (
                    wr[n, pl.ds(d + u, 1), :] * a - wi[n, pl.ds(d + u, 1), :] * b
                )
        for u in range(group):
            at = pl.ds(pl.multiple_of((d + u) * inner, inner), inner)
            k_ref[at, :] = acc[u].astype(BF16)
        return carry

    lax.fori_loop(0, outer // group, rows, 0)


def power_scratch(modes, inner, outer):
    return (
        [pltpu.VMEM((modes, inner, LANES), F32)] * 2
        + [pltpu.VMEM((modes, outer, LANES), F32)] * 2
        + [pltpu.VMEM((20, modes, LANES), F32)]
    )


def make_kernel(packed, log_dt, length):
    channels, modes = packed.shape[0], packed.shape[1] // 4
    return pl.pallas_call(
        kernel_body,
        grid=(channels // LANES,),
        in_specs=[
            pl.BlockSpec((LANES, 4 * modes), lambda i: (i, 0)),
            pl.BlockSpec((1, LANES), lambda i: (0, i)),
        ],
        out_specs=pl.BlockSpec((length, LANES), lambda i: (0, i)),
        out_shape=jax.ShapeDtypeStruct((length, channels), BF16),
        scratch_shapes=power_scratch(modes, KERNEL_INNER, length // KERNEL_INNER),
        compiler_params=params_of(),
        name="make_kernel",
    )(packed, log_dt)


def moments_body(
    packed_ref, log_dt_ref, g_ref, out_ref, zr, zi, wr, wi, tmp, sums
):
    step, rate, freq, c_real, c_imag, z = split_params(packed_ref, log_dt_ref)
    inner, outer = zr.shape[1], wr.shape[1]
    z_inner = fill_powers(z, inner, zr, zi, tmp)
    fill_powers(z_inner, outer, wr, wi, tmp)
    modes = c_real.shape[0]
    pos = lax.broadcasted_iota(jnp.int32, (inner, LANES), 0).astype(F32)

    def mode(n, carry):
        zero = jnp.zeros((inner, LANES), F32)
        sr, si, tr, ti = zero, zero, zero, zero
        for d in reversed(range(outer)):
            v = g_ref[0, d * inner : (d + 1) * inner, :]
            sr = sr + v * wr[n, d : d + 1, :]
            si = si + v * wi[n, d : d + 1, :]
            if d > 0:
                tr = tr + sr
                ti = ti + si
        zn = (zr[n], zi[n])
        first = cmul(zn, (sr, si))
        second = cmul(zn, (pos * sr + float(inner) * tr, pos * si + float(inner) * ti))
        for j, v in enumerate(first + second):
            sums[j, pl.ds(n, 1), :] = jnp.sum(v, axis=0, keepdims=True)
        return carry

    lax.fori_loop(0, modes, mode, 0)
    scale = 2.0 * step
    real_grad, imag_grad = scale * sums[0], -scale * sums[1]
    slope_r = scale * (c_real * sums[2] - c_imag * sums[3])
    slope_i = scale * (c_real * sums[3] + c_imag * sums[2])
    log_a_grad = -step * rate * slope_r
    freq_grad = -step * slope_i
    log_dt_grad = jnp.sum(
        c_real * real_grad + c_imag * imag_grad + log_a_grad + freq * freq_grad,
        axis=0, keepdims=True,
    )
    for i, part in enumerate((log_a_grad, freq_grad, real_grad, imag_grad)):
        out_ref[i * modes : (i + 1) * modes, :] = part
    top = 4 * modes
    row = lax.broadcasted_iota(jnp.int32, (8, LANES), 0)
    out_ref[top : top + 8, :] = jnp.where(row == 0, log_dt_grad, 0.0)


def make_moments(packed, log_dt, g, at):
    half, modes = packed.shape[0], packed.shape[1] // 4
    length = g.shape[1]
    return pl.pallas_call(
        moments_body,
        grid=(half // LANES,),
        in_specs=[
            pl.BlockSpec((LANES, 4 * modes), lambda i: (i, 0)),
            pl.BlockSpec((1, LANES), lambda i: (0, i)),
            pl.BlockSpec((1, length, LANES), lambda i: (at, 0, i)),
        ],
        out_specs=pl.BlockSpec((4 * modes + 8, LANES), lambda i: (0, i)),
        scratch_shapes=power_scratch(modes, MOMENT_INNER, length // MOMENT_INNER)
        + [pltpu.VMEM((4, modes, LANES), F32)],
        out_shape=jax.ShapeDtypeStruct((4 * modes + 8, half), F32),
        compiler_params=params_of(),
        name="make_moments",
    )(packed, log_dt, g)


def gelu_both(v):
    sq = v * v
    th = jnp.tanh(v * (GELU_A + (GELU_A * GELU_B) * sq))
    rise = 0.5 + 0.5 * th
    slope = rise + v * (0.5 - 0.5 * th * th) * (GELU_A + (3.0 * GELU_A * GELU_B) * sq)
    return v * rise, slope


def gelu(v):
    return gelu_both(v)[0]


def gelu_slope(v):
    return gelu_both(v)[1]


def dot(a, b):
    return jnp.dot(a, b, preferred_element_type=F32)


def conv_body(
    where_ref, x_ref, k0, k1, k2, k3, skip_ref, fwd_ref, inv_ref,
    mixed_ref, act_ref, xs_ref, ks_ref, k, ys,
):
    n = x_ref.shape[0]
    block = pl.program_id(0)
    here = 2 * lax.rem(block // 2 + where_ref[0], 2) + lax.rem(block + where_ref[1], 2)
    for i, ref in enumerate((k0, k1, k2, k3)):
        @pl.when(here == i)
        def _():
            k[...] = ref[...]

    x = x_ref[...]
    kernel = k[...]
    for i in range(n // DFT_ROWS):
        re = pl.ds(i * DFT_ROWS, DFT_ROWS)
        im = pl.ds(n + i * DFT_ROWS, DFT_ROWS)
        xr, xi = dot(fwd_ref[re, :], x), dot(fwd_ref[im, :], x)
        kr, ki = dot(fwd_ref[re, :], kernel), dot(fwd_ref[im, :], kernel)
        xs_ref[re, :] = xr.astype(BF16)
        xs_ref[im, :] = xi.astype(BF16)
        ks_ref[re, :] = kr.astype(BF16)
        ks_ref[im, :] = ki.astype(BF16)
        ys[re, :] = (xr * kr - xi * ki).astype(BF16)
        ys[im, :] = (xr * ki + xi * kr).astype(BF16)
    y = ys[...]
    for i in range(n // TOKEN_ROWS):
        at = pl.ds(i * TOKEN_ROWS, TOKEN_ROWS)
        mixed = dot(inv_ref[at, :], y) + skip_ref[...] * x_ref[at, :].astype(F32)
        mixed_ref[at, :] = mixed
        act_ref[at, :] = gelu(mixed).astype(BF16)


def conv_forward(where, x, kernels, skip, fwd, inv):
    n, channels = x.shape

    def col(rows):
        return pl.BlockSpec((rows, CB), lambda i, w: (0, i))

    def whole(a):
        return pl.BlockSpec(a.shape, lambda i, w: (0, 0), pipeline_mode=pl.Buffered(1))

    return pl.pallas_call(
        conv_body,
        grid_spec=pltpu.PrefetchScalarGridSpec(
            num_scalar_prefetch=1,
            grid=(channels // CB,),
            in_specs=[col(n)] + [whole(k) for k in kernels] + [col(1), whole(fwd), whole(inv)],
            out_specs=[col(n), col(n), col(2 * n), col(2 * n)],
            scratch_shapes=[pltpu.VMEM((n, CB), BF16), pltpu.VMEM((2 * n, CB), BF16)],
        ),
        out_shape=[
            jax.ShapeDtypeStruct((n, channels), F32),
            jax.ShapeDtypeStruct((n, channels), BF16),
            jax.ShapeDtypeStruct((2 * n, channels), BF16),
            jax.ShapeDtypeStruct((2 * n, channels), BF16),
        ],
        compiler_params=params_of(),
        name="conv_forward",
    )(where, x, *kernels, skip, fwd, inv)


def back_body(
    ga_ref, mixed_ref, x_ref, xs_ref, ks_ref, skip_ref, fwd_ref, inv_ref,
    gn_ref, gk_ref, sg_ref, gm, gy, ax, ak, mine, theirs, send, recv,
):
    step = pl.program_id(0)
    first = step < 2
    cores = CoreExchange([(mine, theirs)], send, recv)
    pl.when(step == 0)(cores.greet)
    n = x_ref.shape[0]
    total = jnp.zeros((1, CB), F32)
    for i in range(n // TOKEN_ROWS):
        at = pl.ds(i * TOKEN_ROWS, TOKEN_ROWS)
        v = ga_ref[at, :] * gelu_slope(mixed_ref[at, :])
        gm[at, :] = v
        gy[at, :] = v.astype(BF16)
        total += jnp.sum(v * x_ref[at, :].astype(F32), axis=0, keepdims=True)
    sg_ref[...] = total
    g = gy[...]
    for i in range(n // DFT_ROWS):
        re = pl.ds(i * DFT_ROWS, DFT_ROWS)
        im = pl.ds(n + i * DFT_ROWS, DFT_ROWS)
        gr, gi = dot(fwd_ref[re, :], g), dot(fwd_ref[im, :], g)
        for src, dst in ((ks_ref, ax), (xs_ref, ak)):
            a, b = src[re, :].astype(F32), src[im, :].astype(F32)
            dst[re, :] = (a * gr + b * gi).astype(BF16)
            dst[im, :] = (a * gi - b * gr).astype(BF16)
    yx = ax[...]
    yk = ak[...]
    for i in range(n // TOKEN_ROWS):
        at = pl.ds(i * TOKEN_ROWS, TOKEN_ROWS)
        gk_ref[0, at, :] = dot(inv_ref[at, :], yk)
        gn_ref[at, :] = dot(inv_ref[at, :], yx) + skip_ref[...] * gm[at, :]
    pl.when(step == 0)(cores.meet)

    @pl.when(first)
    def _():
        mine[step] = gk_ref[0]
        cores.start(step)

    @pl.when(jnp.logical_not(first))
    def _():
        cores.arrived(step - 2)
        gk_ref[0] = gk_ref[0] + theirs[step - 2]

    @pl.when(step == 3)
    def _():
        cores.sent(2)


def conv_backward(ga, mixed, x, xs, ks, skip, fwd, inv):
    n, channels = x.shape

    def block(i):
        side = lax.rem(lax.axis_index("tensor") + 1 + i, 2)
        half = lax.rem(lax.axis_index("core") + 1 + i // 2, 2)
        return 2 * side + half

    def col(rows):
        return pl.BlockSpec((rows, CB), lambda i: (0, block(i)))

    def whole(a):
        return pl.BlockSpec(a.shape, lambda i: (0, 0), pipeline_mode=pl.Buffered(1))

    return pl.pallas_call(
        back_body,
        grid=(channels // CB,),
        in_specs=[col(n), col(n), col(n), col(2 * n), col(2 * n), col(1), whole(fwd), whole(inv)],
        out_specs=[col(n), pl.BlockSpec((1, n, CB), lambda i: (jnp.maximum(i - 2, 0), 0, 0)), col(1)],
        out_shape=[
            jax.ShapeDtypeStruct((n, channels), F32),
            jax.ShapeDtypeStruct((2, n, CB), F32),
            jax.ShapeDtypeStruct((1, channels), F32),
        ],
        scratch_shapes=[pltpu.VMEM((n, CB), F32), pltpu.VMEM((n, CB), BF16)]
        + [pltpu.VMEM((2 * n, CB), BF16)] * 2
        + [pltpu.VMEM((2, n, CB), F32)] * 2
        + exchange_sems(1, 2),
        compiler_params=params_of(collective_id=3, has_side_effects=True),
        name="conv_backward",
    )(ga, mixed, x, xs, ks, skip, fwd, inv)


def glu_body(
    act, source, value_w, gate_w, gain, bias, value_ref, sig_ref, residual_ref, n2_ref, n2t_ref
):
    value = dot(act[...], value_w[...])
    sig = 1.0 / (1.0 + jnp.exp(-dot(act[...], gate_w[...])))
    value_ref[...] = value.astype(BF16)
    sig_ref[...] = sig.astype(BF16)
    residual = source[...].astype(F32) + (value * sig).astype(BF16).astype(F32)
    residual_ref[...] = residual
    n2 = norm_forward(residual, gain[...], bias[...])[0].astype(BF16)
    n2_ref[...] = n2
    n2t_ref[...] = n2.T


def glu_kernel(act, source, value_w, gate_w, gain, bias):
    n, d = act.shape
    rows = pl.BlockSpec((TOKEN_ROWS, d), lambda i: (i, 0))

    def whole(a):
        return pl.BlockSpec(a.shape, lambda i: (0, 0), pipeline_mode=pl.Buffered(1))

    return pl.pallas_call(
        glu_body,
        grid=(n // TOKEN_ROWS,),
        in_specs=[rows, rows, whole(value_w), whole(gate_w), whole(gain), whole(bias)],
        out_specs=[rows] * 4 + [pl.BlockSpec((d, TOKEN_ROWS), lambda i: (0, i))],
        out_shape=[
            jax.ShapeDtypeStruct((n, d), BF16), jax.ShapeDtypeStruct((n, d), BF16),
            jax.ShapeDtypeStruct((n, d), F32), jax.ShapeDtypeStruct((n, d), BF16),
            jax.ShapeDtypeStruct((d, n), BF16),
        ],
        compiler_params=params_of(),
        name="glu_kernel",
    )(act, source, value_w, gate_w, gain, bias)


def glu_back_body(
    g_far, g_own, residual, cot, value, sig, act, value_w, gate_w, gain,
    resid_ref, ga_ref, gain_ref, bias_ref, there_ref, here_ref, gv, gt, mine, theirs, send, recv,
):
    step = pl.program_id(0)
    cores = CoreExchange([(mine, theirs)], send, recv)
    pl.when(step == 0)(cores.greet)
    chunks = act.shape[0] // TOKEN_ROWS
    width = gv.shape[2]

    @pl.when(step < chunks)
    def _():
        standard, inv_std = norm_forward(residual[...], 1.0, 0.0)[1:]
        part, gain_grad, bias_grad = norm_backward(
            g_far[...] + g_own[...], standard, inv_std, gain[...]
        )
        new = step == 0
        gain_ref[...] = jnp.where(new, 0.0, gain_ref[...]) + gain_grad[None]
        bias_ref[...] = jnp.where(new, 0.0, bias_ref[...]) + bias_grad[None]
        resid = cot[...].astype(F32) + part
        resid_ref[...] = resid
        grad = resid.astype(BF16).astype(F32)
        gate = sig[...].astype(F32)
        grad_value = (grad * gate).astype(BF16)
        grad_gate = (grad * value[...].astype(F32) * gate * (1.0 - gate)).astype(BF16)
        ga_ref[...] = contract_cols(grad_value, value_w[...]) + contract_cols(grad_gate, gate_w[...])
        at = pl.ds(pl.multiple_of(step * TOKEN_ROWS, TOKEN_ROWS), TOKEN_ROWS)
        for i in range(gv.shape[0]):
            gv[i, at, :] = grad_value[:, i * width : (i + 1) * width]
            gt[i, at, :] = grad_gate[:, i * width : (i + 1) * width]

    @pl.when(step >= chunks)
    def _():
        j = step - chunks
        side = lax.rem(lax.axis_index("tensor") + 1 + j, 2)
        half = lax.rem(lax.axis_index("core") + 1 + j // 2, 2)
        block = 2 * side + half
        grads = [contract_rows(act[...], gv[block]), contract_rows(act[...], gt[block])]
        pl.when(j == 0)(cores.meet)

        @pl.when(j < 2)
        def _():
            for i, g in enumerate(grads):
                mine[j, :, i * width : (i + 1) * width] = g.astype(BF16)
            cores.start(j)

        @pl.when(j == 2)
        def _():
            cores.arrived(0)
            for i, g in enumerate(grads):
                at = pl.ds(i * width, width)
                there_ref[:, at] = (g + theirs[0, :, at].astype(F32)).astype(BF16)

        @pl.when(j == 3)
        def _():
            cores.arrived(1)
            for i, g in enumerate(grads):
                at = pl.ds(i * width, width)
                here_ref[:, at] = g + theirs[1, :, at].astype(F32)
            cores.sent(2)


def glu_back_kernel(g_far, g_own, residual, cot, value, sig, act, value_w, gate_w, gain):
    n, d = act.shape
    chunks = n // TOKEN_ROWS
    width = d // 4

    def whole(a):
        return pl.BlockSpec(a.shape, lambda i: (0, 0), pipeline_mode=pl.Buffered(1))

    rows = pl.BlockSpec((TOKEN_ROWS, d), lambda i: (jnp.minimum(i, chunks - 1), 0))
    vector = pl.BlockSpec((1, d), lambda i: (0, 0))
    weight = pl.BlockSpec((d, 2 * width), lambda i: (0, 0))
    return pl.pallas_call(
        glu_back_body,
        grid=(chunks + 4,),
        in_specs=[rows] * 6 + [whole(act), whole(value_w), whole(gate_w), whole(gain)],
        out_specs=[rows, rows, vector, vector, weight, weight],
        scratch_shapes=[pltpu.VMEM((4, n, width), BF16)] * 2
        + [pltpu.VMEM((2, d, 2 * width), BF16)] * 2
        + exchange_sems(1, 2),
        out_shape=[
            jax.ShapeDtypeStruct((n, d), F32), jax.ShapeDtypeStruct((n, d), F32),
            jax.ShapeDtypeStruct((1, d), F32), jax.ShapeDtypeStruct((1, d), F32),
            jax.ShapeDtypeStruct((d, 2 * width), BF16), jax.ShapeDtypeStruct((d, 2 * width), F32),
        ],
        compiler_params=params_of(collective_id=2, has_side_effects=True),
        name="glu_back_kernel",
    )(g_far, g_own, residual, cot, value, sig, act, value_w, gate_w, gain)


def ffn_body(
    n2, n2t, gl, ia, ib, oa, ob, ffn, gn2, in_ref, out_ref,
    wi, wo, h, gp, in_mine, out_mine, in_theirs, out_theirs, send, recv,
):
    step, half = pl.program_id(0), in_mine.shape[0]
    first = step < half
    cores = CoreExchange([(in_mine, in_theirs), (out_mine, out_theirs)], send, recv)
    pl.when(step == 0)(cores.greet)

    @pl.when(first)
    def _():
        wi[...] = ia[...]
        wo[...] = oa[...]

    @pl.when(jnp.logical_not(first))
    def _():
        wi[...] = ib[...]
        wo[...] = ob[...]

    @pl.when(step == 0)
    def _():
        ffn[...] = jnp.zeros_like(ffn)
        gn2[...] = jnp.zeros_like(gn2)

    w1, w2 = wi[...], wo[...]
    for r in range(n2.shape[0] // TOKEN_ROWS):
        at = pl.ds(r * TOKEN_ROWS, TOKEN_ROWS)
        act, slope = gelu_both(dot(n2[at, :], w1))
        hidden = act.astype(BF16)
        grad_pre = (contract_cols(gl[at, :], w2) * slope).astype(BF16)
        h[at, :] = hidden
        gp[at, :] = grad_pre
        ffn[at, :] += dot(hidden, w2)
        gn2[at, :] += contract_cols(grad_pre, w1)
    out_grad = contract_rows(h[...], gl[...])
    in_grad = dot(n2t[...], gp[...])

    pl.when(step == 0)(cores.meet)

    @pl.when(first)
    def _():
        in_mine[step] = in_grad.astype(BF16)
        out_mine[step] = out_grad.astype(BF16)
        cores.start(step)

    @pl.when(jnp.logical_not(first))
    def _():
        cores.arrived(step - half)
        in_ref[...] = (in_grad + in_theirs[step - half].astype(F32)).astype(in_ref.dtype)
        out_ref[...] = (out_grad + out_theirs[step - half].astype(F32)).astype(out_ref.dtype)

    @pl.when(step == 2 * half - 1)
    def _():
        cores.sent(half)


def ffn_kernel(n2, n2t, gl, ins, outs, units, own):
    n, d = n2.shape
    half = units // FFN_TILE

    def whole(a):
        return pl.BlockSpec(a.shape, lambda s: (0, 0), pipeline_mode=pl.Buffered(1))

    def fst(s):
        at = jnp.minimum(s, half - 1)
        return at + (1 - lax.axis_index("core")) * half if own else at

    def snd(s):
        at = jnp.maximum(s - half, 0)
        return at + lax.axis_index("core") * half if own else at

    total = pl.BlockSpec((n, d), lambda s: (0, 0))
    dtype = F32 if own else BF16
    return pl.pallas_call(
        ffn_body,
        grid=(2 * half,),
        in_specs=[
            whole(n2), whole(n2t), whole(gl),
            pl.BlockSpec((d, FFN_TILE), lambda s: (0, fst(s))),
            pl.BlockSpec((d, FFN_TILE), lambda s: (0, snd(s))),
            pl.BlockSpec((FFN_TILE, d), lambda s: (fst(s), 0)),
            pl.BlockSpec((FFN_TILE, d), lambda s: (snd(s), 0)),
        ],
        out_specs=[
            total, total,
            pl.BlockSpec((d, FFN_TILE), lambda s: (0, jnp.maximum(s - half, 0))),
            pl.BlockSpec((FFN_TILE, d), lambda s: (jnp.maximum(s - half, 0), 0)),
        ],
        scratch_shapes=[
            pltpu.VMEM((d, FFN_TILE), BF16), pltpu.VMEM((FFN_TILE, d), BF16),
            pltpu.VMEM((n, FFN_TILE), BF16), pltpu.VMEM((n, FFN_TILE), BF16),
        ]
        + [pltpu.VMEM((half, d, FFN_TILE), BF16), pltpu.VMEM((half, FFN_TILE, d), BF16)] * 2
        + exchange_sems(2, half),
        out_shape=[
            jax.ShapeDtypeStruct((n, d), F32), jax.ShapeDtypeStruct((n, d), F32),
            jax.ShapeDtypeStruct((d, units), dtype), jax.ShapeDtypeStruct((units, d), dtype),
        ],
        compiler_params=params_of(collective_id=int(own), has_side_effects=True),
        name="ffn_kernel",
    )(n2, n2t, gl, *ins, *outs)


def norm_forward(values, norm_gain, norm_bias):
    center = values - jnp.mean(values, axis=-1, keepdims=True)
    inv_std = lax.rsqrt(jnp.mean(center * center, axis=-1, keepdims=True) + norm_eps)
    standard = center * inv_std
    return (standard * norm_gain + norm_bias, standard, inv_std)


def norm_backward(incoming, standard, inv_std, norm_gain):
    scaled = incoming * norm_gain
    value_grad = inv_std * (
        scaled
        - jnp.mean(scaled, axis=-1, keepdims=True)
        - standard * jnp.mean(scaled * standard, axis=-1, keepdims=True)
    )
    return (value_grad, jnp.sum(incoming * standard, axis=0), jnp.sum(incoming, axis=0))


def contract_rows(left, right):
    return lax.dot_general(left, right, (((0,), (0,)), ((), ())), preferred_element_type=F32)


def contract_cols(left, right):
    return lax.dot_general(left, right, (((1,), (1,)), ((), ())), preferred_element_type=F32)


SWAP = ((0, 1), (1, 0))


def over_core(values):
    return lax.ppermute(values, "core", SWAP)


def over_tensor(values):
    return lax.ppermute(values, "tensor", SWAP)


def over_pair(values, flip):
    size = lax.axis_size("pair")
    return lax.ppermute(values, "pair", [(p, p ^ flip) for p in range(size)])


def bit_groups():
    bits = log2_of(lax.axis_size("pair"))
    return [(0, 1)] + [(b, min(2, bits - b)) for b in range(1, bits, 2)]


def place_in(group):
    first, count = group
    return (lax.axis_index("pair") // (1 << first)) % (1 << count)


def flips_of(group):
    first, count = group
    return [j << first for j in range(1, 1 << count)]


def by_groups(values):
    sizes = [1 << count for _, count in bit_groups()]
    return values.reshape(*sizes, values.shape[0] // math.prod(sizes), values.shape[1])


def scatter_parts(total, i):
    me = place_in(bit_groups()[i])

    def at(place):
        return lax.dynamic_slice_in_dim(total, place, 1, i)

    return at(me), [at(me ^ j).astype(BF16) for j in range(1, total.shape[i])]


def gathered(keep, come, group, axis):
    me = place_in(group)
    parts = [keep] + come
    bit = 1
    while bit < len(parts):
        swapped = (me & bit) != 0
        parts = [jnp.where(swapped, parts[k ^ bit], parts[k]) for k in range(len(parts))]
        bit *= 2
    return jnp.concatenate(parts, axis=axis)


def ordered(index, mine, other, axis):
    first = jnp.where(index == 0, mine, other)
    second = jnp.where(index == 0, other, mine)
    return jnp.concatenate([first, second], axis=axis)


def part(values, index, axis):
    half = values.shape[axis] // 2
    return lax.dynamic_slice_in_dim(values, index * half, half, axis)


def together(*values):
    return lax.optimization_barrier(values)


class Reduction:
    def __init__(self, keep, arrivals, done=0):
        groups = range(len(bit_groups()))
        self.keep, self.flying, self.shared = keep, arrivals, None
        self.steps = [("scatter", i) for i in groups[done:]]
        self.steps += [("share", i) for i in reversed(groups)] + [("core", 0)]

    def advance(self):
        kind, i = self.steps.pop(0)
        if self.shared is not None:
            self.keep = gathered(self.keep, self.flying, bit_groups()[self.shared], self.shared)
        else:
            self.keep = sum((come.astype(F32) for come in self.flying), self.keep)
        if kind == "scatter":
            self.keep, self.boxes = scatter_parts(self.keep, i)
        else:
            self.keep = self.keep.astype(BF16)
            self.boxes, self.shared = [self.keep], i
        self.kind = kind, i

    def launch(self):
        kind, i = self.kind
        if kind == "core":
            return [over_core(self.boxes[0])]
        flips = flips_of(bit_groups()[i])
        boxes = self.boxes if kind == "scatter" else self.boxes * len(flips)
        return [over_pair(box, flip) for box, flip in zip(boxes, flips)]

    def result(self):
        return tuple(v.reshape(-1, v.shape[-1]) for v in (self.keep, self.flying[0]))


class SmallSum:
    def __init__(self, keep, arrivals):
        self.keep, self.flying = keep, arrivals
        self.steps = [flips_of(group) for group in bit_groups()] + [None]

    def advance(self):
        self.keep = sum(self.flying, self.keep)
        self.boxes, self.flips = [self.keep], self.steps.pop(0)

    def launch(self):
        if self.flips is None:
            return [over_core(self.boxes[0])]
        return [over_pair(self.boxes[0], flip) for flip in self.flips]

    def result(self):
        return self.keep, self.flying[0]


def proceed(main, *sums):
    sums = [s for s in sums if s.steps]
    if not sums:
        return main
    main, flying = together(main, [s.flying for s in sums])
    for s, come in zip(sums, flying):
        s.flying = come
        s.advance()
    main, boxes, keeps = together(main, [s.boxes for s in sums], [s.keep for s in sums])
    for s, box, keep in zip(sums, boxes, keeps):
        s.keep, s.boxes = keep, box
        s.flying = s.launch()
    return main


def shards(
    inputs, counts, ln1_gain, ln1_bias, log_dt, log_a, freq, c_real, c_imag, skip_gain,
    w_value, w_gate, ln2_gain, ln2_bias, w_in, w_out, cotangent,
):
    _, length, width = inputs.shape
    core, side = lax.axis_index("core"), lax.axis_index("tensor")
    where = jnp.stack([side, core]).astype(jnp.int32)
    used_flag = (side < counts[0]).astype(F32)
    source = inputs.reshape(length, width).astype(F32)
    gain_first, bias_first = ln1_gain.astype(F32), ln1_bias.astype(F32)
    gain_second, bias_second = ln2_gain.astype(F32), ln2_bias.astype(F32)
    table = transform_table(length)
    fwd = jnp.asarray(table.astype(ml_dtypes.bfloat16))
    inv = jnp.asarray(np.ascontiguousarray((table.T / length).astype(ml_dtypes.bfloat16)))

    packed = jnp.concatenate([log_a, freq, c_real, c_imag], axis=1)
    vectors = jnp.stack([log_dt, skip_gain])
    core_next, packed, vectors = together(core, packed, vectors)
    packed_other, vectors_other = over_tensor(packed), over_tensor(vectors)
    share = (0, min(2, log2_of(lax.axis_size("pair"))))
    place, flips = place_in(share), flips_of(share)

    def asked(weight):
        rows = weight.shape[0] // (len(flips) + 1)
        return over_tensor(lax.dynamic_slice_in_dim(weight, place * rows, rows, 0))

    def handed(rows):
        return [over_pair(rows, flip) for flip in flips]

    def joined(rows, come):
        return gathered(rows, come, share, 0)

    glu_mine = jnp.concatenate([part(w_value, core_next, 1), part(w_gate, core_next, 1)], axis=1)
    glu_rows = asked(glu_mine)
    in_rows, out_rows = asked(part(w_in, core_next, 1)), asked(part(w_out, core_next, 0))
    own, own_dt = part(packed, core, 0), part(vectors[:1], core, 1)
    own_kernel = make_kernel(own, own_dt, length)
    own_kernel, packed_other, glu_rows = together(own_kernel, packed_other, glu_rows)
    glu_come = handed(glu_rows)
    other, other_dt = part(packed_other, core, 0), part(vectors_other[:1], core, 1)
    other_kernel = make_kernel(other, other_dt, length)
    normed1_full, standard1, inv_std1 = norm_forward(source, gain_first, bias_first)
    normed1 = normed1_full.astype(BF16)
    skip = ordered(side, vectors[1:], vectors_other[1:], 1)
    other_kernel, in_rows, normed1 = together(other_kernel, in_rows, normed1)
    in_come = handed(in_rows)
    kernels = (own_kernel, over_core(own_kernel), other_kernel, over_core(other_kernel))
    conv = conv_forward(where, normed1, kernels, skip, fwd, inv)
    (mixed, act, spectrum, kernel_spectrum), glu_come, in_come, out_rows = together(
        conv, glu_come, in_come, out_rows
    )
    out_come = handed(out_rows)
    glu_direct = joined(glu_rows, glu_come)
    glu_via = over_core(glu_direct)
    cut = glu_direct.shape[1] // 2
    value_far = ordered(core, glu_direct[:, :cut], glu_via[:, :cut], 1)
    gate_far = ordered(core, glu_direct[:, cut:], glu_via[:, cut:], 1)
    value_w, gate_w = ordered(side, w_value, value_far, 1), ordered(side, w_gate, gate_far, 1)
    gain_second, bias_second = gain_second[None], bias_second[None]
    glu = glu_kernel(act, inputs.reshape(length, width), value_w, gate_w, gain_second, bias_second)
    (value_proj, gate_sig, residual, normed2, normed2_t), out_come = together(glu, out_come)
    grad_low = (used_flag * cotangent.reshape(length, width).astype(F32)).astype(BF16)
    in_direct, out_direct = joined(in_rows, in_come), joined(out_rows, out_come)
    units = in_direct.shape[1]
    far_ffn, far_normed2, there_in, there_out = ffn_kernel(
        normed2, normed2_t, grad_low, (over_core(in_direct), in_direct),
        (over_core(out_direct), out_direct), units, False,
    )
    keep, boxes = scatter_parts(by_groups(there_in), 0)
    normed2, there_out, boxes, keep = together(normed2, there_out, boxes, keep)
    out_come, in_come = over_tensor(there_out), over_pair(boxes[0], 1)
    own_sums = ffn_kernel(normed2, normed2_t, grad_low, (w_in, w_in), (w_out, w_out), units, True)
    own_sums, out_come, in_come = together(own_sums, out_come, in_come)
    own_ffn, own_normed2, here_in, here_out = own_sums
    there_in = (keep.astype(F32) + in_come.astype(F32)).astype(BF16)
    here_in, boxes = scatter_parts(by_groups(here_in), 0)
    out_sum = Reduction(by_groups(here_out), [by_groups(out_come)])
    out_sum.advance()
    own_normed2, there_in, boxes, here_in, out_sum.boxes, out_sum.keep = together(
        own_normed2, there_in, boxes, here_in, out_sum.boxes, out_sum.keep
    )
    out_sum.flying = out_sum.launch()
    in_come = over_tensor(there_in)
    back = glu_back_kernel(
        far_normed2, own_normed2, residual, grad_low, value_proj, gate_sig, act, value_w, gate_w,
        gain_second,
    )
    back, out_sum.flying, in_come = together(back, out_sum.flying, in_come)
    grad_residual, grad_act, gain_second_grad, bias_second_grad, there_glu, here_glu = back
    here_in = here_in + in_come.astype(F32)
    out_sum.advance()
    grad_act, there_glu, here_glu, out_sum.boxes, out_sum.keep, here_in, boxes = together(
        grad_act, there_glu, here_glu, out_sum.boxes, out_sum.keep, here_in, boxes
    )
    out_sum.flying = out_sum.launch()
    in_sum = Reduction(here_in, [over_pair(boxes[0], 1)], 1)
    glu_sum = Reduction(by_groups(here_glu), [by_groups(over_tensor(there_glu))])

    conv = conv_backward(
        grad_act, mixed, normed1, spectrum, kernel_spectrum, skip, fwd, inv
    )
    grad_normed1, grad_kernel, skip_grad = conv = proceed(conv, out_sum, glu_sum, in_sum)
    moments_far = make_moments(other, other_dt, grad_kernel, 0)
    moments_far, grad_kernel = proceed((moments_far, grad_kernel), out_sum, glu_sum, in_sum)
    moments = make_moments(own, own_dt, grad_kernel, 1)
    moments = proceed(moments, out_sum, glu_sum, in_sum)
    grad_normed1, moments = together(grad_normed1, moments)
    grad_source, gain_first_grad, bias_first_grad = norm_backward(
        grad_normed1, standard1, inv_std1, gain_first
    )
    input_grad = (grad_residual + grad_source).astype(BF16).reshape(inputs.shape)
    output = (used_flag * (residual + (far_ffn + own_ffn))).astype(BF16).reshape(inputs.shape)

    rows = jnp.concatenate(
        [skip_grad, gain_first_grad[None], bias_first_grad[None], gain_second_grad, bias_second_grad]
        + [jnp.zeros((3, width), F32)],
        axis=0,
    )

    def shared(at):
        half = part(rows, at, 1)
        return part(half, core, 1) + over_core(part(half, 1 - core, 1))

    small_keep = jnp.concatenate([moments, shared(side)], axis=0)
    small_box = jnp.concatenate([moments_far, shared(1 - side)], axis=0)
    small = SmallSum(small_keep, [over_tensor(small_box)])
    token = small_keep
    while out_sum.steps or in_sum.steps or glu_sum.steps or small.steps:
        token = proceed(token, out_sum, in_sum, glu_sum, small)

    def whole_of(pieces, axis):
        return ordered(core, *pieces, axis).astype(F32)

    small = ordered(core, *small.result(), 1)
    out_total = whole_of(out_sum.result(), 0)
    in_total = whole_of(in_sum.result(), 1)
    glu_mine, glu_other = glu_sum.result()
    cols = glu_mine.shape[1] // 2
    value_total = whole_of((glu_mine[:, :cols], glu_other[:, :cols]), 1)
    gate_total = whole_of((glu_mine[:, cols:], glu_other[:, cols:]), 1)

    modes = log_a.shape[1]
    top = 4 * modes
    return (
        output,
        input_grad,
        small[top + 9],
        small[top + 10],
        small[top],
        small[:modes].T,
        small[modes : 2 * modes].T,
        small[2 * modes : 3 * modes].T,
        small[3 * modes : 4 * modes].T,
        small[top + 8],
        value_total,
        gate_total,
        small[top + 11],
        small[top + 12],
        in_total,
        out_total,
    )


def solution(mesh):
    devices = mesh.devices
    cores = jax.sharding.Mesh(
        devices.reshape(devices.shape[0] // 2, 2, devices.shape[1]), ("pair", "core", "tensor")
    )
    batch, every = ("pair", "core"), ("pair", "core", "tensor")
    in_specs = (
        P(every, None, None), P(batch), P(), P(), P("tensor"), P("tensor", None), P("tensor", None),
        P("tensor", None), P("tensor", None), P("tensor"), P(None, "tensor"), P(None, "tensor"),
        P(), P(), P(None, "tensor"), P("tensor", None), P(every, None, None),
    )
    out_specs = (
        P(every, None, None), P(every, None, None), P("tensor"), P("tensor"), P("tensor"),
        P("tensor", None), P("tensor", None), P("tensor", None), P("tensor", None), P("tensor"),
        P(None, "tensor"), P(None, "tensor"), P("tensor"), P("tensor"), P(None, "tensor"),
        P("tensor", None),
    )
    return jax.shard_map(shards, mesh=cores, in_specs=in_specs, out_specs=out_specs, check_vma=False)
```

time: 661 us -> 451 us (0.68)
  waiting for transfers between devices: 255 us -> 72.6 us
  matrix products: 134 us -> 0 us
  Pallas kernels: 132 us -> 206 us
  starting transfers between devices: 14.2 us -> 74 us
  between operations: 17.4 us -> 2.5 us
  other arithmetic: 68.6 us -> 61.6 us
    psum x2 -> x0, waiting for transfers between devices: 154 us -> none  [the longest x1 82.1 us: shards(): small = lax.psum(mine, ('pair', 'core'))]
    dot_general x24 -> x0, matrix products: 134 us -> none  [the longest x8 50 us: contract_cols(): lax.dot_general(left, right, (((1,), (1,)), ((), ())), preferred_element_...]
    ppermute x10 -> x9, waiting for transfers between devices: 100 us -> 4.44 us  [over_tensor(): return lax.ppermute(values, 'tensor', SWAP)]
    pallas_call x2 -> x7, Pallas kernels: 71.4 us -> 164 us  [the longest x2 79.8 us: ffn_kernel(): pl.pallas_call(ffn_body, grid=(2 * half,), in_specs=[whole(n2), whole(n2t...]
    ppermute x0 -> x38, waiting for transfers between devices: none -> 65.5 us  [over_pair(): return lax.ppermute(values, 'pair', [(p, p ^ flip) for p in range(size)])]
    ppermute x0 -> x38, starting transfers between devices: none -> 60.5 us  [over_pair(): return lax.ppermute(values, 'pair', [(p, p ^ flip) for p in range(size)])]
    pallas_call x1 -> x2, Pallas kernels: 36.9 us -> 18.1 us  [make_kernel(): pl.pallas_call(kernel_body, grid=(channels // LANES,), in_specs=[pl.Block...]
    convert_element_type x15 -> x9, other arithmetic: 38.2 us -> 20 us  [the longest x4 12.1 us: whole_of(): return ordered(core, *pieces, axis).astype(F32)]
  transfers between devices with their start and end apart: 28 -> 58, of which waited for: 5 -> 17; matrix products, arithmetic and copies ran while one was open for 32% -> 11% of each run, Pallas kernels for 20% -> 37%
where the time goes in v2:
time: 451 us; the launch traced here: 447 us
  Pallas kernels  206 us (46%)
  starting transfers between devices  74 us (16%)
  waiting for transfers between devices  72.6 us (16%)
  other arithmetic  61.6 us (14%)
  local copies, waits for them, and re-layouts  31.2 us (7%)
    pallas_call x2, Pallas kernels, ffn_kernel(): pl.pallas_call(ffn_body, grid=(2 * half,), in_specs=[whole(n2), whole(n2t...  79.8 us
    ppermute x38, waiting for transfers between devices, over_pair(): return lax.ppermute(values, 'pair', [(p, p ^ flip) for p in range(size)])  65.5 us
    ppermute x38, starting transfers between devices, over_pair(): return lax.ppermute(values, 'pair', [(p, p ^ flip) for p in range(size)])  60.5 us
    pallas_call x2, Pallas kernels, make_moments(): pl.pallas_call(moments_body, grid=(half // LANES,), in_specs=[pl.BlockSpe...  27.5 us
    pallas_call x1, Pallas kernels, conv_backward(): pl.pallas_call(back_body, grid=(channels // CB,), in_specs=[col(n), col(n...  23.6 us
    pallas_call x1, Pallas kernels, glu_back_kernel(): pl.pallas_call(glu_back_body, grid=(chunks + 4,), in_specs=[rows] * 6 + [...  23.4 us
    pallas_call x1, Pallas kernels, conv_forward(): pl.pallas_call(conv_body, grid_spec=pltpu.PrefetchScalarGridSpec(num_scal...  21.8 us
    pallas_call x2, Pallas kernels, make_kernel(): pl.pallas_call(kernel_body, grid=(channels // LANES,), in_specs=[pl.Block...  18.1 us
  transfers between devices with their start and end apart: 58, of which 17 were waited for; matrix products, arithmetic and copies ran while one was open for 11% of the time, Pallas kernels for 37%

profile of v2, /device:TPU:0, one launch (start us, length us, event | category | flops | bytes accessed | tf_op | source)
XLA Modules:
  0.0 447.5 jit_solution(12111045709917448080)
XLA Ops:
  5.6 3.0 collective-permute-start.2
  19.1 9.2 %make_kernel.2.k0 = bf16[1024,256]{1,0:T(8,128)(2,1)} custom-call(f32[256,128]{1,0:T(8,128)} %constant_dynamic-slice_fusion.18.packed_ref, f32[1,256]{1,0:T(1,128)} %constant_dynamic-slice_fusion.17.log_dt_ref), custom_call_target="tpu_custom_call" | custom-call | tf_op jit(solution)/shard_map/make_kernel/pallas_call | solution.py:177
  34.5 8.9 %make_kernel.3.k2 = bf16[1024,256]{1,0:T(8,128)(2,1)} custom-call(f32[256,128]{1,0:T(8,128)} %constant_dynamic-slice_fusion.14.packed_ref, f32[1,256]{1,0:T(1,128)} %constant_dynamic-slice_fusion.13.log_dt_ref), custom_call_target="tpu_custom_call" | custom-call | tf_op jit(solution)/shard_map/make_kernel/pallas_call | solution.py:177
  48.5 3.9 collective-permute-done.7
  54.3 2.7 collective-permute-start.8
  58.2 21.8 %conv_forward.1 = (f32[1024,1024]{1,0:T(8,128)}, bf16[1024,1024]{1,0:T(8,128)(2,1)}, bf16[2048,1024]{1,0:T(8,128)(2,1)}, bf16[2048,1024]{1,0:T(8,128)(2,1)}) custom-call(s32[2]{0:T(128)} %pad_add_fusion.where_ref, bf16[1024,1024]{1,0:T(8,128)(2,1)} %fusion.7.x_ref, bf16[1024,256]{1,0:T(8,128)(2,1)} %make_kernel.2.k0, ...), custom_call_target="tpu_custom_call" | custom-call | tf_op jit(solution)/shard_map/conv_forward/pallas_call | solution.py:319
  95.8 11.5 %glu_kernel.1 = (bf16[1024,1024]{1,0:T(8,128)(2,1)}, bf16[1024,1024]{1,0:T(8,128)(2,1)}, f32[1024,1024]{1,0:T(8,128)}, bf16[1024,1024]{1,0:T(8,128)(2,1)}, bf16[1024,1024]{1,0:T(8,128)(2,1)}) custom-call(bf16[1024,1024]{1,0:T(8,128)(2,1)} %get-tuple-element.193.act, bf16[1024,1024]{1,0:T(8,128)(2,1)} %bitcast.48, ...), custom_call_target="tpu_custom_call" | custom-call | tf_op jit(solution)/shard_map/glu_kernel/pallas_call | solution.py:442
  107.3 4.9 %collective-permute-done.16 = bf16[256,1024]{1,0:T(8,128)(2,1)S(1)} collective-permute-done((bf16[256,1024]{1,0:T(8,128)(2,1)}, bf16[256,1024]{1,0:T(8,128)(2,1)S(1)}, u32[]{:S(2)}, u32[]{:S(2)}) %collective-permute-start.16) | collective-permute-done | bytes 524320 | tf_op jit(solution)/shard_map/ppermute | solution.py:689
  115.6 3.4 fusion.15.gl.cot
  119.4 39.7 %ffn_kernel.2 = (f32[1024,1024]{1,0:T(8,128)}, f32[1024,1024]{1,0:T(8,128)}, bf16[1024,1024]{1,0:T(8,128)(2,1)}, bf16[1024,1024]{1,0:T(8,128)(2,1)}) custom-call(bf16[1024,1024]{1,0:T(8,128)(2,1)} %get-tuple-element.215.n2, bf16[1024,1024]{1,0:T(8,128)(2,1)} %get-tuple-element.205.n2t, bf16[1024,1024]{1,0:T(8,128)(2,1)} %fusion.15.gl.cot, ...), custom_call_target="tpu_custom_call" | custom-call | tf_op jit(solution)/shard_map/ffn_kernel/pallas_call | solution.py:621
  164.5 40.1 %ffn_kernel.3 = (f32[1024,1024]{1,0:T(8,128)}, f32[1024,1024]{1,0:T(8,128)}, f32[1024,1024]{1,0:T(8,128)}, f32[1024,1024]{1,0:T(8,128)}) custom-call(bf16[1024,1024]{1,0:T(8,128)(2,1)} %get-tuple-element.215.n2, bf16[1024,1024]{1,0:T(8,128)(2,1)} %get-tuple-element.205.n2t, bf16[1024,1024]{1,0:T(8,128)(2,1)} %fusion.15.gl.cot, bf16[1024,2048]{1,0:T(8,128)(2,1)} %ib.1, ...), custom_call_target="tpu_custom_call" | custom-call | tf_op jit(solution)/shard_map/ffn_kernel/pallas_call | solution.py:621
  204.6 4.4 collective-permute-done.19
  209.0 2.7 dynamic-slice_convert_fusion.1
  222.8 23.4 %glu_back_kernel.1 = (f32[1024,1024]{1,0:T(8,128)}, f32[1024,1024]{1,0:T(8,128)}, f32[1,1024]{1,0:T(1,128)}, f32[1,1024]{1,0:T(1,128)}, bf16[1024,512]{1,0:T(8,128)(2,1)}, /*index=5*/f32[1024,512]{1,0:T(8,128)}) custom-call(f32[1024,1024]{1,0:T(8,128)} %get-tuple-element.223.g_far, f32[1024,1024]{1,0:T(8,128)} %get-tuple-element.230.g_own, ...), custom_call_target="tpu_custom_call" | custom-call | tf_op jit(solution)/shard_map/glu_back_kernel/pallas_call | solution.py:530
  255.1 23.6 %conv_backward.1 = (f32[1024,1024]{1,0:T(8,128)}, f32[2,1024,256]{2,1,0:T(8,128)}, f32[1,1024]{1,0:T(1,128)}) custom-call(f32[1024,1024]{1,0:T(8,128)} %get-tuple-element.250.ga_ref, f32[1024,1024]{1,0:T(8,128)} %get-tuple-element.251.mixed_ref, bf16[1024,1024]{1,0:T(8,128)(2,1)} %fusion.7.x_ref, bf16[2048,1024]{1,0:T(8,128)(2,1)} %get-tuple-element.252.xs_ref, ...), custom_call_target="tpu_custom_call" | custom-call | tf_op jit(solution)/shard_map/conv_backward/pallas_call | solution.py:402
  284.9 3.5 collective-permute-start.29
  290.3 8.0 %collective-permute-done.28 = bf16[1,1,128,1024]{3,2,1,0:T(8,128)(2,1)S(1)} collective-permute-done((bf16[1,1,128,1024]{3,2,1,0:T(8,128)(2,1)S(1)}, bf16[1,1,128,1024]{3,2,1,0:T(8,128)(2,1)S(1)}, u32[]{:S(2)}, u32[]{:S(2)}) %collective-permute-start.28) | collective-permute-done | bytes 262176 | tf_op jit(solution)/shard_map/ppermute | solution.py:689
  300.2 6.6 %collective-permute-done.29 = bf16[1,1,128,1024]{3,2,1,0:T(8,128)(2,1)S(1)} collective-permute-done((bf16[1,1,128,1024]{3,2,1,0:T(8,128)(2,1)S(1)}, bf16[1,1,128,1024]{3,2,1,0:T(8,128)(2,1)S(1)}, u32[]{:S(2)}, u32[]{:S(2)}) %collective-permute-start.29) | collective-permute-done | bytes 262176 | tf_op jit(solution)/shard_map/ppermute | solution.py:689
  309.9 13.6 %make_moments.2 = f32[136,256]{1,0:T(8,128)} custom-call(f32[256,128]{1,0:T(8,128)} %constant_dynamic-slice_fusion.14.packed_ref, f32[1,256]{1,0:T(1,128)} %constant_dynamic-slice_fusion.13.log_dt_ref, f32[2,1024,256]{2,1,0:T(8,128)} %get-tuple-element.292.g_ref), custom_call_target="tpu_custom_call" | custom-call | tf_op jit(solution)/shard_map/make_moments/pallas_call | solution.py:240
  323.6 5.6 %collective-permute-done.33 = bf16[1,1,128,1024]{3,2,1,0:T(8,128)(2,1)} collective-permute-done((bf16[1,1,128,1024]{3,2,1,0:T(8,128)(2,1)S(1)}, bf16[1,1,128,1024]{3,2,1,0:T(8,128)(2,1)}, u32[]{:S(2)}, u32[]{:S(2)}) %collective-permute-start.33) | collective-permute-done | bytes 262176 | tf_op jit(solution)/shard_map/ppermute | solution.py:689
  333.3 3.4 collective-permute-start.36
  339.7 5.7 %collective-permute-done.36 = bf16[1,1,128,512]{3,2,1,0:T(8,128)(2,1)} collective-permute-done((bf16[1,1,128,512]{3,2,1,0:T(8,128)(2,1)S(1)}, bf16[1,1,128,512]{3,2,1,0:T(8,128)(2,1)}, u32[]{:S(2)}, u32[]{:S(2)}) %collective-permute-start.36) | collective-permute-done | bytes 131104 | tf_op jit(solution)/shard_map/ppermute | solution.py:689
  349.6 13.9 %make_moments.3 = f32[136,256]{1,0:T(8,128)} custom-call(f32[256,128]{1,0:T(8,128)} %constant_dynamic-slice_fusion.18.packed_ref, f32[1,256]{1,0:T(1,128)} %constant_dynamic-slice_fusion.17.log_dt_ref, f32[2,1024,256]{2,1,0:T(8,128)} %get-tuple-element.292.g_ref), custom_call_target="tpu_custom_call" | custom-call | tf_op jit(solution)/shard_map/make_moments/pallas_call | solution.py:240
  377.3 7.0 %collective-permute-start.44 = (bf16[1,1,128,512]{3,2,1,0:T(8,128)(2,1)S(1)}, bf16[1,1,128,512]{3,2,1,0:T(8,128)(2,1)S(1)}, u32[]{:S(2)}, u32[]{:S(2)}) collective-permute-start(bf16[1,1,128,512]{3,2,1,0:T(8,128)(2,1)S(1)} %add_convert_fusion.3), channel_id=1, source_target_pairs={{0,8},{4,12},{8,0},{12,4},{16,24},{20,28},{24,16},{28,20},{1,9},{5... | collective-permute-start | bytes 393224 | tf_op jit(solution)/shard_map/ppermute | solution.py:689
  386.7 2.7 collective-permute-done.44
  389.4 7.8 %collective-permute-done.45 = bf16[1,1,128,512]{3,2,1,0:T(8,128)(2,1)S(1)} collective-permute-done((bf16[1,1,128,512]{3,2,1,0:T(8,128)(2,1)S(1)}, bf16[1,1,128,512]{3,2,1,0:T(8,128)(2,1)S(1)}, u32[]{:S(2)}, u32[]{:S(2)}) %collective-permute-start.45) | collective-permute-done | bytes 131104 | tf_op jit(solution)/shard_map/ppermute | solution.py:689
  401.3 5.3 %fusion.16 = bf16[1,1024,1024]{2,1,0:T(8,128)(2,1)} fusion(f32[1024,1024]{1,0:T(8,128)S(1)} %copy-done.4, f32[1024,1024]{1,0:T(8,128)S(1)} %copy-done.8, f32[1024,1024]{1,0:T(8,128)} %get-tuple-element.222, f32[]{:T(128)S(6)} %convert_element_type.144), kind=kLoop, calls=%fused_computation.24 | loop fusion | flops 4194304 | bytes 14680068 | tf_op jit(solution)/shard_map/reshape | solution.py:923
  407.4 6.1 %collective-permute-done.50 = f32[144,256]{1,0:T(8,128)S(1)} collective-permute-done((f32[144,256]{1,0:T(8,128)S(1)}, f32[144,256]{1,0:T(8,128)S(1)}, u32[]{:S(2)}, u32[]{:S(2)}) %collective-permute-start.50) | collective-permute-done | bytes 147488 | tf_op jit(solution)/shard_map/ppermute | solution.py:689
  413.8 3.5 collective-permute-start.51
  421.7 8.1 %collective-permute-done.52 = f32[144,256]{1,0:T(8,128)S(1)} collective-permute-done((f32[144,256]{1,0:T(8,128)S(1)}, f32[144,256]{1,0:T(8,128)S(1)}, u32[]{:S(2)}, u32[]{:S(2)}) %collective-permute-start.52) | collective-permute-done | bytes 147488 | tf_op jit(solution)/shard_map/ppermute | solution.py:689
  434.6 4.5 %maximum_convert_fusion.1 = f32[2048,1024]{1,0:T(8,128)} fusion(bf16[1024,1024]{1,0:T(8,128)(2,1)S(1)} %bitcast.54, bf16[1024,1024]{1,0:T(8,128)(2,1)S(1)} %bitcast.53), kind=kLoop, calls=%fused_computation.18 | loop fusion | flops 8388608 | bytes 12582912 | tf_op jit(solution)/shard_map/convert_element_type | solution.py:943
  442.8 4.4 maximum_convert_fusion
  (269 shorter events, 131.8 us)
Async XLA Ops:
  16.6 26.9 %collective-permute-start.3 = (bf16[256,1024]{1,0:T(8,128)(2,1)S(1)}, bf16[256,1024]{1,0:T(8,128)(2,1)S(1)}, u32[]{:S(2)}, u32[]{:S(2)}) collective-permute-start(bf16[256,1024]{1,0:T(8,128)(2,1)S(1)} %dynamic_slice.125), channel_id=1, source_target_pairs={{0,1},{1,0},{2,3},{3,2},{4,5},{5,4},{6,7},{7,6},{8,9},{9,8},{10,11... | collective-permute-start | bytes 1572872 | tf_op jit(solution)/shard_map/ppermute | solution.py:684
  28.3 25.8 %collective-permute-start.4 = (bf16[1024,256]{1,0:T(8,128)(2,1)}, bf16[1024,256]{1,0:T(8,128)(2,1)}, u32[]{:S(2)}, u32[]{:S(2)}) collective-permute-start(bf16[1024,256]{1,0:T(8,128)(2,1)} %make_kernel.2.k0), channel_id=1, source_target_pairs={{0,2},{2,0},{1,3},{3,1},{4,6},{6,4},{5,7},{7,5},{8,10},{10,8},{9,1... | collective-permute-start | bytes 1572872 | tf_op jit(solution)/shard_map/ppermute | solution.py:680
  46.4 36.3 %collective-permute-start.12 = (bf16[256,1024]{1,0:T(8,128)(2,1)S(1)}, bf16[256,1024]{1,0:T(8,128)(2,1)}, u32[]{:S(2)}, u32[]{:S(2)}) collective-permute-start(bf16[256,1024]{1,0:T(8,128)(2,1)S(1)} %constant_dynamic-slice_fusion.12), channel_id=1, source_target_pairs={{0,1},{1,0},{2,3},{3,2},{4,5},{5,4},{6,7},{7,6},{8,9},{9,8},{10,11... | collective-permute-start | bytes 1572872 | tf_op jit(solution)/shard_map/ppermute | solution.py:684
  48.0 34.7 %collective-permute-start.9 = (bf16[256,1024]{1,0:T(8,128)(2,1)S(1)}, bf16[256,1024]{1,0:T(8,128)(2,1)S(1)}, u32[]{:S(2)}, u32[]{:S(2)}) collective-permute-start(bf16[256,1024]{1,0:T(8,128)(2,1)S(1)} %collective-permute-done.3), channel_id=1, source_target_pairs={{0,4},{4,0},{8,12},{12,8},{16,20},{20,16},{24,28},{28,24},{1,5},{5... | collective-permute-start | bytes 1572872 | tf_op jit(solution)/shard_map/ppermute | solution.py:689
  52.5 30.2 %collective-permute-start.10 = (bf16[256,1024]{1,0:T(8,128)(2,1)S(1)}, bf16[256,1024]{1,0:T(8,128)(2,1)S(1)}, u32[]{:S(2)}, u32[]{:S(2)}) collective-permute-start(bf16[256,1024]{1,0:T(8,128)(2,1)S(1)} %collective-permute-done.3), channel_id=1, source_target_pairs={{0,8},{4,12},{8,0},{12,4},{16,24},{20,28},{24,16},{28,20},{1,9},{5... | collective-permute-start | bytes 1572872 | tf_op jit(solution)/shard_map/ppermute | solution.py:689
  54.0 28.6 %collective-permute-start.11 = (bf16[256,1024]{1,0:T(8,128)(2,1)S(1)}, bf16[256,1024]{1,0:T(8,128)(2,1)S(1)}, u32[]{:S(2)}, u32[]{:S(2)}) collective-permute-start(bf16[256,1024]{1,0:T(8,128)(2,1)S(1)} %collective-permute-done.3), channel_id=1, source_target_pairs={{0,12},{4,8},{8,4},{12,0},{16,28},{20,24},{24,20},{28,16},{1,13},{... | collective-permute-start | bytes 1572872 | tf_op jit(solution)/shard_map/ppermute | solution.py:689
  54.3 28.3 %collective-permute-start.8 = (bf16[256,512]{1,0:T(8,128)(2,1)}, bf16[256,512]{1,0:T(8,128)(2,1)}, u32[]{:S(2)}, u32[]{:S(2)}) collective-permute-start(bf16[256,512]{1,0:T(8,128)(2,1)} %collective-permute-done.1), channel_id=1, source_target_pairs={{0,12},{4,8},{8,4},{12,0},{16,28},{20,24},{24,20},{28,16},{1,13},{... | collective-permute-start | bytes 786440 | tf_op jit(solution)/shard_map/ppermute | solution.py:689
  85.3 22.0 %collective-permute-start.14 = (bf16[256,1024]{1,0:T(8,128)(2,1)}, bf16[256,1024]{1,0:T(8,128)(2,1)S(1)}, u32[]{:S(2)}, u32[]{:S(2)}) collective-permute-start(bf16[256,1024]{1,0:T(8,128)(2,1)} %collective-permute-done.12), channel_id=1, source_target_pairs={{0,4},{4,0},{8,12},{12,8},{16,20},{20,16},{24,28},{28,24},{1,5},{5... | collective-permute-start | bytes 1572872 | tf_op jit(solution)/shard_map/ppermute | solution.py:689
  88.4 23.8 %collective-permute-start.16 = (bf16[256,1024]{1,0:T(8,128)(2,1)}, bf16[256,1024]{1,0:T(8,128)(2,1)S(1)}, u32[]{:S(2)}, u32[]{:S(2)}) collective-permute-start(bf16[256,1024]{1,0:T(8,128)(2,1)} %collective-permute-done.12), channel_id=1, source_target_pairs={{0,12},{4,8},{8,4},{12,0},{16,28},{20,24},{24,20},{28,16},{1,13},{... | collective-permute-start | bytes 1572872 | tf_op jit(solution)/shard_map/ppermute | solution.py:689
  89.1 29.9 %collective-permute-start.17 = (bf16[1024,1024]{1,0:T(8,128)(2,1)S(1)}, bf16[1024,1024]{1,0:T(8,128)(2,1)}, u32[]{:S(2)}, u32[]{:S(2)}) collective-permute-start(bf16[1024,1024]{1,0:T(8,128)(2,1)S(1)} %pad_maximum_fusion.2.ib), channel_id=1, source_target_pairs={{0,2},{2,0},{1,3},{3,1},{4,6},{6,4},{5,7},{7,5},{8,10},{10,8},{9,1... | collective-permute-start | bytes 6291464 | tf_op jit(solution)/shard_map/ppermute | solution.py:680
  161.4 47.6 %collective-permute-start.19 = (bf16[1024,1024]{1,0:T(8,128)(2,1)S(1)}, bf16[1024,1024]{1,0:T(8,128)(2,1)S(1)}, u32[]{:S(2)}, u32[]{:S(2)}) collective-permute-start(bf16[1024,1024]{1,0:T(8,128)(2,1)S(1)} %copy-done.38), channel_id=1, source_target_pairs={{0,1},{1,0},{2,3},{3,2},{4,5},{5,4},{6,7},{7,6},{8,9},{9,8},{10,11... | collective-permute-start | bytes 6291464 | tf_op jit(solution)/shard_map/ppermute | solution.py:684
  163.0 41.6 %collective-permute-start.20 = (bf16[1,4,128,1024]{3,2,1,0:T(8,128)(2,1)S(1)}, bf16[1,4,128,1024]{3,2,1,0:T(8,128)(2,1)S(1)}, u32[]{:S(2)}, u32[]{:S(2)}) collective-permute-start(bf16[1,4,128,1024]{3,2,1,0:T(8,128)(2,1)S(1)} %get-tuple-element.221), channel_id=1, source_target_pairs={{0,4},{4,0},{8,12},{12,8},{16,20},{20,16},{24,28},{28,24},{1,5},{5... | collective-permute-start | bytes 3145736 | tf_op jit(solution)/shard_map/ppermute | solution.py:689
  219.7 26.5 %collective-permute-start.21 = (bf16[1,4,128,1024]{3,2,1,0:T(8,128)(2,1)}, bf16[1,4,128,1024]{3,2,1,0:T(8,128)(2,1)S(1)}, u32[]{:S(2)}, u32[]{:S(2)}) collective-permute-start(bf16[1,4,128,1024]{3,2,1,0:T(8,128)(2,1)} %dynamic-slice_convert_fusion), channel_id=1, source_target_pairs={{0,4},{4,0},{8,12},{12,8},{16,20},{20,16},{24,28},{28,24},{1,5},{5... | collective-permute-start | bytes 3145736 | tf_op jit(solution)/shard_map/ppermute | solution.py:689
  221.3 24.9 %collective-permute-start.22 = (bf16[1,4,128,1024]{3,2,1,0:T(8,128)(2,1)}, bf16[1,4,128,1024]{3,2,1,0:T(8,128)(2,1)}, u32[]{:S(2)}, u32[]{:S(2)}) collective-permute-start(bf16[1,4,128,1024]{3,2,1,0:T(8,128)(2,1)} %add_convert_fusion), channel_id=1, source_target_pairs={{0,1},{1,0},{2,3},{3,2},{4,5},{5,4},{6,7},{7,6},{8,9},{9,8},{10,11... | collective-permute-start | bytes 3145736 | tf_op jit(solution)/shard_map/ppermute | solution.py:684
  249.2 29.5 %collective-permute-start.26 = (bf16[1024,512]{1,0:T(8,128)(2,1)}, bf16[1024,512]{1,0:T(8,128)(2,1)S(1)}, u32[]{:S(2)}, u32[]{:S(2)}) collective-permute-start(bf16[1024,512]{1,0:T(8,128)(2,1)} %get-tuple-element.260), channel_id=1, source_target_pairs={{0,1},{1,0},{2,3},{3,2},{4,5},{5,4},{6,7},{7,6},{8,9},{9,8},{10,11... | collective-permute-start | bytes 3145736 | tf_op jit(solution)/shard_map/ppermute | solution.py:684
  250.1 28.6 %collective-permute-start.27 = (bf16[1,4,128,1024]{3,2,1,0:T(8,128)(2,1)}, bf16[1,4,128,1024]{3,2,1,0:T(8,128)(2,1)S(1)}, u32[]{:S(2)}, u32[]{:S(2)}) collective-permute-start(bf16[1,4,128,1024]{3,2,1,0:T(8,128)(2,1)} %dynamic-slice_convert_fusion.1), channel_id=1, source_target_pairs={{0,4},{4,0},{8,12},{12,8},{16,20},{20,16},{24,28},{28,24},{1,5},{5... | collective-permute-start | bytes 3145736 | tf_op jit(solution)/shard_map/ppermute | solution.py:689
  250.7 28.0 %collective-permute-start.23 = (bf16[1,1,128,1024]{3,2,1,0:T(8,128)(2,1)}, bf16[1,1,128,1024]{3,2,1,0:T(8,128)(2,1)S(1)}, u32[]{:S(2)}, u32[]{:S(2)}) collective-permute-start(bf16[1,1,128,1024]{3,2,1,0:T(8,128)(2,1)} %get-tuple-element.257), channel_id=1, source_target_pairs={{0,8},{4,12},{8,0},{12,4},{16,24},{20,28},{24,16},{28,20},{1,9},{5... | collective-permute-start | bytes 786440 | tf_op jit(solution)/shard_map/ppermute | solution.py:689
  252.3 26.4 %collective-permute-start.24 = (bf16[1,1,128,1024]{3,2,1,0:T(8,128)(2,1)}, bf16[1,1,128,1024]{3,2,1,0:T(8,128)(2,1)S(1)}, u32[]{:S(2)}, u32[]{:S(2)}) collective-permute-start(bf16[1,1,128,1024]{3,2,1,0:T(8,128)(2,1)} %get-tuple-element.258), channel_id=1, source_target_pairs={{0,16},{4,20},{8,24},{12,28},{16,0},{20,4},{24,8},{28,12},{1,17},{... | collective-permute-start | bytes 786440 | tf_op jit(solution)/shard_map/ppermute | solution.py:689
  254.8 23.9 %collective-permute-start.25 = (bf16[1,1,128,1024]{3,2,1,0:T(8,128)(2,1)S(1)}, bf16[1,1,128,1024]{3,2,1,0:T(8,128)(2,1)S(1)}, u32[]{:S(2)}, u32[]{:S(2)}) collective-permute-start(bf16[1,1,128,1024]{3,2,1,0:T(8,128)(2,1)S(1)} %get-tuple-element.259), channel_id=1, source_target_pairs={{0,24},{4,28},{8,16},{12,20},{16,8},{20,12},{24,0},{28,4},{1,25},{... | collective-permute-start | bytes 786440 | tf_op jit(solution)/shard_map/ppermute | solution.py:689
  284.9 21.9 %collective-permute-start.29 = (bf16[1,1,128,1024]{3,2,1,0:T(8,128)(2,1)S(1)}, bf16[1,1,128,1024]{3,2,1,0:T(8,128)(2,1)S(1)}, u32[]{:S(2)}, u32[]{:S(2)}) collective-permute-start(bf16[1,1,128,1024]{3,2,1,0:T(8,128)(2,1)S(1)} %add_convert_fusion.2), channel_id=1, source_target_pairs={{0,16},{4,20},{8,24},{12,28},{16,0},{20,4},{24,8},{28,12},{1,17},{... | collective-permute-start | bytes 786440 | tf_op jit(solution)/shard_map/ppermute | solution.py:689
  288.3 40.8 %collective-permute-start.31 = (bf16[1,4,128,512]{3,2,1,0:T(8,128)(2,1)}, bf16[1,4,128,512]{3,2,1,0:T(8,128)(2,1)S(1)}, u32[]{:S(2)}, u32[]{:S(2)}) collective-permute-start(bf16[1,4,128,512]{3,2,1,0:T(8,128)(2,1)} %dynamic-slice_convert_fusion.2), channel_id=1, source_target_pairs={{0,4},{4,0},{8,12},{12,8},{16,20},{20,16},{24,28},{28,24},{1,5},{5... | collective-permute-start | bytes 1572872 | tf_op jit(solution)/shard_map/ppermute | solution.py:689
  289.8 33.8 %collective-permute-start.30 = (bf16[1,1,128,1024]{3,2,1,0:T(8,128)(2,1)S(1)}, bf16[1,1,128,1024]{3,2,1,0:T(8,128)(2,1)}, u32[]{:S(2)}, u32[]{:S(2)}) collective-permute-start(bf16[1,1,128,1024]{3,2,1,0:T(8,128)(2,1)S(1)} %add_convert_fusion.2), channel_id=1, source_target_pairs={{0,24},{4,28},{8,16},{12,20},{16,8},{20,12},{24,0},{28,4},{1,25},{... | collective-permute-start | bytes 786440 | tf_op jit(solution)/shard_map/ppermute | solution.py:689
  290.1 33.4 %collective-permute-start.32 = (bf16[1,1,128,1024]{3,2,1,0:T(8,128)(2,1)S(1)}, bf16[1,1,128,1024]{3,2,1,0:T(8,128)(2,1)S(1)}, u32[]{:S(2)}, u32[]{:S(2)}) collective-permute-start(bf16[1,1,128,1024]{3,2,1,0:T(8,128)(2,1)S(1)} %get-tuple-element.277), channel_id=1, source_target_pairs={{0,8},{4,12},{8,0},{12,4},{16,24},{20,28},{24,16},{28,20},{1,9},{5... | collective-permute-start | bytes 786440 | tf_op jit(solution)/shard_map/ppermute | solution.py:689
  298.4 30.8 %collective-permute-start.33 = (bf16[1,1,128,1024]{3,2,1,0:T(8,128)(2,1)S(1)}, bf16[1,1,128,1024]{3,2,1,0:T(8,128)(2,1)}, u32[]{:S(2)}, u32[]{:S(2)}) collective-permute-start(bf16[1,1,128,1024]{3,2,1,0:T(8,128)(2,1)S(1)} %get-tuple-element.278), channel_id=1, source_target_pairs={{0,16},{4,20},{8,24},{12,28},{16,0},{20,4},{24,8},{28,12},{1,17},{... | collective-permute-start | bytes 786440 | tf_op jit(solution)/shard_map/ppermute | solution.py:689
  307.5 21.6 %collective-permute-start.34 = (bf16[1,1,128,1024]{3,2,1,0:T(8,128)(2,1)S(1)}, bf16[1,1,128,1024]{3,2,1,0:T(8,128)(2,1)}, u32[]{:S(2)}, u32[]{:S(2)}) collective-permute-start(bf16[1,1,128,1024]{3,2,1,0:T(8,128)(2,1)S(1)} %get-tuple-element.279), channel_id=1, source_target_pairs={{0,24},{4,28},{8,16},{12,20},{16,8},{20,12},{24,0},{28,4},{1,25},{... | collective-permute-start | bytes 786440 | tf_op jit(solution)/shard_map/ppermute | solution.py:689
  331.8 33.3 %collective-permute-start.35 = (bf16[1,4,128,1024]{3,2,1,0:T(8,128)(2,1)S(1)}, bf16[1,4,128,1024]{3,2,1,0:T(8,128)(2,1)S(1)}, u32[]{:S(2)}, u32[]{:S(2)}) collective-permute-start(bf16[1,4,128,1024]{3,2,1,0:T(8,128)(2,1)S(1)} %pad_maximum_fusion.9), channel_id=1, source_target_pairs={{0,4},{4,0},{8,12},{12,8},{16,20},{20,16},{24,28},{28,24},{1,5},{5... | collective-permute-start | bytes 3145736 | tf_op jit(solution)/shard_map/ppermute | solution.py:689
  337.7 25.8 %collective-permute-start.39 = (bf16[1,1,128,1024]{3,2,1,0:T(8,128)(2,1)S(1)}, bf16[1,1,128,1024]{3,2,1,0:T(8,128)(2,1)S(1)}, u32[]{:S(2)}, u32[]{:S(2)}) collective-permute-start(bf16[1,1,128,1024]{3,2,1,0:T(8,128)(2,1)S(1)} %add_convert_fusion.1), channel_id=1, source_target_pairs={{0,8},{4,12},{8,0},{12,4},{16,24},{20,28},{24,16},{28,20},{1,9},{5... | collective-permute-start | bytes 786440 | tf_op jit(solution)/shard_map/ppermute | solution.py:689
  339.7 25.4 %collective-permute-start.40 = (bf16[1,1,128,1024]{3,2,1,0:T(8,128)(2,1)S(1)}, bf16[1,1,128,1024]{3,2,1,0:T(8,128)(2,1)S(1)}, u32[]{:S(2)}, u32[]{:S(2)}) collective-permute-start(bf16[1,1,128,1024]{3,2,1,0:T(8,128)(2,1)S(1)} %add_convert_fusion.1), channel_id=1, source_target_pairs={{0,16},{4,20},{8,24},{12,28},{16,0},{20,4},{24,8},{28,12},{1,17},{... | collective-permute-start | bytes 786440 | tf_op jit(solution)/shard_map/ppermute | solution.py:689
  369.3 27.9 %collective-permute-start.43 = (bf16[1,4,128,1024]{3,2,1,0:T(8,128)(2,1)S(1)}, bf16[1,4,128,1024]{3,2,1,0:T(8,128)(2,1)}, u32[]{:S(2)}, u32[]{:S(2)}) collective-permute-start(bf16[1,4,128,1024]{3,2,1,0:T(8,128)(2,1)S(1)} %pad_maximum_fusion.10), channel_id=1, source_target_pairs={{0,4},{4,0},{8,12},{12,8},{16,20},{20,16},{24,28},{28,24},{1,5},{5... | collective-permute-start | bytes 3145736 | tf_op jit(solution)/shard_map/ppermute | solution.py:689
  375.7 21.5 %collective-permute-start.48 = (f32[144,256]{1,0:T(8,128)S(1)}, f32[144,256]{1,0:T(8,128)S(1)}, u32[]{:S(2)}, u32[]{:S(2)}) collective-permute-start(f32[144,256]{1,0:T(8,128)S(1)} %pad_maximum_fusion.15), channel_id=1, source_target_pairs={{0,1},{1,0},{2,3},{3,2},{4,5},{5,4},{6,7},{7,6},{8,9},{9,8},{10,11... | collective-permute-start | bytes 442376 | tf_op jit(solution)/shard_map/ppermute | solution.py:684
  406.6 27.7 %collective-permute-start.57 = (bf16[2,4,128,1024]{3,2,1,0:T(8,128)(2,1)S(1)}, bf16[2,4,128,1024]{3,2,1,0:T(8,128)(2,1)S(1)}, u32[]{:S(2)}, u32[]{:S(2)}) collective-permute-start(bf16[2,4,128,1024]{3,2,1,0:T(8,128)(2,1)S(1)} %copy-done.7), channel_id=1, source_target_pairs={{0,2},{2,0},{1,3},{3,1},{4,6},{6,4},{5,7},{7,5},{8,10},{10,8},{9,1... | collective-permute-start | bytes 6291464 | tf_op jit(solution)/shard_map/ppermute | solution.py:680
  420.1 22.5 %collective-permute-start.56 = (bf16[2,4,128,1024]{3,2,1,0:T(8,128)(2,1)S(1)}, bf16[2,4,128,1024]{3,2,1,0:T(8,128)(2,1)S(1)}, u32[]{:S(2)}, u32[]{:S(2)}) collective-permute-start(bf16[2,4,128,1024]{3,2,1,0:T(8,128)(2,1)S(1)} %pad_maximum_fusion.5), channel_id=1, source_target_pairs={{0,2},{2,0},{1,3},{3,1},{4,6},{6,4},{5,7},{7,5},{8,10},{10,8},{9,1... | collective-permute-start | bytes 6291464 | tf_op jit(solution)/shard_map/ppermute | solution.py:680
  (65 other events, 496.5 us)

commit v3 on v2

--- a/solution.py
+++ b/solution.py
@@ -1,4 +1,4 @@
-import math
+import functools
 
 import ml_dtypes
 import numpy as np
@@ -189,9 +189,7 @@
     )(packed, log_dt)
 
 
-def moments_body(
-    packed_ref, log_dt_ref, g_ref, out_ref, zr, zi, wr, wi, tmp, sums
-):
+def moments_block(packed_ref, log_dt_ref, g_ref, out_ref, zr, zi, wr, wi, tmp, sums):
     step, rate, freq, c_real, c_imag, z = split_params(packed_ref, log_dt_ref)
     inner, outer = zr.shape[1], wr.shape[1]
     z_inner = fill_powers(z, inner, zr, zi, tmp)
@@ -203,7 +201,7 @@
         zero = jnp.zeros((inner, LANES), F32)
         sr, si, tr, ti = zero, zero, zero, zero
         for d in reversed(range(outer)):
-            v = g_ref[0, d * inner : (d + 1) * inner, :]
+            v = g_ref[d * inner : (d + 1) * inner, :]
             sr = sr + v * wr[n, d : d + 1, :]
             si = si + v * wi[n, d : d + 1, :]
             if d > 0:
@@ -232,26 +230,6 @@
     top = 4 * modes
     row = lax.broadcasted_iota(jnp.int32, (8, LANES), 0)
     out_ref[top : top + 8, :] = jnp.where(row == 0, log_dt_grad, 0.0)
-
-
-def make_moments(packed, log_dt, g, at):
-    half, modes = packed.shape[0], packed.shape[1] // 4
-    length = g.shape[1]
-    return pl.pallas_call(
-        moments_body,
-        grid=(half // LANES,),
-        in_specs=[
-            pl.BlockSpec((LANES, 4 * modes), lambda i: (i, 0)),
-            pl.BlockSpec((1, LANES), lambda i: (0, i)),
-            pl.BlockSpec((1, length, LANES), lambda i: (at, 0, i)),
-        ],
-        out_specs=pl.BlockSpec((4 * modes + 8, LANES), lambda i: (0, i)),
-        scratch_shapes=power_scratch(modes, MOMENT_INNER, length // MOMENT_INNER)
-        + [pltpu.VMEM((4, modes, LANES), F32)],
-        out_shape=jax.ShapeDtypeStruct((4 * modes + 8, half), F32),
-        compiler_params=params_of(),
-        name="make_moments",
-    )(packed, log_dt, g)
 
 
 def gelu_both(v):
@@ -673,6 +651,238 @@
     return lax.dot_general(left, right, (((1,), (1,)), ((), ())), preferred_element_type=F32)
 
 
+class Posts:
+    def __init__(self, bits, send, recv):
+        self.bits, self.send, self.recv, self.used = bits, send, recv, 0
+        self.place = lax.axis_index("pair")
+        self.started = []
+
+    def bit(self, b):
+        return lax.rem(lax.div(self.place, 1 << b), 2)
+
+    def device(self, link):
+        if isinstance(link, str):
+            return {link: 1 - lax.axis_index(link)}
+        return {"pair": self.place + (1 - 2 * self.bit(link)) * (1 << link)}
+
+    def block(self, flipped):
+        at = 0
+        for b in range(self.bits):
+            here = 1 - self.bit(b) if flipped >> b & 1 else self.bit(b)
+            at = at + here * (1 << (self.bits - 1 if b == 0 else b - 1))
+        return at
+
+    def slot(self):
+        self.used += 1
+        return self.used - 1
+
+    def copy(self, src, dst, slot, link):
+        return pltpu.make_async_remote_copy(
+            src_ref=src, dst_ref=dst, send_sem=self.send.at[slot], recv_sem=self.recv.at[slot],
+            device_id=self.device(link), device_id_type=MESH,
+        )
+
+    def post(self, src, dst, slot, link):
+        copy = self.copy(src, dst, slot, link)
+        copy.start()
+        self.started.append(copy)
+
+    def await_(self, dst, slot, link):
+        self.copy(dst, dst, slot, link).wait_recv()
+
+    def greet(self):
+        links = list(range(self.bits)) + ["core", "tensor"]
+        barrier = pltpu.get_barrier_semaphore()
+        for link in links:
+            pl.semaphore_signal(barrier, inc=1, device_id=self.device(link), device_id_type=MESH)
+        pl.semaphore_wait(barrier, len(links))
+
+    def finish(self):
+        for copy in self.started:
+            copy.wait_send()
+
+
+def scatter_steps(posts, acc, bits, order, boxes, come):
+    def at(known, flipped):
+        place = 0
+        for i, b in enumerate(bits):
+            here = posts.bit(b)
+            if b in known:
+                bit = 1 - here if known[b] else here
+            else:
+                bit = flipped >> i & 1
+            place = place + bit * (1 << i)
+        return place
+
+    done = {}
+    used = 0
+    for n, b in enumerate(order):
+        rest = [bits.index(i) for i in order[n + 1 :]]
+        combos = [sum((c >> k & 1) << i for k, i in enumerate(rest)) for c in range(1 << len(rest))]
+        slots = []
+        for c, combo in enumerate(combos):
+            slot = posts.slot()
+            boxes[used + c] = acc[at({**done, b: True}, combo)].astype(BF16)
+            posts.post(boxes.at[used + c], come.at[used + c], slot, b)
+            slots.append(slot)
+        yield
+        done[b] = False
+        for c, combo in enumerate(combos):
+            posts.await_(come.at[used + c], slots[c], b)
+            keep = at(done, combo)
+            acc[keep] = acc[keep] + come[used + c].astype(F32)
+        used += len(combos)
+    posts.result = at(done, 0)
+
+
+def gather_steps(posts, own, whole, local):
+    core = lax.axis_index("core")
+    count = 1 << posts.bits
+    slots = {(rel, link): posts.slot() for rel in range(count) for link in ("bit", "core")}
+    first = pltpu.make_async_copy(own, whole.at[core, posts.block(0)], local)
+    first.start()
+
+    def pass_on(src, rel, bits):
+        dst = whole.at[core, posts.block(rel)]
+        for b in bits:
+            posts.post(src, dst, slots[rel ^ (1 << b), "bit"], b)
+        posts.post(src, dst, slots[rel, "core"], "core")
+
+    pass_on(own, 0, reversed(range(posts.bits)))
+    for b in reversed(range(posts.bits)):
+        higher = [sum((c >> k & 1) << (b + 1 + k) for k in range(posts.bits - 1 - b)) for c in range(1 << (posts.bits - 1 - b))]
+        for rest in higher:
+            yield
+            rel = rest | 1 << b
+            block = whole.at[core, posts.block(rel)]
+            posts.await_(block, slots[rel, "bit"], b)
+            pass_on(block, rel, reversed(range(b)))
+    yield
+    first.wait()
+    for rel in range(count):
+        posts.await_(whole.at[1 - core, posts.block(rel)], slots[rel, "core"], "core")
+
+
+def finish_body(
+    in_keep, in_come, out_keep, out_come, glu_keep, glu_come, packed, log_dt, gk, rows_mine,
+    rows_other, in_all, out_all, glu_all, small_all,
+    zr, zi, wr, wi, tmp, sums, moments, rows_come, in_own, out_own, glu_own, out_acc, glu_acc,
+    out_boxes, out_got, glu_boxes, glu_got, small, small_far, small_got, local, send, recv, *, bits
+):
+    posts = Posts(bits, send, recv)
+    posts.greet()
+    near, far = list(range(1, bits)), list(range(2, bits))
+
+    def in_steps():
+        in_own[...] = sum((come[...].astype(F32) for come in in_come), in_keep[...]).astype(BF16)
+        yield from gather_steps(posts, in_own, in_all, local.at[0])
+
+    def out_steps():
+        out_acc[...] = out_keep[...] + out_come[...].astype(F32)
+        yield from scatter_steps(posts, out_acc, far, far, out_boxes, out_got)
+        out_own[...] = out_acc[posts.result].astype(BF16)
+        yield from gather_steps(posts, out_own, out_all, local.at[1])
+
+    def glu_steps():
+        glu_acc[...] = glu_keep[...] + glu_come[...].astype(F32)
+        yield from scatter_steps(posts, glu_acc, near + [0], [0] + near, glu_boxes, glu_got)
+        glu_own[...] = glu_acc[posts.result].astype(BF16)
+        yield from gather_steps(posts, glu_own, glu_all, local.at[2])
+
+    def small_steps():
+        slot = posts.slot()
+        posts.post(rows_other, rows_come, slot, "core")
+        yield
+        posts.await_(rows_come, slot, "core")
+        top = moments.shape[1]
+        for j, ref in ((0, small_far), (1, small)):
+            ref[:top, :] = moments[j]
+            ref[top:, :] = rows_mine[j] + rows_come[j]
+        slot = posts.slot()
+        posts.post(small_far, small_got.at[0], slot, "tensor")
+        yield
+        posts.await_(small_got.at[0], slot, "tensor")
+        small[...] = small[...] + small_got[0]
+        for b in range(bits):
+            slot = posts.slot()
+            small_all[b] = small[...]
+            posts.post(small_all.at[b], small_got.at[1 + b], slot, b)
+            yield
+            posts.await_(small_got.at[1 + b], slot, b)
+            small[...] = small[...] + small_got[1 + b]
+        slot = posts.slot()
+        small_all[bits] = small[...]
+        posts.post(small_all.at[bits], small_got.at[1 + bits], slot, "core")
+        yield
+        posts.await_(small_got.at[1 + bits], slot, "core")
+        small_all[bits + 1] = small_got[1 + bits]
+
+    def block(j, i):
+        at = pl.ds(i * LANES, LANES)
+        moments_block(
+            packed.at[j, at, :], log_dt.at[j, :, at], gk.at[j, :, at], moments.at[j, :, at],
+            zr, zi, wr, wi, tmp, sums,
+        )
+
+    work = [(j, i) for j in range(2) for i in range(packed.shape[1] // LANES)]
+    flows = [in_steps(), glu_steps(), out_steps()]
+    late = small_steps()
+    for flow in flows:
+        next(flow, None)
+    next(late)
+    while flows or late is not None:
+        if work:
+            block(*work.pop(0))
+        flows = [flow for flow in flows if next(flow, posts) is not posts]
+        if not work and late is not None and next(late, posts) is posts:
+            late = None
+    posts.finish()
+
+
+def finish_kernel(in_keep, in_come, out_keep, out_come, glu_keep, glu_come, packed, log_dt, gk, rows_mine, rows_other):
+    bits = log2_of(lax.axis_size("pair"))
+    blocks = 1 << bits
+    half, modes = packed.shape[1], packed.shape[2] // 4
+    length = gk.shape[1]
+    rows, d = in_keep.shape
+    cols = glu_keep.shape[2]
+    kept = len(range(2, bits))
+    small_rows = 4 * modes + 8 + rows_mine.shape[1]
+    vmem = pl.BlockSpec(memory_space=pltpu.VMEM)
+    hbm = pl.BlockSpec(memory_space=pl.ANY)
+    copies = 3 * 2 * blocks + (1 << kept) + blocks + bits + 8
+    operands = (
+        in_keep, in_come, out_keep, out_come, glu_keep, glu_come, packed, log_dt, gk, rows_mine, rows_other
+    )
+    small = pltpu.VMEM((small_rows, half), F32)
+    return pl.pallas_call(
+        functools.partial(finish_body, bits=bits),
+        in_specs=jax.tree.map(lambda _: vmem, operands),
+        out_specs=[hbm, hbm, hbm, vmem],
+        out_shape=[
+            jax.ShapeDtypeStruct((2, blocks, rows, d), BF16),
+            jax.ShapeDtypeStruct((2, blocks, rows, d), BF16),
+            jax.ShapeDtypeStruct((2, blocks, rows, cols), BF16),
+            jax.ShapeDtypeStruct((bits + 2, small_rows, half), F32),
+        ],
+        scratch_shapes=power_scratch(modes, MOMENT_INNER, length // MOMENT_INNER)
+        + [
+            pltpu.VMEM((4, modes, LANES), F32),
+            pltpu.VMEM((2, 4 * modes + 8, half), F32),
+            pltpu.VMEM(rows_mine.shape, F32),
+            pltpu.VMEM((rows, d), BF16), pltpu.VMEM((rows, d), BF16), pltpu.VMEM((rows, cols), BF16),
+            pltpu.VMEM(out_keep.shape, F32), pltpu.VMEM(glu_keep.shape, F32),
+        ]
+        + [pltpu.VMEM((max((1 << kept) - 1, 1), rows, d), BF16)] * 2
+        + [pltpu.VMEM((blocks - 1, rows, cols), BF16)] * 2
+        + [small, small, pltpu.VMEM((bits + 2, small_rows, half), F32)]
+        + [pltpu.SemaphoreType.DMA((3,))]
+        + [pltpu.SemaphoreType.DMA((copies,))] * 2,
+        compiler_params=params_of(collective_id=4, has_side_effects=True),
+        name="finish_kernel",
+    )(*operands)
+
+
 SWAP = ((0, 1), (1, 0))
 
 
@@ -689,11 +899,6 @@
     return lax.ppermute(values, "pair", [(p, p ^ flip) for p in range(size)])
 
 
-def bit_groups():
-    bits = log2_of(lax.axis_size("pair"))
-    return [(0, 1)] + [(b, min(2, bits - b)) for b in range(1, bits, 2)]
-
-
 def place_in(group):
     first, count = group
     return (lax.axis_index("pair") // (1 << first)) % (1 << count)
@@ -704,18 +909,18 @@
     return [j << first for j in range(1, 1 << count)]
 
 
-def by_groups(values):
-    sizes = [1 << count for _, count in bit_groups()]
-    return values.reshape(*sizes, values.shape[0] // math.prod(sizes), values.shape[1])
-
-
-def scatter_parts(total, i):
-    me = place_in(bit_groups()[i])
-
-    def at(place):
-        return lax.dynamic_slice_in_dim(total, place, 1, i)
-
-    return at(me), [at(me ^ j).astype(BF16) for j in range(1, total.shape[i])]
+def pair_bits():
+    return log2_of(lax.axis_size("pair"))
+
+
+def by_bits(values):
+    bits = pair_bits()
+    return values.reshape(*[2] * bits, values.shape[0] >> bits, values.shape[1])
+
+
+def split_over(total, bit):
+    axis = 0 if bit == 0 else pair_bits() - bit
+    return part(total, place_in((bit, 1)), axis), part(total, 1 - place_in((bit, 1)), axis).astype(BF16)
 
 
 def gathered(keep, come, group, axis):
@@ -742,71 +947,6 @@
 
 def together(*values):
     return lax.optimization_barrier(values)
-
-
-class Reduction:
-    def __init__(self, keep, arrivals, done=0):
-        groups = range(len(bit_groups()))
-        self.keep, self.flying, self.shared = keep, arrivals, None
-        self.steps = [("scatter", i) for i in groups[done:]]
-        self.steps += [("share", i) for i in reversed(groups)] + [("core", 0)]
-
-    def advance(self):
-        kind, i = self.steps.pop(0)
-        if self.shared is not None:
-            self.keep = gathered(self.keep, self.flying, bit_groups()[self.shared], self.shared)
-        else:
-            self.keep = sum((come.astype(F32) for come in self.flying), self.keep)
-        if kind == "scatter":
-            self.keep, self.boxes = scatter_parts(self.keep, i)
-        else:
-            self.keep = self.keep.astype(BF16)
-            self.boxes, self.shared = [self.keep], i
-        self.kind = kind, i
-
-    def launch(self):
-        kind, i = self.kind
-        if kind == "core":
-            return [over_core(self.boxes[0])]
-        flips = flips_of(bit_groups()[i])
-        boxes = self.boxes if kind == "scatter" else self.boxes * len(flips)
-        return [over_pair(box, flip) for box, flip in zip(boxes, flips)]
-
-    def result(self):
-        return tuple(v.reshape(-1, v.shape[-1]) for v in (self.keep, self.flying[0]))
-
-
-class SmallSum:
-    def __init__(self, keep, arrivals):
-        self.keep, self.flying = keep, arrivals
-        self.steps = [flips_of(group) for group in bit_groups()] + [None]
-
-    def advance(self):
-        self.keep = sum(self.flying, self.keep)
-        self.boxes, self.flips = [self.keep], self.steps.pop(0)
-
-    def launch(self):
-        if self.flips is None:
-            return [over_core(self.boxes[0])]
-        return [over_pair(self.boxes[0], flip) for flip in self.flips]
-
-    def result(self):
-        return self.keep, self.flying[0]
-
-
-def proceed(main, *sums):
-    sums = [s for s in sums if s.steps]
-    if not sums:
-        return main
-    main, flying = together(main, [s.flying for s in sums])
-    for s, come in zip(sums, flying):
-        s.flying = come
-        s.advance()
-    main, boxes, keeps = together(main, [s.boxes for s in sums], [s.keep for s in sums])
-    for s, box, keep in zip(sums, boxes, keeps):
-        s.keep, s.boxes = keep, box
-        s.flying = s.launch()
-    return main
 
 
 def shards(
@@ -828,7 +968,7 @@
     vectors = jnp.stack([log_dt, skip_gain])
     core_next, packed, vectors = together(core, packed, vectors)
     packed_other, vectors_other = over_tensor(packed), over_tensor(vectors)
-    share = (0, min(2, log2_of(lax.axis_size("pair"))))
+    share = (0, min(2, pair_bits()))
     place, flips = place_in(share), flips_of(share)
 
     def asked(weight):
@@ -877,45 +1017,47 @@
         normed2, normed2_t, grad_low, (over_core(in_direct), in_direct),
         (over_core(out_direct), out_direct), units, False,
     )
-    keep, boxes = scatter_parts(by_groups(there_in), 0)
-    normed2, there_out, boxes, keep = together(normed2, there_out, boxes, keep)
-    out_come, in_come = over_tensor(there_out), over_pair(boxes[0], 1)
+    keep, box = split_over(by_bits(there_in), 0)
+    normed2, there_out, box, keep = together(normed2, there_out, box, keep)
+    out_come, in_come = over_tensor(there_out), over_pair(box, 1)
     own_sums = ffn_kernel(normed2, normed2_t, grad_low, (w_in, w_in), (w_out, w_out), units, True)
     own_sums, out_come, in_come = together(own_sums, out_come, in_come)
     own_ffn, own_normed2, here_in, here_out = own_sums
     there_in = (keep.astype(F32) + in_come.astype(F32)).astype(BF16)
-    here_in, boxes = scatter_parts(by_groups(here_in), 0)
-    out_sum = Reduction(by_groups(here_out), [by_groups(out_come)])
-    out_sum.advance()
-    own_normed2, there_in, boxes, here_in, out_sum.boxes, out_sum.keep = together(
-        own_normed2, there_in, boxes, here_in, out_sum.boxes, out_sum.keep
-    )
-    out_sum.flying = out_sum.launch()
-    in_come = over_tensor(there_in)
+    here_in, in_box = split_over(by_bits(here_in), 0)
+    here_out, out_box = split_over(by_bits(here_out) + by_bits(out_come).astype(F32), 1)
+    own_normed2, there_in, in_box, out_box, here_in, here_out = together(
+        own_normed2, there_in, in_box, out_box, here_in, here_out
+    )
+    in_come = [over_tensor(there_in), over_pair(in_box, 1)]
+    out_come = over_pair(out_box, 2)
     back = glu_back_kernel(
         far_normed2, own_normed2, residual, grad_low, value_proj, gate_sig, act, value_w, gate_w,
         gain_second,
     )
-    back, out_sum.flying, in_come = together(back, out_sum.flying, in_come)
+    back, out_come, in_come = together(back, out_come, in_come)
     grad_residual, grad_act, gain_second_grad, bias_second_grad, there_glu, here_glu = back
-    here_in = here_in + in_come.astype(F32)
-    out_sum.advance()
-    grad_act, there_glu, here_glu, out_sum.boxes, out_sum.keep, here_in, boxes = together(
-        grad_act, there_glu, here_glu, out_sum.boxes, out_sum.keep, here_in, boxes
-    )
-    out_sum.flying = out_sum.launch()
-    in_sum = Reduction(here_in, [over_pair(boxes[0], 1)], 1)
-    glu_sum = Reduction(by_groups(here_glu), [by_groups(over_tensor(there_glu))])
-
+    here_out, out_box = split_over(here_out + out_come.astype(F32), 0)
+    here_in = sum((come.astype(F32) for come in in_come), here_in)
+    here_in = here_in.reshape(-1, *here_in.shape[-2:])
+    others = (1, pair_bits() - 1)
+    in_flips, place = flips_of(others), place_in(others)
+
+    def in_part(at):
+        return lax.dynamic_index_in_dim(here_in, at, 0, False)
+
+    in_boxes = [in_part(place ^ (flip >> 1)).astype(BF16) for flip in in_flips]
+    here_in = in_part(place)
+    grad_act, there_glu, out_box, in_boxes, here_out, here_in = together(
+        grad_act, there_glu, out_box, in_boxes, here_out, here_in
+    )
+    glu_come, out_come = over_tensor(there_glu), over_pair(out_box, 1)
+    in_come = [over_pair(box, flip) for box, flip in zip(in_boxes, in_flips)]
     conv = conv_backward(
         grad_act, mixed, normed1, spectrum, kernel_spectrum, skip, fwd, inv
     )
-    grad_normed1, grad_kernel, skip_grad = conv = proceed(conv, out_sum, glu_sum, in_sum)
-    moments_far = make_moments(other, other_dt, grad_kernel, 0)
-    moments_far, grad_kernel = proceed((moments_far, grad_kernel), out_sum, glu_sum, in_sum)
-    moments = make_moments(own, own_dt, grad_kernel, 1)
-    moments = proceed(moments, out_sum, glu_sum, in_sum)
-    grad_normed1, moments = together(grad_normed1, moments)
+    conv, glu_come, out_come, in_come = together(conv, glu_come, out_come, in_come)
+    grad_normed1, grad_kernel, skip_grad = conv
     grad_source, gain_first_grad, bias_first_grad = norm_backward(
         grad_normed1, standard1, inv_std1, gain_first
     )
@@ -928,27 +1070,25 @@
         axis=0,
     )
 
-    def shared(at):
-        half = part(rows, at, 1)
-        return part(half, core, 1) + over_core(part(half, 1 - core, 1))
-
-    small_keep = jnp.concatenate([moments, shared(side)], axis=0)
-    small_box = jnp.concatenate([moments_far, shared(1 - side)], axis=0)
-    small = SmallSum(small_keep, [over_tensor(small_box)])
-    token = small_keep
-    while out_sum.steps or in_sum.steps or glu_sum.steps or small.steps:
-        token = proceed(token, out_sum, in_sum, glu_sum, small)
-
-    def whole_of(pieces, axis):
-        return ordered(core, *pieces, axis).astype(F32)
-
-    small = ordered(core, *small.result(), 1)
-    out_total = whole_of(out_sum.result(), 0)
-    in_total = whole_of(in_sum.result(), 1)
-    glu_mine, glu_other = glu_sum.result()
-    cols = glu_mine.shape[1] // 2
-    value_total = whole_of((glu_mine[:, :cols], glu_other[:, :cols]), 1)
-    gate_total = whole_of((glu_mine[:, cols:], glu_other[:, cols:]), 1)
+    def quarter(far, theirs):
+        return part(part(rows, (side + far) % 2, 1), (core + theirs) % 2, 1)
+
+    in_all, out_all, glu_all, small = finish_kernel(
+        here_in, in_come, here_out.reshape(-1, *here_out.shape[-2:]),
+        out_come.reshape(-1, *out_come.shape[-2:]),
+        here_glu.reshape(2 * len(in_flips) + 2, -1, here_glu.shape[1]),
+        glu_come.reshape(2 * len(in_flips) + 2, -1, glu_come.shape[1]),
+        jnp.stack([other, own]), jnp.stack([other_dt, own_dt]), grad_kernel,
+        jnp.stack([quarter(1, 0), quarter(0, 0)]), jnp.stack([quarter(1, 1), quarter(0, 1)]),
+    )
+    small = ordered(core, small[-2], small[-1], 1)
+    out_total = out_all.reshape(-1, width).astype(F32)
+    in_all = in_all.reshape(2, width, -1)
+    in_total = jnp.concatenate([in_all[0], in_all[1]], axis=1).astype(F32)
+    glu_all = glu_all.reshape(2, width, -1)
+    cut = glu_all.shape[2] // 2
+    value_total = jnp.concatenate([glu_all[0, :, :cut], glu_all[1, :, :cut]], axis=1).astype(F32)
+    gate_total = jnp.concatenate([glu_all[0, :, cut:], glu_all[1, :, cut:]], axis=1).astype(F32)
 
     modes = log_a.shape[1]
     top = 4 * modes

time: 451 us -> 414 us (0.918)
  Pallas kernels: 206 us -> 272 us
  waiting for transfers between devices: 72.6 us -> 16 us
  starting transfers between devices: 74 us -> 30 us
  other arithmetic: 61.6 us -> 56 us
    pallas_call x2 -> x1, Pallas kernels: 27.5 us -> 93.6 us  [finish_kernel(): pl.pallas_call(functools.partial(finish_body, bits=bits), in_specs=jax.tr...]
    ppermute x38 -> x16, waiting for transfers between devices: 65.5 us -> 10.8 us  [over_pair(): return lax.ppermute(values, 'pair', [(p, p ^ flip) for p in range(size)])]
    ppermute x38 -> x16, starting transfers between devices: 60.5 us -> 19.2 us  [over_pair(): return lax.ppermute(values, 'pair', [(p, p ^ flip) for p in range(size)])]
    dynamic_slice x7 -> x0, local copies, waits for them, and re-layouts: 5.46 us -> none  [at(): return lax.dynamic_slice_in_dim(total, place, 1, i)]
    dynamic_slice x7 -> x9, local copies, waits for them, and re-layouts: 6.29 us -> 11.3 us  [part(): return lax.dynamic_slice_in_dim(values, index * half, half, axis)]
    ppermute x9 -> x8, starting transfers between devices: 12.4 us -> 10.3 us  [over_tensor(): return lax.ppermute(values, 'tensor', SWAP)]
    convert_element_type x7 -> x4, other arithmetic: 15.1 us -> 13.2 us  [the longest x1 5.28 us: shards(): in_total = jnp.concatenate([in_all[0], in_all[1]], axis=1).astype(F32)]
    unnamed x82 -> x68, local copies, waits for them, and re-layouts: 11 us -> 9.67 us
  transfers between devices with their start and end apart: 58 -> 29, of which waited for: 17 -> 5; matrix products, arithmetic and copies ran while one was open for 11% -> 8% of each run, Pallas kernels for 37% -> 34%
where the time goes in v3:
time: 414 us; the launch traced here: 411 us
  Pallas kernels  272 us (66%)
  other arithmetic  56 us (14%)
  local copies, waits for them, and re-layouts  34.8 us (8%)
  starting transfers between devices  30 us (7%)
  waiting for transfers between devices  16 us (4%)
    pallas_call x1, Pallas kernels, finish_kernel(): pl.pallas_call(functools.partial(finish_body, bits=bits), in_specs=jax.tr...  93.6 us
    pallas_call x2, Pallas kernels, ffn_kernel(): pl.pallas_call(ffn_body, grid=(2 * half,), in_specs=[whole(n2), whole(n2t...  79.8 us
    pallas_call x1, Pallas kernels, conv_backward(): pl.pallas_call(back_body, grid=(channels // CB,), in_specs=[col(n), col(n...  23.7 us
    pallas_call x1, Pallas kernels, glu_back_kernel(): pl.pallas_call(glu_back_body, grid=(chunks + 4,), in_specs=[rows] * 6 + [...  23.5 us
    pallas_call x1, Pallas kernels, conv_forward(): pl.pallas_call(conv_body, grid_spec=pltpu.PrefetchScalarGridSpec(num_scal...  21.8 us
    ppermute x16, starting transfers between devices, over_pair(): return lax.ppermute(values, 'pair', [(p, p ^ flip) for p in range(size)])  19.2 us
    pallas_call x2, Pallas kernels, make_kernel(): pl.pallas_call(kernel_body, grid=(channels // LANES,), in_specs=[pl.Block...  18.1 us
    pallas_call x1, Pallas kernels, glu_kernel(): pl.pallas_call(glu_body, grid=(n // TOKEN_ROWS,), in_specs=[rows, rows, w...  11.5 us
  transfers between devices with their start and end apart: 29, of which 5 were waited for; matrix products, arithmetic and copies ran while one was open for 8% of the time, Pallas kernels for 34%

profile of v3, /device:TPU:0, one launch (start us, length us, event | category | flops | bytes accessed | tf_op | source)
XLA Modules:
  0.0 411.0 jit_solution(1185082895117786128)
XLA Ops:
  5.7 3.0 collective-permute-start.2
  11.7 1.9 collective-permute-start.1
  13.7 2.1 dynamic_slice.104
  18.2 9.2 %make_kernel.2.k0 = bf16[1024,256]{1,0:T(8,128)(2,1)} custom-call(f32[256,128]{1,0:T(8,128)} %constant_dynamic-slice_fusion.10.packed_ref, f32[1,256]{1,0:T(1,128)} %constant_dynamic-slice_fusion.9.log_dt_ref), custom_call_target="tpu_custom_call" | custom-call | tf_op jit(solution)/shard_map/make_kernel/pallas_call | solution.py:177
  27.5 2.1 fusion.7.x_ref
  30.2 2.9 collective-permute-start.8
  34.7 8.9 %make_kernel.3.k2 = bf16[1024,256]{1,0:T(8,128)(2,1)} custom-call(f32[256,128]{1,0:T(8,128)} %constant_dynamic-slice_fusion.6.packed_ref, f32[1,256]{1,0:T(1,128)} %constant_dynamic-slice_fusion.5.log_dt_ref), custom_call_target="tpu_custom_call" | custom-call | tf_op jit(solution)/shard_map/make_kernel/pallas_call | solution.py:177
  44.4 2.0 constant_dynamic-slice_fusion.4
  49.4 3.9 collective-permute-done.7
  57.1 21.8 %conv_forward.1 = (f32[1024,1024]{1,0:T(8,128)}, bf16[1024,1024]{1,0:T(8,128)(2,1)}, bf16[2048,1024]{1,0:T(8,128)(2,1)}, bf16[2048,1024]{1,0:T(8,128)(2,1)}) custom-call(s32[2]{0:T(128)} %pad_add_fusion.where_ref, bf16[1024,1024]{1,0:T(8,128)(2,1)} %fusion.7.x_ref, bf16[1024,256]{1,0:T(8,128)(2,1)} %make_kernel.2.k0, bf16[1024,256]{1,0:T(8,128)(2,1)} %copy-done.20, ...), custom_call_target="tpu_custom_call" | custom-call | tf_op jit(solution)/shard_map/conv_forward/pallas_call | solution.py:297
  78.9 1.9 collective-permute-done.6
  87.5 2.2 broadcast_select_fusion.21
  93.8 11.5 %glu_kernel.1 = (bf16[1024,1024]{1,0:T(8,128)(2,1)}, bf16[1024,1024]{1,0:T(8,128)(2,1)}, f32[1024,1024]{1,0:T(8,128)}, bf16[1024,1024]{1,0:T(8,128)(2,1)}, bf16[1024,1024]{1,0:T(8,128)(2,1)}) custom-call(bf16[1024,1024]{1,0:T(8,128)(2,1)} %get-tuple-element.128.act, bf16[1024,1024]{1,0:T(8,128)(2,1)} %bitcast.91, ...), custom_call_target="tpu_custom_call" | custom-call | tf_op jit(solution)/shard_map/glu_kernel/pallas_call | solution.py:420
  105.3 4.9 %collective-permute-done.15 = bf16[256,1024]{1,0:T(8,128)(2,1)S(1)} collective-permute-done((bf16[256,1024]{1,0:T(8,128)(2,1)}, bf16[256,1024]{1,0:T(8,128)(2,1)S(1)}, u32[]{:S(2)}, u32[]{:S(2)}) %collective-permute-start.15) | collective-permute-done | bytes 524320 | tf_op jit(solution)/shard_map/ppermute | solution.py:899
  113.7 3.4 fusion.15.gl.cot
  117.5 39.7 %ffn_kernel.2 = (f32[1024,1024]{1,0:T(8,128)}, f32[1024,1024]{1,0:T(8,128)}, bf16[1024,1024]{1,0:T(8,128)(2,1)}, bf16[1024,1024]{1,0:T(8,128)(2,1)}) custom-call(bf16[1024,1024]{1,0:T(8,128)(2,1)} %get-tuple-element.150.n2, bf16[1024,1024]{1,0:T(8,128)(2,1)} %get-tuple-element.140.n2t, bf16[1024,1024]{1,0:T(8,128)(2,1)} %fusion.15.gl.cot, ...), custom_call_target="tpu_custom_call" | custom-call | tf_op jit(solution)/shard_map/ffn_kernel/pallas_call | solution.py:599
  157.2 2.8 constant_dynamic-slice_fusion.2
  163.0 40.1 %ffn_kernel.3 = (f32[1024,1024]{1,0:T(8,128)}, f32[1024,1024]{1,0:T(8,128)}, f32[1024,1024]{1,0:T(8,128)}, f32[1024,1024]{1,0:T(8,128)}) custom-call(bf16[1024,1024]{1,0:T(8,128)(2,1)} %get-tuple-element.150.n2, bf16[1024,1024]{1,0:T(8,128)(2,1)} %get-tuple-element.140.n2t, bf16[1024,1024]{1,0:T(8,128)(2,1)} %fusion.15.gl.cot, bf16[1024,2048]{1,0:T(8,128)(2,1)} %ib.1, ...), custom_call_target="tpu_custom_call" | custom-call | tf_op jit(solution)/shard_map/ffn_kernel/pallas_call | solution.py:599
  203.1 4.8 %collective-permute-done.19 = bf16[1024,1024]{1,0:T(8,128)(2,1)S(1)} collective-permute-done((bf16[1024,1024]{1,0:T(8,128)(2,1)}, bf16[1024,1024]{1,0:T(8,128)(2,1)S(1)}, u32[]{:S(2)}, u32[]{:S(2)}) %collective-permute-start.19) | collective-permute-done | bytes 2097184 | tf_op jit(solution)/shard_map/ppermute | solution.py:894
  209.3 2.7 dynamic-slice_convert_fusion
  212.0 1.9 constant_dynamic-slice_fusion.1
  218.0 2.6 add_convert_fusion
  224.0 23.5 %glu_back_kernel.1 = (f32[1024,1024]{1,0:T(8,128)}, f32[1024,1024]{1,0:T(8,128)}, f32[1,1024]{1,0:T(1,128)}, f32[1,1024]{1,0:T(1,128)}, bf16[1024,512]{1,0:T(8,128)(2,1)}, /*index=5*/f32[1024,512]{1,0:T(8,128)}) custom-call(f32[1024,1024]{1,0:T(8,128)} %get-tuple-element.158.g_far, f32[1024,1024]{1,0:T(8,128)} %get-tuple-element.165.g_own, ...), custom_call_target="tpu_custom_call" | custom-call | tf_op jit(solution)/shard_map/glu_back_kernel/pallas_call | solution.py:508
  249.2 2.5 convert_add_fusion.1
  257.0 2.6 collective-permute-start.27
  260.4 3.0 fusion.16
  263.5 23.7 %conv_backward.1 = (f32[1024,1024]{1,0:T(8,128)}, f32[2,1024,256]{2,1,0:T(8,128)}, f32[1,1024]{1,0:T(1,128)}) custom-call(f32[1024,1024]{1,0:T(8,128)} %get-tuple-element.185.ga_ref, f32[1024,1024]{1,0:T(8,128)} %get-tuple-element.186.mixed_ref, bf16[1024,1024]{1,0:T(8,128)(2,1)} %fusion.7.x_ref, bf16[2048,1024]{1,0:T(8,128)(2,1)} %get-tuple-element.187.xs_ref, ...), custom_call_target="tpu_custom_call" | custom-call | tf_op jit(solution)/shard_map/conv_backward/pallas_call | solution.py:380
  288.2 4.3 %fusion.13 = (f32[1024]{0:T(1024)S(1)}, f32[1024]{0:T(1024)S(1)}, f32[1024]{0:T(1024)S(1)}, f32[1024]{0:T(1024)S(1)}) fusion(f32[1024,1024]{1,0:T(8,128)} %get-tuple-element.197, f32[1024]{0:T(1024)S(1)} %add_rsqrt_fusion, f32[1024]{0:T(1024)S(1)} %broadcast_multiply_fusion.2, bf16[1,1024,1024]{2,1,0:T(8,128)(2,1)S(1)} %copy-done.1, ...), kind=kLoop, calls=%fused_computation.15 | loop fusion | flops 10481664 | bytes 6320128 | tf_op jit(solution)/shard_map/reduce_sum | solution.py:643
  293.9 93.6 %finish_kernel.1 = (bf16[2,8,128,1024]{3,2,1,0:T(8,128)(2,1)}, bf16[2,8,128,1024]{3,2,1,0:T(8,128)(2,1)}, bf16[2,8,128,512]{3,2,1,0:T(8,128)(2,1)}, f32[5,144,256]{2,1,0:T(8,128)}) custom-call(f32[128,1024]{1,0:T(8,128)} %dynamic-slice_bitcast_fusion.1.in_keep, bf16[128,1024]{1,0:T(8,128)(2,1)} %copy-done.22, bf16[128,1024]{1,0:T(8,128)(2,1)} %copy-done.23, ...), custom_call_target="tpu_custom_call" | custom-call | tf_op jit(solution)/shard_map/finish_kernel/pallas_call | solution.py:858
  393.8 4.7 %bitcast_convert_fusion = f32[2048,1024]{1,0:T(8,128)} fusion(bf16[2,8,128,1024]{3,2,1,0:T(8,128)(2,1)S(1)} %copy-done.9), kind=kLoop, calls=%fused_computation.18 | loop fusion | flops 2097152 | bytes 12582912 | tf_op jit(solution)/shard_map/convert_element_type | solution.py:1085
  401.8 5.3 %maximum_convert_fusion = f32[1024,2048]{1,0:T(8,128)} fusion(bf16[1024,1024]{1,0:T(8,128)(2,1)S(1)} %bitcast.95, bf16[1024,1024]{1,0:T(8,128)(2,1)S(1)} %bitcast.94), kind=kLoop, calls=%fused_computation.17 | loop fusion | flops 8388608 | bytes 12582912 | tf_op jit(solution)/shard_map/convert_element_type | solution.py:1087
  408.3 2.5 fusion.17
  (175 shorter events, 66.5 us)
Async XLA Ops:
  5.7 12.0 %collective-permute-start.2 = (f32[2,512]{1,0:T(2,128)S(1)}, f32[2,512]{1,0:T(2,128)S(1)}, u32[]{:S(2)}, u32[]{:S(2)}) collective-permute-start(f32[2,512]{1,0:T(2,128)S(1)} %pad_maximum_fusion.11), channel_id=1, source_target_pairs={{0,1},{1,0},{2,3},{3,2},{4,5},{5,4},{6,7},{7,6},{8,9},{9,8},{10,11... | collective-permute-start | bytes 12296 | tf_op jit(solution)/shard_map/ppermute | solution.py:894
  8.7 18.7 %collective-permute-start = (f32[512,128]{1,0:T(8,128)S(1)}, f32[512,128]{1,0:T(8,128)}, u32[]{:S(2)}, u32[]{:S(2)}) collective-permute-start(f32[512,128]{1,0:T(8,128)S(1)} %pad_maximum_fusion.7), channel_id=1, source_target_pairs={{0,1},{1,0},{2,3},{3,2},{4,5},{5,4},{6,7},{7,6},{8,9},{9,8},{10,11... | collective-permute-start | bytes 786440 | tf_op jit(solution)/shard_map/ppermute | solution.py:894
  11.7 15.7 %collective-permute-start.1 = (bf16[256,512]{1,0:T(8,128)(2,1)}, bf16[256,512]{1,0:T(8,128)(2,1)}, u32[]{:S(2)}, u32[]{:S(2)}) collective-permute-start(bf16[256,512]{1,0:T(8,128)(2,1)} %fusion.21), channel_id=1, source_target_pairs={{0,1},{1,0},{2,3},{3,2},{4,5},{5,4},{6,7},{7,6},{8,9},{9,8},{10,11... | collective-permute-start | bytes 786440 | tf_op jit(solution)/shard_map/ppermute | solution.py:894
  15.8 27.8 %collective-permute-start.3 = (bf16[256,1024]{1,0:T(8,128)(2,1)}, bf16[256,1024]{1,0:T(8,128)(2,1)S(1)}, u32[]{:S(2)}, u32[]{:S(2)}) collective-permute-start(bf16[256,1024]{1,0:T(8,128)(2,1)} %dynamic_slice.104), channel_id=1, source_target_pairs={{0,1},{1,0},{2,3},{3,2},{4,5},{5,4},{6,7},{7,6},{8,9},{9,8},{10,11... | collective-permute-start | bytes 1572872 | tf_op jit(solution)/shard_map/ppermute | solution.py:894
  27.4 26.4 %collective-permute-start.4 = (bf16[1024,256]{1,0:T(8,128)(2,1)}, bf16[1024,256]{1,0:T(8,128)(2,1)S(1)}, u32[]{:S(2)}, u32[]{:S(2)}) collective-permute-start(bf16[1024,256]{1,0:T(8,128)(2,1)} %make_kernel.2.k0), channel_id=1, source_target_pairs={{0,2},{2,0},{1,3},{3,1},{4,6},{6,4},{5,7},{7,5},{8,10},{10,8},{9,1... | collective-permute-start | bytes 1572872 | tf_op jit(solution)/shard_map/ppermute | solution.py:890
  30.2 17.7 %collective-permute-start.8 = (bf16[256,512]{1,0:T(8,128)(2,1)}, bf16[256,512]{1,0:T(8,128)(2,1)}, u32[]{:S(2)}, u32[]{:S(2)}) collective-permute-start(bf16[256,512]{1,0:T(8,128)(2,1)} %collective-permute-done.1), channel_id=1, source_target_pairs={{0,12},{4,8},{8,4},{12,0},{16,28},{20,24},{24,20},{28,16},{1,13},{... | collective-permute-start | bytes 786440 | tf_op jit(solution)/shard_map/ppermute | solution.py:899
  43.7 35.2 %copy-start.17 = (bf16[256,1024]{1,0:T(8,128)(2,1)}, bf16[256,1024]{1,0:T(8,128)(2,1)S(1)}, u32[]{:S(2)}) copy-start(bf16[256,1024]{1,0:T(8,128)(2,1)S(1)} %collective-permute-done.3) | copy-start | bytes 1572868
  43.7 10.3 %collective-permute-start.5 = (bf16[1024,256]{1,0:T(8,128)(2,1)}, bf16[1024,256]{1,0:T(8,128)(2,1)S(1)}, u32[]{:S(2)}, u32[]{:S(2)}) collective-permute-start(bf16[1024,256]{1,0:T(8,128)(2,1)} %make_kernel.3.k2), channel_id=1, source_target_pairs={{0,2},{2,0},{1,3},{3,1},{4,6},{6,4},{5,7},{7,5},{8,10},{10,8},{9,1... | collective-permute-start | bytes 1572872 | tf_op jit(solution)/shard_map/ppermute | solution.py:890
  43.9 9.4 %collective-permute-start.7 = (bf16[256,512]{1,0:T(8,128)(2,1)}, bf16[256,512]{1,0:T(8,128)(2,1)}, u32[]{:S(2)}, u32[]{:S(2)}) collective-permute-start(bf16[256,512]{1,0:T(8,128)(2,1)} %collective-permute-done.1), channel_id=1, source_target_pairs={{0,8},{4,12},{8,0},{12,4},{16,24},{20,28},{24,16},{28,20},{1,9},{5... | collective-permute-start | bytes 786440 | tf_op jit(solution)/shard_map/ppermute | solution.py:899
  46.4 34.5 %collective-permute-start.12 = (bf16[256,1024]{1,0:T(8,128)(2,1)}, bf16[256,1024]{1,0:T(8,128)(2,1)}, u32[]{:S(2)}, u32[]{:S(2)}) collective-permute-start(bf16[256,1024]{1,0:T(8,128)(2,1)} %constant_dynamic-slice_fusion.4), channel_id=1, source_target_pairs={{0,1},{1,0},{2,3},{3,2},{4,5},{5,4},{6,7},{7,6},{8,9},{9,8},{10,11... | collective-permute-start | bytes 1572872 | tf_op jit(solution)/shard_map/ppermute | solution.py:894
  47.9 32.9 %collective-permute-start.11 = (bf16[256,1024]{1,0:T(8,128)(2,1)S(1)}, bf16[256,1024]{1,0:T(8,128)(2,1)S(1)}, u32[]{:S(2)}, u32[]{:S(2)}) collective-permute-start(bf16[256,1024]{1,0:T(8,128)(2,1)S(1)} %collective-permute-done.3), channel_id=1, source_target_pairs={{0,12},{4,8},{8,4},{12,0},{16,28},{20,24},{24,20},{28,16},{1,13},{... | collective-permute-start | bytes 1572872 | tf_op jit(solution)/shard_map/ppermute | solution.py:899
  53.4 27.5 %collective-permute-start.10 = (bf16[256,1024]{1,0:T(8,128)(2,1)S(1)}, bf16[256,1024]{1,0:T(8,128)(2,1)S(1)}, u32[]{:S(2)}, u32[]{:S(2)}) collective-permute-start(bf16[256,1024]{1,0:T(8,128)(2,1)S(1)} %collective-permute-done.3), channel_id=1, source_target_pairs={{0,8},{4,12},{8,0},{12,4},{16,24},{20,28},{24,16},{28,20},{1,9},{5... | collective-permute-start | bytes 1572872 | tf_op jit(solution)/shard_map/ppermute | solution.py:899
  53.8 27.0 %collective-permute-start.9 = (bf16[256,1024]{1,0:T(8,128)(2,1)S(1)}, bf16[256,1024]{1,0:T(8,128)(2,1)S(1)}, u32[]{:S(2)}, u32[]{:S(2)}) collective-permute-start(bf16[256,1024]{1,0:T(8,128)(2,1)S(1)} %collective-permute-done.3), channel_id=1, source_target_pairs={{0,4},{4,0},{8,12},{12,8},{16,20},{20,16},{24,28},{28,24},{1,5},{5... | collective-permute-start | bytes 1572872 | tf_op jit(solution)/shard_map/ppermute | solution.py:899
  54.0 26.8 %collective-permute-start.6 = (bf16[256,512]{1,0:T(8,128)(2,1)}, bf16[256,512]{1,0:T(8,128)(2,1)}, u32[]{:S(2)}, u32[]{:S(2)}) collective-permute-start(bf16[256,512]{1,0:T(8,128)(2,1)} %collective-permute-done.1), channel_id=1, source_target_pairs={{0,4},{4,0},{8,12},{12,8},{16,20},{20,16},{24,28},{28,24},{1,5},{5... | collective-permute-start | bytes 786440 | tf_op jit(solution)/shard_map/ppermute | solution.py:899
  82.3 5.3 %collective-permute-start.13 = (bf16[1024,512]{1,0:T(8,128)(2,1)S(1)}, bf16[1024,512]{1,0:T(8,128)(2,1)}, u32[]{:S(2)}, u32[]{:S(2)}) collective-permute-start(bf16[1024,512]{1,0:T(8,128)(2,1)S(1)} %pad_maximum_fusion.4), channel_id=1, source_target_pairs={{0,2},{2,0},{1,3},{3,1},{4,6},{6,4},{5,7},{7,5},{8,10},{10,8},{9,1... | collective-permute-start | bytes 3145736 | tf_op jit(solution)/shard_map/ppermute | solution.py:890
  83.6 21.8 %collective-permute-start.16 = (bf16[256,1024]{1,0:T(8,128)(2,1)}, bf16[256,1024]{1,0:T(8,128)(2,1)S(1)}, u32[]{:S(2)}, u32[]{:S(2)}) collective-permute-start(bf16[256,1024]{1,0:T(8,128)(2,1)} %collective-permute-done.12), channel_id=1, source_target_pairs={{0,12},{4,8},{8,4},{12,0},{16,28},{20,24},{24,20},{28,16},{1,13},{... | collective-permute-start | bytes 1572872 | tf_op jit(solution)/shard_map/ppermute | solution.py:899
  84.9 25.3 %collective-permute-start.15 = (bf16[256,1024]{1,0:T(8,128)(2,1)}, bf16[256,1024]{1,0:T(8,128)(2,1)S(1)}, u32[]{:S(2)}, u32[]{:S(2)}) collective-permute-start(bf16[256,1024]{1,0:T(8,128)(2,1)} %collective-permute-done.12), channel_id=1, source_target_pairs={{0,8},{4,12},{8,0},{12,4},{16,24},{20,28},{24,16},{28,20},{1,9},{5... | collective-permute-start | bytes 1572872 | tf_op jit(solution)/shard_map/ppermute | solution.py:899
  86.5 23.8 %collective-permute-start.14 = (bf16[256,1024]{1,0:T(8,128)(2,1)}, bf16[256,1024]{1,0:T(8,128)(2,1)S(1)}, u32[]{:S(2)}, u32[]{:S(2)}) collective-permute-start(bf16[256,1024]{1,0:T(8,128)(2,1)} %collective-permute-done.12), channel_id=1, source_target_pairs={{0,4},{4,0},{8,12},{12,8},{16,20},{20,16},{24,28},{28,24},{1,5},{5... | collective-permute-start | bytes 1572872 | tf_op jit(solution)/shard_map/ppermute | solution.py:899
  87.4 29.7 %collective-permute-start.17 = (bf16[1024,1024]{1,0:T(8,128)(2,1)S(1)}, bf16[1024,1024]{1,0:T(8,128)(2,1)}, u32[]{:S(2)}, u32[]{:S(2)}) collective-permute-start(bf16[1024,1024]{1,0:T(8,128)(2,1)S(1)} %pad_maximum_fusion.2.ib), channel_id=1, source_target_pairs={{0,2},{2,0},{1,3},{3,1},{4,6},{6,4},{5,7},{7,5},{8,10},{10,8},{9,1... | collective-permute-start | bytes 6291464 | tf_op jit(solution)/shard_map/ppermute | solution.py:890
  113.0 4.5 %collective-permute-start.18 = (bf16[1024,1024]{1,0:T(8,128)(2,1)}, bf16[1024,1024]{1,0:T(8,128)(2,1)}, u32[]{:S(2)}, u32[]{:S(2)}) collective-permute-start(bf16[1024,1024]{1,0:T(8,128)(2,1)} %pad_maximum_fusion.3.ob), channel_id=1, source_target_pairs={{0,2},{2,0},{1,3},{3,1},{4,6},{6,4},{5,7},{7,5},{8,10},{10,8},{9,1... | collective-permute-start | bytes 6291464 | tf_op jit(solution)/shard_map/ppermute | solution.py:890
  160.0 47.9 %collective-permute-start.19 = (bf16[1024,1024]{1,0:T(8,128)(2,1)}, bf16[1024,1024]{1,0:T(8,128)(2,1)S(1)}, u32[]{:S(2)}, u32[]{:S(2)}) collective-permute-start(bf16[1024,1024]{1,0:T(8,128)(2,1)} %get-tuple-element.155), channel_id=1, source_target_pairs={{0,1},{1,0},{2,3},{3,2},{4,5},{5,4},{6,7},{7,6},{8,9},{9,8},{10,11... | collective-permute-start | bytes 6291464 | tf_op jit(solution)/shard_map/ppermute | solution.py:894
  161.6 41.6 %collective-permute-start.20 = (bf16[1,2,2,128,1024]{4,3,2,1,0:T(8,128)(2,1)}, bf16[1,2,2,128,1024]{4,3,2,1,0:T(8,128)(2,1)}, u32[]{:S(2)}, u32[]{:S(2)}) collective-permute-start(bf16[1,2,2,128,1024]{4,3,2,1,0:T(8,128)(2,1)} %get-tuple-element.156), channel_id=1, source_target_pairs={{0,4},{4,0},{8,12},{12,8},{16,20},{20,16},{24,28},{28,24},{1,5},{5... | collective-permute-start | bytes 3145736 | tf_op jit(solution)/shard_map/ppermute | solution.py:899
  220.6 26.9 %collective-permute-start.21 = (bf16[2,2,1,128,1024]{4,3,1,2,0:T(8,128)(2,1)}, bf16[2,2,1,128,1024]{4,3,1,2,0:T(8,128)(2,1)S(1)}, u32[]{:S(2)}, u32[]{:S(2)}) collective-permute-start(bf16[2,2,1,128,1024]{4,3,1,2,0:T(8,128)(2,1)} %bitcast_convert_fusion.1), channel_id=1, source_target_pairs={{0,8},{4,12},{8,0},{12,4},{16,24},{20,28},{24,16},{28,20},{1,9},{5... | collective-permute-start | bytes 3145736 | tf_op jit(solution)/shard_map/ppermute | solution.py:899
  221.0 26.5 %collective-permute-start.22 = (bf16[1,2,2,128,1024]{4,3,2,1,0:T(8,128)(2,1)}, bf16[1,2,2,128,1024]{4,3,2,1,0:T(8,128)(2,1)}, u32[]{:S(2)}, u32[]{:S(2)}) collective-permute-start(bf16[1,2,2,128,1024]{4,3,2,1,0:T(8,128)(2,1)} %add_convert_fusion), channel_id=1, source_target_pairs={{0,1},{1,0},{2,3},{3,2},{4,5},{5,4},{6,7},{7,6},{8,9},{9,8},{10,11... | collective-permute-start | bytes 3145736 | tf_op jit(solution)/shard_map/ppermute | solution.py:894
  222.6 25.0 %collective-permute-start.23 = (bf16[1,2,2,128,1024]{4,3,2,1,0:T(8,128)(2,1)}, bf16[1,2,2,128,1024]{4,3,2,1,0:T(8,128)(2,1)}, u32[]{:S(2)}, u32[]{:S(2)}) collective-permute-start(bf16[1,2,2,128,1024]{4,3,2,1,0:T(8,128)(2,1)} %dynamic-slice_convert_fusion), channel_id=1, source_target_pairs={{0,4},{4,0},{8,12},{12,8},{16,20},{20,16},{24,28},{28,24},{1,5},{5... | collective-permute-start | bytes 3145736 | tf_op jit(solution)/shard_map/ppermute | solution.py:899
  224.0 23.5 %copy-start.5 = (f32[2,2,1,128,1024]{4,3,1,2,0:T(8,128)S(1)}, f32[2,2,1,128,1024]{4,3,1,2,0:T(8,128)}, u32[]{:S(2)}) copy-start(f32[2,2,1,128,1024]{4,3,1,2,0:T(8,128)} %dynamic-slice_bitcast_fusion) | copy-start | bytes 6291460
  252.6 34.6 %collective-permute-start.24 = (bf16[1024,512]{1,0:T(8,128)(2,1)}, bf16[1024,512]{1,0:T(8,128)(2,1)S(1)}, u32[]{:S(2)}, u32[]{:S(2)}) collective-permute-start(bf16[1024,512]{1,0:T(8,128)(2,1)} %get-tuple-element.192), channel_id=1, source_target_pairs={{0,1},{1,0},{2,3},{3,2},{4,5},{5,4},{6,7},{7,6},{8,9},{9,8},{10,11... | collective-permute-start | bytes 3145736 | tf_op jit(solution)/shard_map/ppermute | solution.py:894
  255.4 31.8 %collective-permute-start.26 = (bf16[128,1024]{1,0:T(8,128)(2,1)S(1)}, bf16[128,1024]{1,0:T(8,128)(2,1)S(1)}, u32[]{:S(2)}, u32[]{:S(2)}) collective-permute-start(bf16[128,1024]{1,0:T(8,128)(2,1)S(1)} %get-tuple-element.194), channel_id=1, source_target_pairs={{0,8},{4,12},{8,0},{12,4},{16,24},{20,28},{24,16},{28,20},{1,9},{5... | collective-permute-start | bytes 786440 | tf_op jit(solution)/shard_map/ppermute | solution.py:899
  257.0 30.2 %collective-permute-start.27 = (bf16[128,1024]{1,0:T(8,128)(2,1)S(1)}, bf16[128,1024]{1,0:T(8,128)(2,1)S(1)}, u32[]{:S(2)}, u32[]{:S(2)}) collective-permute-start(bf16[128,1024]{1,0:T(8,128)(2,1)S(1)} %get-tuple-element.195), channel_id=1, source_target_pairs={{0,16},{4,20},{8,24},{12,28},{16,0},{20,4},{24,8},{28,12},{1,17},{... | collective-permute-start | bytes 786440 | tf_op jit(solution)/shard_map/ppermute | solution.py:899
  259.6 27.6 %collective-permute-start.28 = (bf16[128,1024]{1,0:T(8,128)(2,1)S(1)}, bf16[128,1024]{1,0:T(8,128)(2,1)S(1)}, u32[]{:S(2)}, u32[]{:S(2)}) collective-permute-start(bf16[128,1024]{1,0:T(8,128)(2,1)S(1)} %get-tuple-element.196), channel_id=1, source_target_pairs={{0,24},{4,28},{8,16},{12,20},{16,8},{20,12},{24,0},{28,4},{1,25},{... | collective-permute-start | bytes 786440 | tf_op jit(solution)/shard_map/ppermute | solution.py:899
  259.8 27.4 %collective-permute-start.25 = (bf16[1,2,1,128,1024]{4,3,1,2,0:T(8,128)(2,1)S(1)}, bf16[1,2,1,128,1024]{4,3,1,2,0:T(8,128)(2,1)S(1)}, u32[]{:S(2)}, u32[]{:S(2)}) collective-permute-start(bf16[1,2,1,128,1024]{4,3,1,2,0:T(8,128)(2,1)S(1)} %dynamic-slice_convert_fusion.1), channel_id=1, source_target_pairs={{0,4},{4,0},{8,12},{12,8},{16,20},{20,16},{24,28},{28,24},{1,5},{5... | collective-permute-start | bytes 1572872 | tf_op jit(solution)/shard_map/ppermute | solution.py:899
  263.5 24.7 %copy-start.1 = (bf16[1,1024,1024]{2,1,0:T(8,128)(2,1)S(1)}, bf16[1,1024,1024]{2,1,0:T(8,128)(2,1)}, u32[]{:S(2)}) copy-start(bf16[1,1024,1024]{2,1,0:T(8,128)(2,1)} %param.19) | copy-start | bytes 6291460
  (29 other events, 157.7 us)

commit v4 on v3

v4 whole, which is shorter than its diff:
```python
import functools

import ml_dtypes
import numpy as np

import jax
import jax.numpy as jnp
from jax import lax
from jax.experimental import pallas as pl
from jax.experimental.pallas import tpu as pltpu
from jax.sharding import PartitionSpec as P

VMEM_LIMIT = 60 * 1024 * 1024
F32, BF16 = jnp.float32, jnp.bfloat16
LANES = 128
MESH = pl.DeviceIdType.MESH
KERNEL_INNER = 64
MOMENT_INNER = 32
CB = 256
DFT_ROWS = 512
TOKEN_ROWS = 256
FFN_TILE = 512
GELU_A = 0.7978845608028654
GELU_B = 0.044715
norm_eps = 1e-05


def params_of(**extra):
    return pltpu.CompilerParams(vmem_limit_bytes=VMEM_LIMIT, **extra)


class CoreExchange:
    def __init__(self, pairs, send, recv):
        self.pairs, self.send, self.recv = pairs, send, recv
        self.other = {"core": 1 - lax.axis_index("core")}

    def greet(self):
        pl.semaphore_signal(
            pltpu.get_barrier_semaphore(), inc=1, device_id=self.other, device_id_type=MESH
        )

    def meet(self):
        pl.semaphore_wait(pltpu.get_barrier_semaphore(), 1)

    def copies(self, slot):
        return [
            pltpu.make_async_remote_copy(
                src_ref=mine.at[slot], dst_ref=theirs.at[slot],
                send_sem=self.send.at[i, slot], recv_sem=self.recv.at[i, slot],
                device_id=self.other, device_id_type=MESH,
            )
            for i, (mine, theirs) in enumerate(self.pairs)
        ]

    def start(self, slot):
        for copy in self.copies(slot):
            copy.start()

    def arrived(self, slot):
        for copy in self.copies(slot):
            copy.wait_recv()

    def sent(self, slots):
        for slot in range(slots):
            for copy in self.copies(slot):
                copy.wait_send()


class Posts:
    def __init__(self, bits, send, recv):
        self.bits, self.send, self.recv, self.used = bits, send, recv, 0
        self.place = lax.axis_index("pair")
        self.started = []

    def bit(self, b):
        return lax.rem(lax.div(self.place, 1 << b), 2)

    def device(self, link):
        if isinstance(link, str):
            return {link: 1 - lax.axis_index(link)}
        return {"pair": self.place + (1 - 2 * self.bit(link)) * (1 << link)}

    def block(self, flipped):
        at = 0
        for b in range(self.bits):
            here = 1 - self.bit(b) if flipped >> b & 1 else self.bit(b)
            at = at + here * (1 << (self.bits - 1 if b == 0 else b - 1))
        return at

    def slot(self):
        self.used += 1
        return self.used - 1

    def copy(self, src, dst, slot, link):
        return pltpu.make_async_remote_copy(
            src_ref=src, dst_ref=dst, send_sem=self.send.at[slot], recv_sem=self.recv.at[slot],
            device_id=self.device(link), device_id_type=MESH,
        )

    def post(self, src, dst, slot, link):
        copy = self.copy(src, dst, slot, link)
        copy.start()
        self.started.append(copy)

    def await_(self, dst, slot, link):
        self.copy(dst, dst, slot, link).wait_recv()

    def greet(self, links):
        for link in links:
            pl.semaphore_signal(
                pltpu.get_barrier_semaphore(), inc=1, device_id=self.device(link),
                device_id_type=MESH,
            )

    def meet(self, count):
        pl.semaphore_wait(pltpu.get_barrier_semaphore(), count)

    def finish(self):
        for copy in self.started:
            copy.wait_send()


def exchange_sems(pairs, slots):
    return [pltpu.SemaphoreType.DMA((pairs, slots))] * 2


def transform_table(length):
    f = np.arange(length, dtype=np.int64)[:, None]
    t = np.arange(length, dtype=np.int64)[None, :]
    turn = ((4 * f + 1) * t) % (4 * length)
    angle = turn * (2.0 * np.pi / (4 * length))
    return np.concatenate([np.cos(angle), -np.sin(angle)], axis=0)


def cmul(a, b):
    return a[0] * b[0] - a[1] * b[1], a[0] * b[1] + a[1] * b[0]


def log2_of(count):
    bits = count.bit_length() - 1
    assert 1 << bits == count
    return bits


def fill_powers(base, count, out_r, out_i, tmp, scale=None):
    bits = log2_of(count)
    p = base
    for i in range(bits):
        tmp[2 * i] = p[0]
        tmp[2 * i + 1] = p[1]
        p = cmul(p, p)
    if scale is not None:
        tmp[2 * bits] = scale[0]
        tmp[2 * bits + 1] = scale[1]
    row = lax.broadcasted_iota(jnp.int32, (8, LANES), 0)

    def mode(n, carry):
        def at(i):
            return tuple(
                jnp.broadcast_to(tmp[2 * i + j, pl.ds(n, 1), :], (8, LANES)) for j in range(2)
            )

        if scale is None:
            p = (jnp.ones((8, LANES), F32), jnp.zeros((8, LANES), F32))
        else:
            p = at(bits)
        for bit in range(3):
            q = cmul(p, at(bit))
            on = (row & (1 << bit)) != 0
            p = (jnp.where(on, q[0], p[0]), jnp.where(on, q[1], p[1]))
        parts = [p]
        for bit in range(3, bits):
            w = at(bit)
            parts += [cmul(x, w) for x in parts]
        for j, part in enumerate(parts):
            out_r[n, 8 * j : 8 * j + 8, :] = part[0]
            out_i[n, 8 * j : 8 * j + 8, :] = part[1]
        return carry

    lax.fori_loop(0, base[0].shape[0], mode, 0)
    return p


def split_params(packed_ref, log_dt_ref):
    rows = packed_ref[...]
    modes = rows.shape[0] // 4
    log_a, freq, c_real, c_imag = (rows[i * modes : (i + 1) * modes] for i in range(4))
    step = jnp.exp(log_dt_ref[...])
    rate = jnp.exp(log_a)
    decay = jnp.exp(-(step * rate))
    turn = step * freq
    return step, rate, freq, c_real, c_imag, (decay * jnp.cos(turn), decay * jnp.sin(turn))


def kernel_block(packed_ref, log_dt_ref, k_ref, zr, zi, wr, wi, tmp):
    step, _, _, c_real, c_imag, z = split_params(packed_ref, log_dt_ref)
    inner = KERNEL_INNER
    outer = k_ref.shape[0] // inner
    modes = c_real.shape[0]
    z_inner = fill_powers(z, inner, zr, zi, tmp)
    fill_powers(z_inner, outer, wr, wi, tmp, (2.0 * step * c_real, 2.0 * step * c_imag))
    group = 2

    def rows(i, carry):
        d = i * group
        acc = [jnp.zeros((inner, LANES), F32) for _ in range(group)]
        for n in range(modes):
            a, b = zr[n], zi[n]
            for u in range(group):
                acc[u] = acc[u] + (
                    wr[n, pl.ds(d + u, 1), :] * a - wi[n, pl.ds(d + u, 1), :] * b
                )
        for u in range(group):
            at = pl.ds(pl.multiple_of((d + u) * inner, inner), inner)
            k_ref[at, :] = acc[u].astype(BF16)
        return carry

    lax.fori_loop(0, outer // group, rows, 0)


def power_scratch(modes, inner, outer):
    return (
        [pltpu.VMEM((modes, inner, LANES), F32)] * 2
        + [pltpu.VMEM((modes, outer, LANES), F32)] * 2
        + [pltpu.VMEM((20, modes, LANES), F32)]
    )


def moments_block(packed_ref, log_dt_ref, g_ref, out_ref, zr, zi, wr, wi, tmp, sums):
    step, rate, freq, c_real, c_imag, z = split_params(packed_ref, log_dt_ref)
    inner, outer = zr.shape[1], wr.shape[1]
    z_inner = fill_powers(z, inner, zr, zi, tmp)
    fill_powers(z_inner, outer, wr, wi, tmp)
    modes = c_real.shape[0]
    pos = lax.broadcasted_iota(jnp.int32, (inner, LANES), 0).astype(F32)

    def mode(n, carry):
        zero = jnp.zeros((inner, LANES), F32)
        sr, si, tr, ti = zero, zero, zero, zero
        for d in reversed(range(outer)):
            v = g_ref[d * inner : (d + 1) * inner, :]
            sr = sr + v * wr[n, d : d + 1, :]
            si = si + v * wi[n, d : d + 1, :]
            if d > 0:
                tr = tr + sr
                ti = ti + si
        zn = (zr[n], zi[n])
        first = cmul(zn, (sr, si))
        second = cmul(zn, (pos * sr + float(inner) * tr, pos * si + float(inner) * ti))
        for j, v in enumerate(first + second):
            sums[j, pl.ds(n, 1), :] = jnp.sum(v, axis=0, keepdims=True)
        return carry

    lax.fori_loop(0, modes, mode, 0)
    scale = 2.0 * step
    real_grad, imag_grad = scale * sums[0], -scale * sums[1]
    slope_r = scale * (c_real * sums[2] - c_imag * sums[3])
    slope_i = scale * (c_real * sums[3] + c_imag * sums[2])
    log_a_grad = -step * rate * slope_r
    freq_grad = -step * slope_i
    log_dt_grad = jnp.sum(
        c_real * real_grad + c_imag * imag_grad + log_a_grad + freq * freq_grad,
        axis=0, keepdims=True,
    )
    for i, part in enumerate((log_a_grad, freq_grad, real_grad, imag_grad)):
        out_ref[i * modes : (i + 1) * modes, :] = part
    top = 4 * modes
    row = lax.broadcasted_iota(jnp.int32, (8, LANES), 0)
    out_ref[top : top + 8, :] = jnp.where(row == 0, log_dt_grad, 0.0)


def gelu_both(v):
    sq = v * v
    th = jnp.tanh(v * (GELU_A + (GELU_A * GELU_B) * sq))
    rise = 0.5 + 0.5 * th
    slope = rise + v * (0.5 - 0.5 * th * th) * (GELU_A + (3.0 * GELU_A * GELU_B) * sq)
    return v * rise, slope


def gelu(v):
    return gelu_both(v)[0]


def gelu_slope(v):
    return gelu_both(v)[1]


def dot(a, b):
    return jnp.dot(a, b, preferred_element_type=F32)


def conv_block(x, k, skip, fwd_ref, inv_ref, mixed_ref, act_ref, xs_ref, ks_ref, ys):
    n = x.shape[0]
    for i in range(n // DFT_ROWS):
        re = pl.ds(i * DFT_ROWS, DFT_ROWS)
        im = pl.ds(n + i * DFT_ROWS, DFT_ROWS)
        xr, xi = dot(fwd_ref[re, :], x), dot(fwd_ref[im, :], x)
        kr, ki = dot(fwd_ref[re, :], k), dot(fwd_ref[im, :], k)
        xs_ref[re, :] = xr.astype(BF16)
        xs_ref[im, :] = xi.astype(BF16)
        ks_ref[re, :] = kr.astype(BF16)
        ks_ref[im, :] = ki.astype(BF16)
        ys[re, :] = (xr * kr - xi * ki).astype(BF16)
        ys[im, :] = (xr * ki + xi * kr).astype(BF16)
    y = ys[...]
    for i in range(n // TOKEN_ROWS):
        at = pl.ds(i * TOKEN_ROWS, TOKEN_ROWS)
        mixed = dot(inv_ref[at, :], y) + skip * x[i * TOKEN_ROWS : (i + 1) * TOKEN_ROWS].astype(F32)
        mixed_ref[at, :] = mixed
        act_ref[at, :] = gelu(mixed).astype(BF16)


def front_body(
    inputs, cot, counts, gains, log_dt, skip, log_a, freq, c_real, c_imag, fwd_hbm, inv_hbm,
    w_value, w_gate, w_in, w_out,
    packed_ref, vec_ref, skip_ref, grad_ref, x_out, mixed_out, act_out, xs_out, ks_out,
    value_direct, value_via, gate_direct, gate_via, in_direct, in_via, out_direct, out_via,
    zr, zi, wr, wi, tmp, fwd, inv, packed, vec, got_vec, nx, k, mixed, act, xs, ks, ys,
    local, send, recv, *, bits
):
    posts = Posts(bits, send, recv)
    core, side = lax.axis_index("core"), lax.axis_index("tensor")
    half = packed.shape[2]
    modes = log_a.shape[0]
    posts.greet([0, 1, "core", "tensor"])
    tables = [
        pltpu.make_async_copy(src, dst, local.at[i])
        for i, (src, dst) in enumerate(((fwd_hbm, fwd), (inv_hbm, inv)))
    ]
    for copy in tables:
        copy.start()
    mine = pl.ds(pl.multiple_of(core * half, half), half)
    for i, ref in enumerate((log_a, freq, c_real, c_imag)):
        packed[1, i * modes : (i + 1) * modes, :] = ref[:, mine]
    vec[0:1, :] = log_dt[...]
    vec[1:2, :] = skip[...]
    posts.meet(4)

    def exchange(src, dst, link):
        slot = posts.slot()
        posts.post(src, dst, slot, link)
        return lambda: posts.await_(dst, slot, link)

    params_come = [
        exchange(packed.at[1], packed.at[0], "tensor"), exchange(vec, got_vec, "tensor")
    ]
    rows = value_direct.shape[0] // 4
    place = 2 * posts.bit(1) + posts.bit(0)

    def quarter(at, part=None):
        first, count = (0, rows) if part is None else (part * (rows // 2), rows // 2)
        return pl.ds(pl.multiple_of(at * rows + first, rows // 2), count)

    def cols(count):
        return pl.ds(pl.multiple_of(core * count, count), count)

    near, up, across = (place + 1 - 2 * posts.bit(0)), (place + 2 - 4 * posts.bit(1)), 3 - place
    out_row = pl.multiple_of(core * (4 * rows) + place * rows, rows)
    sources = [
        [(w_value.at[quarter(place), cols(half)], value_direct, value_via),
         (w_gate.at[quarter(place), cols(half)], gate_direct, gate_via)],
        [(w_in.at[quarter(place), cols(in_direct.shape[1])], in_direct, in_via)],
        [(w_out.at[pl.ds(out_row, rows), :], out_direct, out_via)],
    ]

    def fetch_steps(items):
        slots = []
        for src, direct, via in items:
            took = [posts.slot() for _ in range(9)]
            slots.append(took)
            posts.post(src, direct.at[quarter(place)], took[0], "tensor")
        yield
        for (src, direct, via), took in zip(items, slots):
            own = direct.at[quarter(place)]
            posts.await_(own, took[0], "tensor")
            posts.post(own, own, took[1], 0)
            posts.post(own, own, took[2], 1)
            posts.post(own, via.at[quarter(place)], took[5], "core")
        yield
        for (src, direct, via), took in zip(items, slots):
            for link, at, slot, on, over, piece in (
                (0, near, 1, 3, 1, 0), (1, up, 2, 4, 0, 1)
            ):
                come = direct.at[quarter(at)]
                posts.await_(come, took[slot], link)
                passed = direct.at[quarter(at, piece)]
                posts.post(passed, passed, took[on], over)
                posts.post(come, via.at[quarter(at)], took[5 + slot], "core")
        yield
        for (src, direct, via), took in zip(items, slots):
            for slot, link, piece in ((3, 1, 0), (4, 0, 1)):
                posts.await_(direct.at[quarter(across, piece)], took[slot], link)
            come = direct.at[quarter(across)]
            posts.post(come, via.at[quarter(across)], took[8], "core")
        yield
        for (src, direct, via), took in zip(items, slots):
            for at, slot in ((place, 5), (near, 6), (up, 7), (across, 8)):
                posts.await_(via.at[quarter(at)], took[slot], "core")

    flows = [fetch_steps(items) for items in sources]
    for flow in flows:
        next(flow)

    def kernel_of(j, log_dt):
        for i in range(half // LANES):
            at = pl.ds(i * LANES, LANES)
            kernel_block(packed.at[1 - j, :, at], log_dt.at[:, at], k.at[2 * j, :, at], zr, zi, wr, wi, tmp)

    vec_ref[1] = vec[0:1, mine]
    kernel_of(0, vec_ref.at[1])
    kernels_come = [exchange(k.at[0], k.at[1], "core")]
    for come in params_come:
        come()
    vec_ref[0] = got_vec[0:1, mine]
    next(flows[0])
    kernel_of(1, vec_ref.at[0])
    kernels_come.append(exchange(k.at[2], k.at[3], "core"))
    next(flows[1])
    for i in range(nx.shape[0] // TOKEN_ROWS):
        at = pl.ds(i * TOKEN_ROWS, TOKEN_ROWS)
        source = inputs[at, :].astype(F32)
        nx[at, :] = norm_forward(source, gains[0:1, :], gains[1:2, :])[0].astype(BF16)
    used = (side < counts[0]).astype(F32)
    grad_ref[...] = (used * cot[...].astype(F32)).astype(BF16)
    width = vec.shape[1]
    for ref, at in ((vec, side), (got_vec, 1 - side)):
        skip_ref[:, pl.ds(pl.multiple_of(at * width, width), width)] = ref[1:2, :]
    stores = [
        pltpu.make_async_copy(nx, x_out, local.at[2]),
        pltpu.make_async_copy(packed, packed_ref, local.at[3]),
    ]
    for copy in stores:
        copy.start()
    for copy in tables:
        copy.wait()
    next(flows[0])
    plan = ((0, flows[2]), (2, flows[1]), (1, flows[0]), (3, flows[2]))
    for n, (j, flow) in enumerate(plan):
        there = lax.rem(side + j // 2, 2)
        which = lax.rem(core + j % 2, 2)
        at = pl.ds(pl.multiple_of((2 * there + which) * half, half), half)
        if j % 2:
            kernels_come[j // 2]()
        params = vec if j < 2 else got_vec
        skip = params[1:2, pl.ds(pl.multiple_of(which * half, half), half)]
        conv_block(
            nx[:, at], k[j], skip, fwd, inv, mixed.at[j], act.at[j], xs.at[j], ks.at[j], ys
        )
        for i, (src, dst) in enumerate(
            ((mixed.at[j], mixed_out.at[j]), (act.at[j], act_out.at[:, at]),
             (xs.at[j], xs_out.at[j]), (ks.at[j], ks_out.at[j]))
        ):
            copy = pltpu.make_async_copy(src, dst, local.at[4 + 4 * j + i])
            copy.start()
            stores.append(copy)
        next(flow)
    for flow in (flows[0], flows[1], flows[1], flows[2], flows[2]):
        next(flow, None)
    for copy in stores:
        copy.wait()
    posts.finish()


def front_kernel(
    inputs, cot, counts, gains, log_dt, skip, log_a, freq, c_real, c_imag, fwd, inv,
    w_value, w_gate, w_in, w_out,
):
    bits = log2_of(lax.axis_size("pair"))
    n, d = inputs.shape
    modes = log_a.shape[0]
    half = d // 4
    units = w_in.shape[1] // 2
    vmem = pl.BlockSpec(memory_space=pltpu.VMEM)
    hbm = pl.BlockSpec(memory_space=pl.ANY)
    shape = jax.ShapeDtypeStruct
    return pl.pallas_call(
        functools.partial(front_body, bits=bits),
        in_specs=[vmem] * 2 + [pl.BlockSpec(memory_space=pltpu.SMEM)] + [vmem] * 7 + [hbm] * 6,
        out_specs=[hbm, vmem, vmem, vmem] + [hbm] * 13,
        out_shape=[
            shape((2, 4 * modes, half), F32), shape((2, 1, half), F32), shape((1, d), F32),
            shape((n, d), BF16), shape((n, d), BF16), shape((4, n, half), F32), shape((n, d), BF16),
            shape((4, 2 * n, half), BF16), shape((4, 2 * n, half), BF16),
        ]
        + [shape((d, half), BF16)] * 4
        + [shape((d, units), BF16)] * 2
        + [shape((units, d), BF16)] * 2,
        scratch_shapes=power_scratch(modes, KERNEL_INNER, n // KERNEL_INNER)
        + [
            pltpu.VMEM(fwd.shape, BF16), pltpu.VMEM(inv.shape, BF16),
            pltpu.VMEM((2, 4 * modes, half), F32),
            pltpu.VMEM((2, d // 2), F32), pltpu.VMEM((2, d // 2), F32),
            pltpu.VMEM((n, d), BF16), pltpu.VMEM((4, n, half), BF16),
            pltpu.VMEM((4, n, half), F32), pltpu.VMEM((4, n, half), BF16),
            pltpu.VMEM((4, 2 * n, half), BF16), pltpu.VMEM((4, 2 * n, half), BF16),
            pltpu.VMEM((2 * n, half), BF16),
            pltpu.SemaphoreType.DMA((20,)),
            pltpu.SemaphoreType.DMA((40,)), pltpu.SemaphoreType.DMA((40,)),
        ],
        compiler_params=params_of(collective_id=5, has_side_effects=True),
        name="front_kernel",
    )(
        inputs, cot, counts, gains, log_dt, skip, log_a, freq, c_real, c_imag, fwd, inv,
        w_value, w_gate, w_in, w_out,
    )


def conv_back_block(ga, mixed, x, xs, ks, skip, fwd, inv, gm, gy, ax, ak, put_gn, put_gk):
    n = x.shape[0]
    total = jnp.zeros((1, x.shape[1]), F32)
    for i in range(n // TOKEN_ROWS):
        at = pl.ds(i * TOKEN_ROWS, TOKEN_ROWS)
        v = ga[at, :] * gelu_slope(mixed[at, :])
        gm[at, :] = v
        gy[at, :] = v.astype(BF16)
        total += jnp.sum(v * x[at, :].astype(F32), axis=0, keepdims=True)
    g = gy[...]
    for i in range(n // DFT_ROWS):
        re = pl.ds(i * DFT_ROWS, DFT_ROWS)
        im = pl.ds(n + i * DFT_ROWS, DFT_ROWS)
        gr, gi = dot(fwd[re, :], g), dot(fwd[im, :], g)
        for src, dst in ((ks, ax), (xs, ak)):
            a, b = src[re, :].astype(F32), src[im, :].astype(F32)
            dst[re, :] = (a * gr + b * gi).astype(BF16)
            dst[im, :] = (a * gi - b * gr).astype(BF16)
    yx = ax[...]
    yk = ak[...]
    for i in range(n // TOKEN_ROWS):
        at = pl.ds(i * TOKEN_ROWS, TOKEN_ROWS)
        put_gk(at, dot(inv[at, :], yk))
        put_gn(at, dot(inv[at, :], yx) + skip * gm[at, :])
    return total


def project_all(left, own, direct, via, out):
    core, side = lax.axis_index("core"), lax.axis_index("tensor")
    width = direct.shape[1]
    far = (1 - side) * 2 * width
    for ref, first, count in (
        (own, side * 2 * width, 2 * width), (direct, far + core * width, width),
        (via, far + (1 - core) * width, width),
    ):
        out[:, pl.ds(pl.multiple_of(first, width), count)] = dot(left, ref[...])


def glu_body(
    act, source, value_own, value_direct, value_via, gate_own, gate_direct, gate_via, gains,
    value_ref, sig_ref, residual_ref, n2_ref, n2t_ref, values, gates,
):
    project_all(act[...], value_own, value_direct, value_via, values)
    project_all(act[...], gate_own, gate_direct, gate_via, gates)
    value = values[...]
    sig = 1.0 / (1.0 + jnp.exp(-gates[...]))
    value_ref[...] = value.astype(BF16)
    sig_ref[...] = sig.astype(BF16)
    residual = source[...].astype(F32) + (value * sig).astype(BF16).astype(F32)
    residual_ref[...] = residual
    n2 = norm_forward(residual, gains[2:3, :], gains[3:4, :])[0].astype(BF16)
    n2_ref[...] = n2
    n2t_ref[...] = n2.T


def glu_kernel(act, source, weights, gains):
    n, d = act.shape
    rows = pl.BlockSpec((TOKEN_ROWS, d), lambda i: (i, 0))

    def whole(a):
        return pl.BlockSpec(a.shape, lambda i: (0, 0), pipeline_mode=pl.Buffered(1))

    return pl.pallas_call(
        glu_body,
        grid=(n // TOKEN_ROWS,),
        in_specs=[rows, rows] + [whole(w) for w in weights] + [whole(gains)],
        out_specs=[rows] * 4 + [pl.BlockSpec((d, TOKEN_ROWS), lambda i: (0, i))],
        out_shape=[
            jax.ShapeDtypeStruct((n, d), BF16), jax.ShapeDtypeStruct((n, d), BF16),
            jax.ShapeDtypeStruct((n, d), F32), jax.ShapeDtypeStruct((n, d), BF16),
            jax.ShapeDtypeStruct((d, n), BF16),
        ],
        scratch_shapes=[pltpu.VMEM((TOKEN_ROWS, d), F32)] * 2,
        compiler_params=params_of(),
        name="glu_kernel",
    )(act, source, *weights, gains)


def glu_back_body(
    g_far, g_own, residual, cot, value, sig, act, value_own, value_direct, value_via,
    gate_own, gate_direct, gate_via, gains,
    there_keep, there_come, in_box, here_out, out_come,
    resid_ref, ga_ref, gain_ref, bias_ref, there_ref, here_ref, in_x, in_y, out_z,
    gv, gt, mine, theirs, in_a, in_b, out_a, out_b, out_box, local, send, recv, *, bits
):
    step = pl.program_id(0)
    posts = Posts(bits, send, recv)
    links = [0, 1, "core", "tensor"]
    slots = {name: posts.slot() for name in ("x", "y", "z")}
    swap = [posts.slot(), posts.slot()]

    def transfers():
        return [
            posts.copy(in_box, in_x, slots["x"], 0),
            posts.copy(in_a, in_y, slots["y"], "tensor"),
            posts.copy(out_box, out_z, slots["z"], 1),
        ]

    @pl.when(step == 0)
    def _():
        posts.greet(links)
        other = 1 - posts.bit(1)
        loads = [
            pltpu.make_async_copy(src, dst, local.at[i])
            for i, (src, dst) in enumerate((
                (there_keep, in_a), (there_come, in_b),
                (here_out.at[:, other], out_a), (out_come.at[:, other], out_b),
            ))
        ]
        for copy in loads:
            copy.start()
        posts.meet(len(links))
        sends = transfers()
        sends[0].start()
        for copy in loads[:2]:
            copy.wait()
        in_a[...] = (in_a[...].astype(F32) + in_b[...].astype(F32)).astype(BF16)
        sends[1].start()
        for copy in loads[2:]:
            copy.wait()
        out_box[...] = (out_a[...] + out_b[...].astype(F32)).astype(BF16)
        sends[2].start()

    chunks = act.shape[0] // TOKEN_ROWS
    width = gv.shape[2]

    @pl.when(step < chunks)
    def _():
        standard, inv_std = norm_forward(residual[...], 1.0, 0.0)[1:]
        part, gain_grad, bias_grad = norm_backward(
            g_far[...] + g_own[...], standard, inv_std, gains[2:3, :]
        )
        new = step == 0
        gain_ref[...] = jnp.where(new, 0.0, gain_ref[...]) + gain_grad[None]
        bias_ref[...] = jnp.where(new, 0.0, bias_ref[...]) + bias_grad[None]
        resid = cot[...].astype(F32) + part
        resid_ref[...] = resid
        grad = resid.astype(BF16).astype(F32)
        gate = sig[...].astype(F32)
        grad_value = (grad * gate).astype(BF16)
        grad_gate = (grad * value[...].astype(F32) * gate * (1.0 - gate)).astype(BF16)
        at = pl.ds(pl.multiple_of(step * TOKEN_ROWS, TOKEN_ROWS), TOKEN_ROWS)
        for i in range(gv.shape[0]):
            gv[i, at, :] = grad_value[:, i * width : (i + 1) * width]
            gt[i, at, :] = grad_gate[:, i * width : (i + 1) * width]
        core, side = lax.axis_index("core"), lax.axis_index("tensor")
        far = 2 * (1 - side)
        total = 0.0
        for grads, own, direct, via in (
            (gv, value_own, value_direct, value_via), (gt, gate_own, gate_direct, gate_via)
        ):
            ours = jnp.concatenate([grads[2 * side, at, :], grads[2 * side + 1, at, :]], axis=1)
            total += contract_cols(ours, own[...])
            total += contract_cols(grads[far + core, at, :], direct[...])
            total += contract_cols(grads[far + 1 - core, at, :], via[...])
        ga_ref[...] = total

    @pl.when(step >= chunks)
    def _():
        j = step - chunks
        side = lax.rem(lax.axis_index("tensor") + 1 + j, 2)
        half = lax.rem(lax.axis_index("core") + 1 + j // 2, 2)
        block = 2 * side + half
        grads = [contract_rows(act[...], gv[block]), contract_rows(act[...], gt[block])]
        for slot in range(2):
            @pl.when(j == slot)
            def _():
                for i, g in enumerate(grads):
                    mine[slot, :, i * width : (i + 1) * width] = g.astype(BF16)
                posts.copy(mine.at[slot], theirs.at[slot], swap[slot], "core").start()

        @pl.when(j == 2)
        def _():
            posts.await_(theirs.at[0], swap[0], "core")
            for i, g in enumerate(grads):
                at = pl.ds(i * width, width)
                there_ref[:, at] = (g + theirs[0, :, at].astype(F32)).astype(BF16)

        @pl.when(j == 3)
        def _():
            posts.await_(theirs.at[1], swap[1], "core")
            for i, g in enumerate(grads):
                at = pl.ds(i * width, width)
                here_ref[:, at] = g + theirs[1, :, at].astype(F32)
            for slot in range(2):
                posts.copy(mine.at[slot], theirs.at[slot], swap[slot], "core").wait_send()
            for copy in transfers():
                copy.wait()


def glu_back_kernel(
    g_far, g_own, residual, cot, value, sig, act, weights, gains,
    there_keep, there_come, in_box, here_out, out_come,
):
    bits = log2_of(lax.axis_size("pair"))
    n, d = act.shape
    chunks = n // TOKEN_ROWS
    width = d // 4
    hbm = pl.BlockSpec(memory_space=pl.ANY)
    extra = (there_keep, there_come, in_box, here_out, out_come)
    split = (here_out.shape[0],) + here_out.shape[2:]

    def whole(a):
        return pl.BlockSpec(a.shape, lambda i: (0, 0), pipeline_mode=pl.Buffered(1))

    rows = pl.BlockSpec((TOKEN_ROWS, d), lambda i: (jnp.minimum(i, chunks - 1), 0))
    vector = pl.BlockSpec((1, d), lambda i: (0, 0))
    weight = pl.BlockSpec((d, 2 * width), lambda i: (0, 0))
    return pl.pallas_call(
        functools.partial(glu_back_body, bits=bits),
        grid=(chunks + 4,),
        in_specs=[rows] * 6 + [whole(act)] + [whole(w) for w in weights] + [whole(gains)] + [hbm] * 5,
        out_specs=[rows, rows, vector, vector, weight, weight] + [hbm] * 3,
        scratch_shapes=[pltpu.VMEM((4, n, width), BF16)] * 2
        + [pltpu.VMEM((2, d, 2 * width), BF16)] * 2
        + [pltpu.VMEM(there_keep.shape, BF16)] * 2
        + [pltpu.VMEM(split, F32), pltpu.VMEM(split, BF16), pltpu.VMEM(split, BF16)]
        + [pltpu.SemaphoreType.DMA((4,))]
        + [pltpu.SemaphoreType.DMA((5,))] * 2,
        out_shape=[
            jax.ShapeDtypeStruct((n, d), F32), jax.ShapeDtypeStruct((n, d), F32),
            jax.ShapeDtypeStruct((1, d), F32), jax.ShapeDtypeStruct((1, d), F32),
            jax.ShapeDtypeStruct((d, 2 * width), BF16), jax.ShapeDtypeStruct((d, 2 * width), F32),
            jax.ShapeDtypeStruct(in_box.shape, BF16), jax.ShapeDtypeStruct(in_box.shape, BF16),
            jax.ShapeDtypeStruct(split, BF16),
        ],
        compiler_params=params_of(collective_id=2, has_side_effects=True),
        name="glu_back_kernel",
    )(g_far, g_own, residual, cot, value, sig, act, *weights, gains, *extra)


def ffn_body(
    n2, n2t, gl, ia, ib, oa, ob, ffn, gn2, box_ref, keep_ref, out_ref,
    wi, wo, h, gp, total, in_mine, out_mine, in_theirs, out_theirs, send, recv,
):
    step, half = pl.program_id(0), in_mine.shape[0]
    first = step < half
    cores = CoreExchange([(in_mine, in_theirs), (out_mine, out_theirs)], send, recv)
    pl.when(step == 0)(cores.greet)

    @pl.when(first)
    def _():
        wi[...] = ia[...]
        wo[...] = oa[...]

    @pl.when(jnp.logical_not(first))
    def _():
        wi[...] = ib[...]
        wo[...] = ob[...]

    @pl.when(step == 0)
    def _():
        ffn[...] = jnp.zeros_like(ffn)
        gn2[...] = jnp.zeros_like(gn2)

    w1, w2 = wi[...], wo[...]
    for r in range(n2.shape[0] // TOKEN_ROWS):
        at = pl.ds(r * TOKEN_ROWS, TOKEN_ROWS)
        act, slope = gelu_both(dot(n2[at, :], w1))
        hidden = act.astype(BF16)
        grad_pre = (contract_cols(gl[at, :], w2) * slope).astype(BF16)
        h[at, :] = hidden
        gp[at, :] = grad_pre
        ffn[at, :] += dot(hidden, w2)
        gn2[at, :] += contract_cols(grad_pre, w1)
    out_grad = contract_rows(h[...], gl[...])
    in_grad = dot(n2t[...], gp[...])

    pl.when(step == 0)(cores.meet)

    @pl.when(first)
    def _():
        in_mine[step] = in_grad.astype(BF16)
        out_mine[step] = out_grad.astype(BF16)
        cores.start(step)

    @pl.when(jnp.logical_not(first))
    def _():
        cores.arrived(step - half)
        total[...] = in_grad + in_theirs[step - half].astype(F32)
        near, rows = lax.rem(lax.axis_index("pair"), 2), keep_ref.shape[0]
        for ref, at in ((keep_ref, near), (box_ref, 1 - near)):
            part = pl.ds(pl.multiple_of(at * rows, rows), rows)
            ref[...] = total[part, :].astype(ref.dtype)
        out_ref[...] = (out_grad + out_theirs[step - half].astype(F32)).astype(out_ref.dtype)

    @pl.when(step == 2 * half - 1)
    def _():
        cores.sent(half)


def ffn_kernel(n2, n2t, gl, ins, outs, units, own):
    n, d = n2.shape
    half = units // FFN_TILE

    def whole(a):
        return pl.BlockSpec(a.shape, lambda s: (0, 0), pipeline_mode=pl.Buffered(1))

    def fst(s):
        at = jnp.minimum(s, half - 1)
        return at + (1 - lax.axis_index("core")) * half if own else at

    def snd(s):
        at = jnp.maximum(s - half, 0)
        return at + lax.axis_index("core") * half if own else at

    total = pl.BlockSpec((n, d), lambda s: (0, 0))
    dtype = F32 if own else BF16
    return pl.pallas_call(
        ffn_body,
        grid=(2 * half,),
        in_specs=[
            whole(n2), whole(n2t), whole(gl),
            pl.BlockSpec((d, FFN_TILE), lambda s: (0, fst(s))),
            pl.BlockSpec((d, FFN_TILE), lambda s: (0, snd(s))),
            pl.BlockSpec((FFN_TILE, d), lambda s: (fst(s), 0)),
            pl.BlockSpec((FFN_TILE, d), lambda s: (snd(s), 0)),
        ],
        out_specs=[
            total, total,
            pl.BlockSpec((d // 2, FFN_TILE), lambda s: (0, jnp.maximum(s - half, 0))),
            pl.BlockSpec((d // 2, FFN_TILE), lambda s: (0, jnp.maximum(s - half, 0))),
            pl.BlockSpec((FFN_TILE, d), lambda s: (jnp.maximum(s - half, 0), 0)),
        ],
        scratch_shapes=[
            pltpu.VMEM((d, FFN_TILE), BF16), pltpu.VMEM((FFN_TILE, d), BF16),
            pltpu.VMEM((n, FFN_TILE), BF16), pltpu.VMEM((n, FFN_TILE), BF16),
            pltpu.VMEM((d, FFN_TILE), F32),
        ]
        + [pltpu.VMEM((half, d, FFN_TILE), BF16), pltpu.VMEM((half, FFN_TILE, d), BF16)] * 2
        + exchange_sems(2, half),
        out_shape=[
            jax.ShapeDtypeStruct((n, d), F32), jax.ShapeDtypeStruct((n, d), F32),
            jax.ShapeDtypeStruct((d // 2, units), BF16), jax.ShapeDtypeStruct((d // 2, units), dtype),
            jax.ShapeDtypeStruct((units, d), dtype),
        ],
        compiler_params=params_of(collective_id=int(own), has_side_effects=True),
        name="ffn_kernel",
    )(n2, n2t, gl, *ins, *outs)


def norm_forward(values, norm_gain, norm_bias):
    center = values - jnp.mean(values, axis=-1, keepdims=True)
    inv_std = lax.rsqrt(jnp.mean(center * center, axis=-1, keepdims=True) + norm_eps)
    standard = center * inv_std
    return (standard * norm_gain + norm_bias, standard, inv_std)


def norm_backward(incoming, standard, inv_std, norm_gain):
    scaled = incoming * norm_gain
    value_grad = inv_std * (
        scaled
        - jnp.mean(scaled, axis=-1, keepdims=True)
        - standard * jnp.mean(scaled * standard, axis=-1, keepdims=True)
    )
    return (value_grad, jnp.sum(incoming * standard, axis=0), jnp.sum(incoming, axis=0))


def contract_rows(left, right):
    return lax.dot_general(left, right, (((0,), (0,)), ((), ())), preferred_element_type=F32)


def contract_cols(left, right):
    return lax.dot_general(left, right, (((1,), (1,)), ((), ())), preferred_element_type=F32)


def scatter_steps(posts, acc, bits, order, boxes, come):
    def at(known, flipped):
        place = 0
        for i, b in enumerate(bits):
            here = posts.bit(b)
            if b in known:
                bit = 1 - here if known[b] else here
            else:
                bit = flipped >> i & 1
            place = place + bit * (1 << i)
        return place

    done = {}
    used = 0
    for n, b in enumerate(order):
        rest = [bits.index(i) for i in order[n + 1 :]]
        combos = [sum((c >> k & 1) << i for k, i in enumerate(rest)) for c in range(1 << len(rest))]
        slots = []
        for c, combo in enumerate(combos):
            slot = posts.slot()
            boxes[used + c] = acc[at({**done, b: True}, combo)].astype(BF16)
            posts.post(boxes.at[used + c], come.at[used + c], slot, b)
            slots.append(slot)
        yield
        done[b] = False
        for c, combo in enumerate(combos):
            posts.await_(come.at[used + c], slots[c], b)
            keep = at(done, combo)
            acc[keep] = acc[keep] + come[used + c].astype(F32)
        used += len(combos)
    posts.result = at(done, 0)


def gather_steps(posts, own, whole, local, order):
    core = lax.axis_index("core")
    count = 1 << posts.bits
    slots = {(rel, link): posts.slot() for rel in range(count) for link in ("bit", "core")}
    first = pltpu.make_async_copy(own, whole.at[core, posts.block(0)], local)
    first.start()

    def pass_on(src, rel, bits):
        dst = whole.at[core, posts.block(rel)]
        for b in bits:
            posts.post(src, dst, slots[rel ^ (1 << b), "bit"], b)
        posts.post(src, dst, slots[rel, "core"], "core")

    pass_on(own, 0, order)
    for n, b in enumerate(order):
        for c in range(1 << n):
            yield
            rel = sum((c >> k & 1) << order[k] for k in range(n)) | 1 << b
            block = whole.at[core, posts.block(rel)]
            posts.await_(block, slots[rel, "bit"], b)
            pass_on(block, rel, order[n + 1 :])
    yield
    first.wait()
    for rel in range(count):
        posts.await_(whole.at[1 - core, posts.block(rel)], slots[rel, "core"], "core")


def back_body(
    ga_hbm, mixed_hbm, x_hbm, xs_hbm, ks_hbm, fwd_hbm, inv_hbm, source_hbm, resid_hbm,
    in_keep, in_x, in_y, out_keep, out_come, out_z, glu_keep, glu_box,
    skip, gains, gain2, bias2, packed, log_dt,
    input_ref, in_all, out_all, glu_all, small_all,
    ga, fwd, inv, mixed, x, xs, ks, gm, gy, ax, ak, gk, gk_mine, gk_theirs, source, resid, staged,
    zr, zi, wr, wi, tmp, sums, moments, rows, rows_mine, rows_other, rows_come,
    in_acc, in_a, in_b, out_acc, out_a, out_b, glu_acc, glu_come, in_own, out_own, glu_own,
    in_boxes, in_got, out_boxes, out_got, glu_boxes, glu_got, small, small_far, small_got,
    local, send, recv, *, bits
):
    posts = Posts(bits, send, recv)
    links = list(range(bits)) + ["core", "tensor"]
    posts.greet(links)
    core, side = lax.axis_index("core"), lax.axis_index("tensor")
    n, width = mixed.shape[1:]
    used = [3]

    def load(src, dst):
        copy = pltpu.make_async_copy(src, dst, local.at[used[0]])
        used[0] += 1
        copy.start()
        return copy

    def columns(i):
        there = lax.rem(side + 1 + i, 2)
        which = lax.rem(core + 1 + i // 2, 2)
        return pl.ds(pl.multiple_of((2 * there + which) * width, width), width)

    def load_block(i):
        j, slot = 2 * ((i + 1) % 2) + 1 - i // 2, i % 2
        return [
            load(mixed_hbm.at[j], mixed.at[slot]), load(x_hbm.at[:, columns(i)], x.at[slot]),
            load(xs_hbm.at[j], xs.at[slot]), load(ks_hbm.at[j], ks.at[slot]),
        ]

    mine = posts.bit(1)
    in_loads = [load(in_keep, in_acc), load(in_x, in_a), load(in_y, in_b)]
    out_loads = [
        load(out_keep.at[:, mine], out_acc), load(out_come.at[:, mine], out_a), load(out_z, out_b)
    ]
    ga_load = load(ga_hbm, ga)
    block_loads = load_block(0)
    tables = [load(fwd_hbm, fwd), load(inv_hbm, inv)]
    glu_load = load(glu_keep, glu_acc)
    posts.meet(len(links))
    near, far = list(range(1, bits)), list(range(2, bits))

    def in_steps():
        for copy in in_loads:
            copy.wait()
        in_acc[...] = in_acc[...] + in_a[...].astype(F32) + in_b[...].astype(F32)
        yield from scatter_steps(posts, in_acc, near, near, in_boxes, in_got)
        in_own[...] = in_acc[posts.result].astype(BF16)
        yield from gather_steps(posts, in_own, in_all, local.at[0], list(reversed(range(bits))))

    def out_steps():
        for copy in out_loads:
            copy.wait()
        out_acc[...] = out_acc[...] + out_a[...].astype(F32) + out_b[...].astype(F32)
        yield from scatter_steps(posts, out_acc, far + [0], [0] + far, out_boxes, out_got)
        out_own[...] = out_acc[posts.result].astype(BF16)
        yield from gather_steps(posts, out_own, out_all, local.at[1], list(reversed(range(bits))))

    def glu_steps():
        slot = posts.slot()
        posts.post(glu_box, glu_come, slot, "tensor")
        yield
        posts.await_(glu_come, slot, "tensor")
        glu_load.wait()
        glu_acc[...] = glu_acc[...] + glu_come[...].astype(F32)
        yield from scatter_steps(posts, glu_acc, near + [0], [0] + near, glu_boxes, glu_got)
        glu_own[...] = glu_acc[posts.result].astype(BF16)
        yield from gather_steps(posts, glu_own, glu_all, local.at[2], GLU_ORDER(bits))

    def small_steps():
        for j in range(2):
            for half, ref in ((core, rows_mine), (1 - core, rows_other)):
                there = lax.rem(side + 1 + j, 2)
                at = pl.multiple_of((2 * there + half) * width, width)
                ref[j] = rows[:, pl.ds(at, width)]
        slot = posts.slot()
        posts.post(rows_other, rows_come, slot, "core")
        yield
        posts.await_(rows_come, slot, "core")
        top = moments.shape[1]
        for j, ref in ((0, small_far), (1, small)):
            ref[:top, :] = moments[j]
            ref[top:, :] = rows_mine[j] + rows_come[j]
        slot = posts.slot()
        posts.post(small_far, small_got.at[0], slot, "tensor")
        yield
        posts.await_(small_got.at[0], slot, "tensor")
        small[...] = small[...] + small_got[0]
        for b in range(bits):
            slot = posts.slot()
            small_all[b] = small[...]
            posts.post(small_all.at[b], small_got.at[1 + b], slot, b)
            yield
            posts.await_(small_got.at[1 + b], slot, b)
            small[...] = small[...] + small_got[1 + b]
        slot = posts.slot()
        small_all[bits] = small[...]
        posts.post(small_all.at[bits], small_got.at[1 + bits], slot, "core")
        yield
        posts.await_(small_got.at[1 + bits], slot, "core")
        small_all[bits + 1] = small_got[1 + bits]

    flows = {"in": in_steps(), "out": out_steps(), "glu": glu_steps()}
    done = object()

    def advance(*names):
        for name in names:
            if name in flows and next(flows[name], done) is done:
                del flows[name]

    advance("glu", "in", "out")
    rows[...] = jnp.zeros_like(rows)
    rows[3:4, :] = gain2[...]
    rows[4:5, :] = bias2[...]
    ga_load.wait()
    slots = [posts.slot(), posts.slot()]
    for i in range(4):
        slot = i % 2
        for copy in block_loads:
            copy.wait()
        if i < 3:
            block_loads = load_block(i + 1)
        if i == 0:
            for copy in tables:
                copy.wait()
        at = columns(i)

        def put_gn(tokens, value, at=at):
            ga[tokens, at] = value

        def put_gk(tokens, value, i=i):
            if i < 2:
                gk_mine[i, tokens, :] = value.astype(BF16)
            else:
                gk[i - 2, tokens, :] = value

        rows[0:1, at] = conv_back_block(
            ga.at[:, at], mixed.at[slot], x.at[slot], xs.at[slot], ks.at[slot], skip[:, at],
            fwd, inv, gm, gy, ax, ak, put_gn, put_gk,
        )
        if i < 2:
            posts.post(gk_mine.at[i], gk_theirs.at[i], slots[i], "core")
        else:
            posts.await_(gk_theirs.at[i - 2], slots[i - 2], "core")
            gk[i - 2] = gk[i - 2] + gk_theirs[i - 2].astype(F32)
        if i in BACK_ROUNDS:
            advance(*BACK_ROUNDS[i])

    chunks = n // TOKEN_ROWS

    def load_rows(r):
        at = pl.ds(r * TOKEN_ROWS, TOKEN_ROWS)
        return [load(source_hbm.at[at], source.at[r % 2]), load(resid_hbm.at[at], resid.at[r % 2])]

    row_loads = load_rows(0)
    stores = []
    for r in range(chunks):
        for copy in row_loads:
            copy.wait()
        if r + 1 < chunks:
            row_loads = load_rows(r + 1)
        at = pl.ds(r * TOKEN_ROWS, TOKEN_ROWS)
        standard, inv_std = norm_forward(source[r % 2].astype(F32), 1.0, 0.0)[1:]
        part, gain_grad, bias_grad = norm_backward(ga[at, :], standard, inv_std, gains[0:1, :])
        rows[1:2, :] = rows[1:2, :] + gain_grad[None]
        rows[2:3, :] = rows[2:3, :] + bias_grad[None]
        staged[r] = (resid[r % 2] + part).astype(BF16)
        stores.append(load(staged.at[r], input_ref.at[at]))
    advance(*BACK_ROUNDS["norm"])

    def block(j, i):
        at = pl.ds(i * LANES, LANES)
        moments_block(
            packed.at[j, :, at], log_dt.at[j, :, at], gk.at[j, :, at], moments.at[j, :, at],
            zr, zi, wr, wi, tmp, sums,
        )

    for j in range(2):
        for i in range(width // LANES):
            block(j, i)
            advance("in", "out", "glu")
    flows["small"] = small_steps()
    while flows:
        advance("small", "in", "out", "glu")
    for copy in stores:
        copy.wait()
    posts.finish()


def back_kernel(
    ga, mixed, x, xs, ks, fwd, inv, source, resid, in_keep, in_x, in_y, out_keep, out_come, out_z,
    glu_keep, glu_box, skip, gains, gain2, bias2, packed, log_dt,
):
    bits = log2_of(lax.axis_size("pair"))
    blocks = 1 << bits
    width, modes = packed.shape[2], packed.shape[1] // 4
    n, d = ga.shape
    block_rows, cols = glu_keep.shape[1:]
    kept = in_keep.shape[0]
    small_rows = 4 * modes + 8 + 8
    vmem = pl.BlockSpec(memory_space=pltpu.VMEM)
    hbm = pl.BlockSpec(memory_space=pl.ANY)
    big = pltpu.VMEM((block_rows, d), BF16)
    small = pltpu.VMEM((small_rows, width), F32)
    rows = pltpu.VMEM((2, 8, width), F32)
    copies = 3 * 2 * blocks + 2 * kept + blocks + bits + 12
    shape = jax.ShapeDtypeStruct
    return pl.pallas_call(
        functools.partial(back_body, bits=bits),
        in_specs=[hbm] * 17 + [vmem] * 6,
        out_specs=[hbm] * 4 + [vmem],
        out_shape=[
            shape((n, d), BF16), shape((2, blocks, block_rows, d), BF16),
            shape((2, blocks, block_rows, d), BF16), shape((2, blocks, block_rows, cols), BF16),
            shape((bits + 2, small_rows, width), F32),
        ],
        scratch_shapes=[
            pltpu.VMEM((n, d), F32), pltpu.VMEM(fwd.shape, BF16), pltpu.VMEM(inv.shape, BF16),
            pltpu.VMEM((2, n, width), F32), pltpu.VMEM((2, n, width), BF16),
            pltpu.VMEM((2, 2 * n, width), BF16), pltpu.VMEM((2, 2 * n, width), BF16),
            pltpu.VMEM((n, width), F32), pltpu.VMEM((n, width), BF16),
            pltpu.VMEM((2 * n, width), BF16), pltpu.VMEM((2 * n, width), BF16),
            pltpu.VMEM((2, n, width), F32), pltpu.VMEM((2, n, width), BF16),
            pltpu.VMEM((2, n, width), BF16),
            pltpu.VMEM((2, TOKEN_ROWS, d), BF16), pltpu.VMEM((2, TOKEN_ROWS, d), F32),
            pltpu.VMEM((n // TOKEN_ROWS, TOKEN_ROWS, d), BF16),
        ]
        + power_scratch(modes, MOMENT_INNER, n // MOMENT_INNER)
        + [
            pltpu.VMEM((4, modes, LANES), F32), pltpu.VMEM((2, 4 * modes + 8, width), F32),
            pltpu.VMEM((8, d), F32), rows, rows, rows,
            pltpu.VMEM(in_keep.shape, F32), pltpu.VMEM(in_keep.shape, BF16),
            pltpu.VMEM(in_keep.shape, BF16),
            pltpu.VMEM(in_keep.shape, F32), pltpu.VMEM(in_keep.shape, BF16),
            pltpu.VMEM(in_keep.shape, BF16),
            pltpu.VMEM(glu_keep.shape, F32), pltpu.VMEM(glu_keep.shape, BF16),
            big, big, pltpu.VMEM((block_rows, cols), BF16),
        ]
        + [pltpu.VMEM((kept - 1, block_rows, d), BF16)] * 4
        + [pltpu.VMEM((blocks - 1, block_rows, cols), BF16)] * 2
        + [small, small, pltpu.VMEM((bits + 2, small_rows, width), F32)]
        + [pltpu.SemaphoreType.DMA((48,))]
        + [pltpu.SemaphoreType.DMA((copies,))] * 2,
        compiler_params=params_of(collective_id=4, has_side_effects=True),
        name="back_kernel",
    )(
        ga, mixed, x, xs, ks, fwd, inv, source, resid, in_keep, in_x, in_y, out_keep, out_come, out_z,
        glu_keep, glu_box, skip, gains, gain2, bias2, packed, log_dt,
    )


def GLU_ORDER(bits):
    return list(reversed(range(bits)))


BACK_ROUNDS = {1: ("in", "out"), 3: ("glu", "in"), "norm": ("out", "in", "glu")}


SWAP = ((0, 1), (1, 0))


def over_core(values):
    return lax.ppermute(values, "core", SWAP)


def over_tensor(values):
    return lax.ppermute(values, "tensor", SWAP)


def over_pair(values, flip):
    size = lax.axis_size("pair")
    return lax.ppermute(values, "pair", [(p, p ^ flip) for p in range(size)])


def place_in(group):
    first, count = group
    return (lax.axis_index("pair") // (1 << first)) % (1 << count)


def flips_of(group):
    first, count = group
    return [j << first for j in range(1, 1 << count)]


def pair_bits():
    return log2_of(lax.axis_size("pair"))


def by_bits(values):
    bits = pair_bits()
    return values.reshape(*[2] * bits, values.shape[0] >> bits, values.shape[1])


def split_over(total, bit):
    axis = 0 if bit == 0 else pair_bits() - bit
    return part(total, place_in((bit, 1)), axis), part(total, 1 - place_in((bit, 1)), axis).astype(BF16)


def gathered(keep, come, group, axis):
    me = place_in(group)
    parts = [keep] + come
    bit = 1
    while bit < len(parts):
        swapped = (me & bit) != 0
        parts = [jnp.where(swapped, parts[k ^ bit], parts[k]) for k in range(len(parts))]
        bit *= 2
    return jnp.concatenate(parts, axis=axis)


def ordered(index, mine, other, axis):
    first = jnp.where(index == 0, mine, other)
    second = jnp.where(index == 0, other, mine)
    return jnp.concatenate([first, second], axis=axis)


def part(values, index, axis):
    half = values.shape[axis] // 2
    return lax.dynamic_slice_in_dim(values, index * half, half, axis)


def together(*values):
    return lax.optimization_barrier(values)


def shards(
    inputs, counts, ln1_gain, ln1_bias, log_dt, log_a, freq, c_real, c_imag, skip_gain,
    w_value, w_gate, ln2_gain, ln2_bias, w_in, w_out, cotangent,
):
    _, length, width = inputs.shape
    core, side = lax.axis_index("core"), lax.axis_index("tensor")
    source = inputs.reshape(length, width)
    gains = jnp.stack([ln1_gain, ln1_bias, ln2_gain, ln2_bias]).astype(F32)
    table = transform_table(length)
    fwd = jnp.asarray(table.astype(ml_dtypes.bfloat16))
    inv = jnp.asarray(np.ascontiguousarray((table.T / length).astype(ml_dtypes.bfloat16)))
    (
        packed, log_dts, skip, grad_low, normed1, mixed, act, spectrum, kernel_spectrum,
        value_direct, value_via, gate_direct, gate_via, in_direct, in_via, out_direct, out_via,
    ) = front_kernel(
        source, cotangent.reshape(length, width), counts, gains, log_dt[None], skip_gain[None],
        log_a.T, freq.T, c_real.T, c_imag.T, fwd, inv, w_value, w_gate, w_in, w_out,
    )
    glu_weights = (w_value, value_direct, value_via, w_gate, gate_direct, gate_via)
    value_proj, gate_sig, residual, normed2, normed2_t = glu_kernel(act, source, glu_weights, gains)
    units = in_direct.shape[1]
    far_ffn, far_normed2, there_box, there_keep, there_out = ffn_kernel(
        normed2, normed2_t, grad_low, (in_via, in_direct), (out_via, out_direct), units, False
    )
    normed2, there_out, there_box = together(normed2, there_out, there_box)
    out_come, there_come = over_tensor(there_out), over_pair(there_box, 1)
    own_sums = ffn_kernel(normed2, normed2_t, grad_low, (w_in, w_in), (w_out, w_out), units, True)
    own_sums, out_come, there_come = together(own_sums, out_come, there_come)
    own_ffn, own_normed2, in_box, in_keep, here_out = own_sums
    blocks = lax.axis_size("pair")
    split = (blocks // 2, 2, width // blocks, width)
    here_out, out_come = here_out.reshape(split), out_come.reshape(split)
    (
        grad_residual, grad_act, gain_second_grad, bias_second_grad, there_glu, here_glu,
        in_x, in_y, out_z,
    ) = glu_back_kernel(
        far_normed2, own_normed2, residual, grad_low, value_proj, gate_sig, act, glu_weights, gains,
        there_keep, there_come, in_box, here_out, out_come,
    )
    halved = (blocks // 2, width // blocks, width)
    by_block = (blocks, width // blocks, -1)
    input_grad, in_all, out_all, glu_all, small = back_kernel(
        grad_act, mixed, normed1, spectrum, kernel_spectrum, fwd, inv, source, grad_residual,
        in_keep.reshape(halved), in_x.reshape(halved), in_y.reshape(halved),
        here_out, out_come, out_z, here_glu.reshape(by_block), there_glu.reshape(by_block),
        skip, gains, gain_second_grad, bias_second_grad, packed, log_dts,
    )
    used_flag = (side < counts[0]).astype(F32)
    output = (used_flag * (residual + (far_ffn + own_ffn))).astype(BF16).reshape(inputs.shape)
    input_grad = input_grad.reshape(inputs.shape)
    small = ordered(core, small[-2], small[-1], 1)
    out_total = out_all.reshape(-1, width).astype(F32)
    in_all = in_all.reshape(2, width, -1)
    in_total = jnp.concatenate([in_all[0], in_all[1]], axis=1).astype(F32)
    glu_all = glu_all.reshape(2, width, -1)
    cut = glu_all.shape[2] // 2
    value_total = jnp.concatenate([glu_all[0, :, :cut], glu_all[1, :, :cut]], axis=1).astype(F32)
    gate_total = jnp.concatenate([glu_all[0, :, cut:], glu_all[1, :, cut:]], axis=1).astype(F32)

    modes = log_a.shape[1]
    top = 4 * modes
    return (
        output,
        input_grad,
        small[top + 9],
        small[top + 10],
        small[top],
        small[:modes].T,
        small[modes : 2 * modes].T,
        small[2 * modes : 3 * modes].T,
        small[3 * modes : 4 * modes].T,
        small[top + 8],
        value_total,
        gate_total,
        small[top + 11],
        small[top + 12],
        in_total,
        out_total,
    )


def solution(mesh):
    devices = mesh.devices
    cores = jax.sharding.Mesh(
        devices.reshape(devices.shape[0] // 2, 2, devices.shape[1]), ("pair", "core", "tensor")
    )
    batch, every = ("pair", "core"), ("pair", "core", "tensor")
    in_specs = (
        P(every, None, None), P(batch), P(), P(), P("tensor"), P("tensor", None), P("tensor", None),
        P("tensor", None), P("tensor", None), P("tensor"), P(None, "tensor"), P(None, "tensor"),
        P(), P(), P(None, "tensor"), P("tensor", None), P(every, None, None),
    )
    out_specs = (
        P(every, None, None), P(every, None, None), P("tensor"), P("tensor"), P("tensor"),
        P("tensor", None), P("tensor", None), P("tensor", None), P("tensor", None), P("tensor"),
        P(None, "tensor"), P(None, "tensor"), P("tensor"), P("tensor"), P(None, "tensor"),
        P("tensor", None),
    )
    return jax.shard_map(shards, mesh=cores, in_specs=in_specs, out_specs=out_specs, check_vma=False)
```

time: 414 us -> 366 us (0.88)
  Pallas kernels: 272 us -> 323 us
  other arithmetic: 56 us -> 18.5 us
  starting transfers between devices: 30 us -> 2.09 us
  local copies, waits for them, and re-layouts: 34.8 us -> 12.8 us
  waiting for transfers between devices: 16 us -> 5.17 us
    pallas_call x7 -> x4, Pallas kernels: 192 us -> 242 us  [the longest x1 126 us: back_kernel(): pl.pallas_call(functools.partial(back_body, bits=bits), in_specs=[hbm] *...]
    ppermute x16 -> x1, starting transfers between devices: 19.2 us -> 1.51 us  [over_pair(): return lax.ppermute(values, 'pair', [(p, p ^ flip) for p in range(size)])]
    dynamic_slice x11 -> x0, local copies, waits for them, and re-layouts: 15.4 us -> none  [the longest x9 11.3 us: part(): return lax.dynamic_slice_in_dim(values, index * half, half, axis)]
    ppermute x16 -> x1, waiting for transfers between devices: 10.8 us -> 0.01 us  [over_pair(): return lax.ppermute(values, 'pair', [(p, p ^ flip) for p in range(size)])]
    ppermute x8 -> x1, starting transfers between devices: 10.3 us -> 0.58 us  [over_tensor(): return lax.ppermute(values, 'tensor', SWAP)]
    convert_element_type x6 -> x1, other arithmetic: 9.77 us -> 0.63 us  [shards(): gains = jnp.stack([ln1_gain, ln1_bias, ln2_gain, ln2_bias]).astype(F32)]
    reduce_sum x3 -> x0, other arithmetic: 5.31 us -> none  [the longest x1 4.27 us: norm_backward(): jnp.sum(incoming * standard, axis=0)]
    unnamed x68 -> x17, local copies, waits for them, and re-layouts: 9.67 us -> 7.74 us
  transfers between devices with their start and end apart: 29 -> 2, of which waited for: 5 -> 1; matrix products, arithmetic and copies ran while one was open for 8% -> 0% of each run, Pallas kernels for 34% -> 11%
where the time goes in v4:
time: 366 us; the launch traced here: 363 us
  Pallas kernels  323 us (88%)
  other arithmetic  18.5 us (5%)
  local copies, waits for them, and re-layouts  12.8 us (3%)
  waiting for transfers between devices  5.17 us (1%)
    pallas_call x1, Pallas kernels, back_kernel(): pl.pallas_call(functools.partial(back_body, bits=bits), in_specs=[hbm] *...  126 us
    pallas_call x2, Pallas kernels, ffn_kernel(): pl.pallas_call(ffn_body, grid=(2 * half,), in_specs=[whole(n2), whole(n2t...  81.1 us
    pallas_call x1, Pallas kernels, front_kernel(): pl.pallas_call(functools.partial(front_body, bits=bits), in_specs=[vmem]...  69.3 us
    pallas_call x1, Pallas kernels, glu_back_kernel(): pl.pallas_call(functools.partial(glu_back_body, bits=bits), grid=(chunks...  34.5 us
    pallas_call x1, Pallas kernels, glu_kernel(): pl.pallas_call(glu_body, grid=(n // TOKEN_ROWS,), in_specs=[rows, rows] +...  12.5 us
    unnamed x17, local copies, waits for them, and re-layouts  7.74 us
  transfers between devices with their start and end apart: 2, of which 1 were waited for; matrix products, arithmetic and copies ran while one was open for 0% of the time, Pallas kernels for 11%

profile of v4, /device:TPU:0, one launch (start us, length us, event | category | flops | bytes accessed | tf_op | source)
XLA Modules:
  0.0 363.5 jit_solution(2081406396278226545)
XLA Ops:
  1.3 0.7 stack.18
  2.0 0.7 stack.17
  2.7 0.7 stack.16
  3.4 0.7 stack.15
  4.0 0.6 maximum_convert_fusion.3.gains
  4.7 69.3 %front_kernel.1 = (f32[2,128,256]{2,1,0:T(8,128)}, f32[2,1,256]{2,1,0:T(1,128)}, f32[1,1024]{1,0:T(1,128)}, bf16[1024,1024]{1,0:T(8,128)(2,1)}, bf16[1024,1024]{...) custom-call(bf16[1024,1024]{1,0:T(8,128)(2,1)} %bitcast.52, ...), custom_call_target="tpu_custom_call" | custom-call | tf_op jit(solution)/shard_map/front_kernel/pallas_call | solution.py:476
  74.0 12.5 %glu_kernel.1 = (bf16[1024,1024]{1,0:T(8,128)(2,1)}, bf16[1024,1024]{1,0:T(8,128)(2,1)}, f32[1024,1024]{1,0:T(8,128)}, bf16[1024,1024]{1,0:T(8,128)(2,1)}, bf16[1024,1024]{1,0:T(8,128)(2,1)}) custom-call(bf16[1024,1024]{1,0:T(8,128)(2,1)} %get-tuple-element.72.act, bf16[1024,1024]{1,0:T(8,128)(2,1)} %bitcast.53, bf16[1024,512]{1,0:T(8,128)(2,1)} %value_own.3, ...), custom_call_target="tpu_custom_call" | custom-call | tf_op jit(solution)/shard_map/glu_kernel/pallas_call | solution.py:570
  86.5 40.1 %ffn_kernel.2 = (f32[1024,1024]{1,0:T(8,128)}, f32[1024,1024]{1,0:T(8,128)}, bf16[512,1024]{1,0:T(8,128)(2,1)}, bf16[512,1024]{1,0:T(8,128)(2,1)}, bf16[1024,1024]{1,0:T(8,128)(2,1)}) custom-call(bf16[1024,1024]{1,0:T(8,128)(2,1)} %get-tuple-element.88.n2, bf16[1024,1024]{1,0:T(8,128)(2,1)} %get-tuple-element.79.n2t, ...), custom_call_target="tpu_custom_call" | custom-call | tf_op jit(solution)/shard_map/ffn_kernel/pallas_call | solution.py:816
  126.6 0.6 collective-permute-start
  127.2 1.5 collective-permute-start.1
  128.7 41.0 %ffn_kernel.3 = (f32[1024,1024]{1,0:T(8,128)}, f32[1024,1024]{1,0:T(8,128)}, bf16[512,1024]{1,0:T(8,128)(2,1)}, f32[512,1024]{1,0:T(8,128)}, f32[1024,1024]{1,0:T(8,128)}) custom-call(bf16[1024,1024]{1,0:T(8,128)(2,1)} %get-tuple-element.88.n2, bf16[1024,1024]{1,0:T(8,128)(2,1)} %get-tuple-element.79.n2t, bf16[1024,1024]{1,0:T(8,128)(2,1)} %get-tuple-element.80.gl.cot, ...), custom_call_target="tpu_custom_call" | custom-call | tf_op jit(solution)/shard_map/ffn_kernel/pallas_call | solution.py:816
  169.7 0.0 collective-permute-done.1.there_come
  169.7 0.0 copy-start.7
  169.7 5.2 %collective-permute-done = bf16[1024,1024]{1,0:T(8,128)(2,1)S(1)} collective-permute-done((bf16[1024,1024]{1,0:T(8,128)(2,1)}, bf16[1024,1024]{1,0:T(8,128)(2,1)S(1)}, u32[]{:S(2)}, u32[]{:S(2)}) %collective-permute-start) | collective-permute-done | bytes 2097184 | tf_op jit(solution)/shard_map/ppermute | solution.py:1206
  174.9 1.3 copy-done.1
  176.2 34.5 %glu_back_kernel.1 = (f32[1024,1024]{1,0:T(8,128)}, f32[1024,1024]{1,0:T(8,128)}, f32[1,1024]{1,0:T(1,128)}, f32[1,1024]{1,0:T(1,128)}, bf16[1024,512]{1,0:T(8,1...) custom-call(f32[1024,1024]{1,0:T(8,128)} %get-tuple-element.97.g_far, ...), custom_call_target="tpu_custom_call" | custom-call | tf_op jit(solution)/shard_map/glu_back_kernel/pallas_call | solution.py:716
  210.8 125.9 %back_kernel.1 = (bf16[1024,1024]{1,0:T(8,128)(2,1)}, bf16[2,8,128,1024]{3,2,1,0:T(8,128)(2,1)}, bf16[2,8,128,1024]{3,2,1,0:T(8,128)(2,1)}, bf16[2,8,128,512]{3,2,1,0:T(8,128)(2,1)}, f32[5,144,256]{2,1,0:T(8,128)}) custom-call(f32[1024,1024]{1,0:T(8,128)} %get-tuple-element.106.ga_hbm, f32[4,1024,256]{2,1,0:T(8,128)} %get-tuple-element.107.mixed_hbm, ...), custom_call_target="tpu_custom_call" | custom-call | tf_op jit(solution)/shard_map/back_kernel/pallas_call | solution.py:1147
  336.7 1.0 select_bitcast_fusion.1
  337.7 0.6 pad_maximum_fusion
  338.3 0.7 fusion.8
  339.0 1.8 slice_bitcast_fusion.1
  340.8 1.0 copy-done.5
  341.8 0.5 fusion.11
  342.3 1.7 copy-done.4
  344.0 4.7 %bitcast_convert_fusion = f32[2048,1024]{1,0:T(8,128)} fusion(bf16[2,8,128,1024]{3,2,1,0:T(8,128)(2,1)S(1)} %copy-done.4), kind=kLoop, calls=%fused_computation.1 | loop fusion | flops 2097152 | bytes 12582912 | tf_op jit(solution)/shard_map/convert_element_type | solution.py:1315
  348.7 5.3 %maximum_convert_fusion = f32[1024,2048]{1,0:T(8,128)} fusion(bf16[1024,1024]{1,0:T(8,128)(2,1)S(1)} %bitcast.58, bf16[1024,1024]{1,0:T(8,128)(2,1)S(1)} %bitcast.57), kind=kLoop, calls=%fused_computation | loop fusion | flops 8388608 | bytes 12582912 | tf_op jit(solution)/shard_map/convert_element_type | solution.py:1317
  354.0 1.2 copy-done.2
  355.2 1.2 copy-done.3
  356.4 3.0 fusion
  359.4 2.6 maximum_convert_fusion.1
  362.0 0.0 copy-done.6
  362.0 1.3 copy.37
  (9 shorter events, 0.0 us)
Async XLA Ops:
  126.6 48.3 %collective-permute-start = (bf16[1024,1024]{1,0:T(8,128)(2,1)}, bf16[1024,1024]{1,0:T(8,128)(2,1)S(1)}, u32[]{:S(2)}, u32[]{:S(2)}) collective-permute-start(bf16[1024,1024]{1,0:T(8,128)(2,1)} %get-tuple-element.94), channel_id=1, source_target_pairs={{0,1},{1,0},{2,3},{3,2},{4,5},{5,4},{6,7},{7,6},{8,9},{9,8},{10,11... | collective-permute-start | bytes 6291464 | tf_op jit(solution)/shard_map/ppermute | solution.py:1206
  127.2 42.5 %collective-permute-start.1 = (bf16[512,1024]{1,0:T(8,128)(2,1)}, bf16[512,1024]{1,0:T(8,128)(2,1)S(1)}, u32[]{:S(2)}, u32[]{:S(2)}) collective-permute-start(bf16[512,1024]{1,0:T(8,128)(2,1)} %get-tuple-element.95), channel_id=1, source_target_pairs={{0,4},{4,0},{8,12},{12,8},{16,20},{20,16},{24,28},{28,24},{1,5},{5... | collective-permute-start | bytes 3145736 | tf_op jit(solution)/shard_map/ppermute | solution.py:1211
  169.7 5.2 %copy-start.7 = (bf16[512,1024]{1,0:T(8,128)(2,1)}, bf16[512,1024]{1,0:T(8,128)(2,1)S(1)}, u32[]{:S(2)}) copy-start(bf16[512,1024]{1,0:T(8,128)(2,1)S(1)} %collective-permute-done.1.there_come) | copy-start | bytes 3145732
  174.9 1.3 copy-start.1
  339.0 2.8 copy-start.5
  341.8 2.2 copy-start.4
  348.7 5.3 %copy-start = (f32[1024,1024]{1,0:T(8,128)S(1)}, f32[1024,1024]{1,0:T(8,128)}, u32[]{:S(2)}) copy-start(f32[1024,1024]{1,0:T(8,128)} %get-tuple-element.77.residual) | copy-start | bytes 12582916
  348.7 6.5 %copy-start.2 = (f32[1024,1024]{1,0:T(8,128)S(1)}, f32[1024,1024]{1,0:T(8,128)}, u32[]{:S(2)}) copy-start(f32[1024,1024]{1,0:T(8,128)} %get-tuple-element.85) | copy-start | bytes 12582916
  348.7 7.7 %copy-start.3 = (f32[1024,1024]{1,0:T(8,128)S(1)}, f32[1024,1024]{1,0:T(8,128)}, u32[]{:S(2)}) copy-start(f32[1024,1024]{1,0:T(8,128)} %get-tuple-element.96) | copy-start | bytes 12582916
  359.4 2.6 copy-start.6

commit v5 on v4

--- a/solution.py
+++ b/solution.py
@@ -314,8 +314,10 @@
     inputs, cot, counts, gains, log_dt, skip, log_a, freq, c_real, c_imag, fwd_hbm, inv_hbm,
     w_value, w_gate, w_in, w_out,
     packed_ref, vec_ref, skip_ref, grad_ref, x_out, mixed_out, act_out, xs_out, ks_out,
+    value_out, sig_out, residual_out, n2_out, n2t_out,
     value_direct, value_via, gate_direct, gate_via, in_direct, in_via, out_direct, out_via,
     zr, zi, wr, wi, tmp, fwd, inv, packed, vec, got_vec, nx, k, mixed, act, xs, ks, ys,
+    owns, fars, values, gates, value_s, sig_s, residual_s, n2_s, n2t_s,
     local, send, recv, *, bits
 ):
     posts = Posts(bits, send, recv)
@@ -325,7 +327,9 @@
     posts.greet([0, 1, "core", "tensor"])
     tables = [
         pltpu.make_async_copy(src, dst, local.at[i])
-        for i, (src, dst) in enumerate(((fwd_hbm, fwd), (inv_hbm, inv)))
+        for i, (src, dst) in enumerate(
+            ((fwd_hbm, fwd), (inv_hbm, inv), (w_value, owns.at[0]), (w_gate, owns.at[1]))
+        )
     ]
     for copy in tables:
         copy.start()
@@ -401,8 +405,10 @@
     for flow in flows:
         next(flow)
 
-    def kernel_of(j, log_dt):
+    def kernel_of(j, log_dt, between=lambda: None):
         for i in range(half // LANES):
+            if i:
+                between()
             at = pl.ds(i * LANES, LANES)
             kernel_block(packed.at[1 - j, :, at], log_dt.at[:, at], k.at[2 * j, :, at], zr, zi, wr, wi, tmp)
 
@@ -412,10 +418,8 @@
     for come in params_come:
         come()
     vec_ref[0] = got_vec[0:1, mine]
-    next(flows[0])
-    kernel_of(1, vec_ref.at[0])
+    kernel_of(1, vec_ref.at[0], lambda: next(flows[0]))
     kernels_come.append(exchange(k.at[2], k.at[3], "core"))
-    next(flows[1])
     for i in range(nx.shape[0] // TOKEN_ROWS):
         at = pl.ds(i * TOKEN_ROWS, TOKEN_ROWS)
         source = inputs[at, :].astype(F32)
@@ -426,15 +430,16 @@
     for ref, at in ((vec, side), (got_vec, 1 - side)):
         skip_ref[:, pl.ds(pl.multiple_of(at * width, width), width)] = ref[1:2, :]
     stores = [
-        pltpu.make_async_copy(nx, x_out, local.at[2]),
-        pltpu.make_async_copy(packed, packed_ref, local.at[3]),
+        pltpu.make_async_copy(nx, x_out, local.at[4]),
+        pltpu.make_async_copy(packed, packed_ref, local.at[5]),
     ]
     for copy in stores:
         copy.start()
     for copy in tables:
         copy.wait()
     next(flows[0])
-    plan = ((0, flows[2]), (2, flows[1]), (1, flows[0]), (3, flows[2]))
+    next(flows[1])
+    plan = ((0, None), (2, flows[2]), (1, flows[1]), (3, flows[0]))
     for n, (j, flow) in enumerate(plan):
         there = lax.rem(side + j // 2, 2)
         which = lax.rem(core + j % 2, 2)
@@ -444,17 +449,52 @@
         params = vec if j < 2 else got_vec
         skip = params[1:2, pl.ds(pl.multiple_of(which * half, half), half)]
         conv_block(
-            nx[:, at], k[j], skip, fwd, inv, mixed.at[j], act.at[j], xs.at[j], ks.at[j], ys
+            nx[:, at], k[j], skip, fwd, inv, mixed.at[j], act.at[:, at], xs.at[j], ks.at[j], ys
         )
         for i, (src, dst) in enumerate(
-            ((mixed.at[j], mixed_out.at[j]), (act.at[j], act_out.at[:, at]),
-             (xs.at[j], xs_out.at[j]), (ks.at[j], ks_out.at[j]))
+            ((mixed.at[j], mixed_out.at[j]), (xs.at[j], xs_out.at[j]), (ks.at[j], ks_out.at[j]))
         ):
-            copy = pltpu.make_async_copy(src, dst, local.at[4 + 4 * j + i])
+            copy = pltpu.make_async_copy(src, dst, local.at[6 + 3 * j + i])
             copy.start()
             stores.append(copy)
-        next(flow)
-    for flow in (flows[0], flows[1], flows[1], flows[2], flows[2]):
+        if flow is not None:
+            next(flow)
+    next(flows[0], None)
+    loads = [
+        pltpu.make_async_copy(src, fars.at[i], local.at[18 + i])
+        for i, src in enumerate((value_direct, value_via, gate_direct, gate_via))
+    ]
+    for copy in loads:
+        copy.start()
+    stores.append(pltpu.make_async_copy(act, act_out, local.at[22]))
+    stores[-1].start()
+    for copy in loads:
+        copy.wait()
+    services = {0: [flows[2]], 1: [flows[1]], 2: [], 3: []}
+    for r in range(nx.shape[0] // TOKEN_ROWS):
+        at = pl.ds(r * TOKEN_ROWS, TOKEN_ROWS)
+        left = act[at, :]
+        project_all(left, owns.at[0], fars.at[0], fars.at[1], values)
+        project_all(left, owns.at[1], fars.at[2], fars.at[3], gates)
+        value = values[...]
+        sig = 1.0 / (1.0 + jnp.exp(-gates[...]))
+        value_s[r] = value.astype(BF16)
+        sig_s[r] = sig.astype(BF16)
+        residual = inputs[at, :].astype(F32) + (value * sig).astype(BF16).astype(F32)
+        residual_s[r] = residual
+        n2 = norm_forward(residual, gains[2:3, :], gains[3:4, :])[0].astype(BF16)
+        n2_s[r] = n2
+        n2t_s[r] = n2.T
+        for i, (src, dst) in enumerate((
+            (value_s, value_out.at[at]), (sig_s, sig_out.at[at]), (residual_s, residual_out.at[at]),
+            (n2_s, n2_out.at[at]), (n2t_s, n2t_out.at[:, at]),
+        )):
+            copy = pltpu.make_async_copy(src.at[r], dst, local.at[23 + 5 * r + i])
+            copy.start()
+            stores.append(copy)
+        for flow in services[r]:
+            next(flow)
+    for flow in (flows[1], flows[2], flows[2]):
         next(flow, None)
     for copy in stores:
         copy.wait()
@@ -470,17 +510,20 @@
     modes = log_a.shape[0]
     half = d // 4
     units = w_in.shape[1] // 2
+    chunks = n // TOKEN_ROWS
     vmem = pl.BlockSpec(memory_space=pltpu.VMEM)
     hbm = pl.BlockSpec(memory_space=pl.ANY)
     shape = jax.ShapeDtypeStruct
     return pl.pallas_call(
         functools.partial(front_body, bits=bits),
         in_specs=[vmem] * 2 + [pl.BlockSpec(memory_space=pltpu.SMEM)] + [vmem] * 7 + [hbm] * 6,
-        out_specs=[hbm, vmem, vmem, vmem] + [hbm] * 13,
+        out_specs=[hbm, vmem, vmem, vmem] + [hbm] * 18,
         out_shape=[
             shape((2, 4 * modes, half), F32), shape((2, 1, half), F32), shape((1, d), F32),
             shape((n, d), BF16), shape((n, d), BF16), shape((4, n, half), F32), shape((n, d), BF16),
             shape((4, 2 * n, half), BF16), shape((4, 2 * n, half), BF16),
+            shape((n, d), BF16), shape((n, d), BF16), shape((n, d), F32), shape((n, d), BF16),
+            shape((d, n), BF16),
         ]
         + [shape((d, half), BF16)] * 4
         + [shape((d, units), BF16)] * 2
@@ -491,10 +534,15 @@
             pltpu.VMEM((2, 4 * modes, half), F32),
             pltpu.VMEM((2, d // 2), F32), pltpu.VMEM((2, d // 2), F32),
             pltpu.VMEM((n, d), BF16), pltpu.VMEM((4, n, half), BF16),
-            pltpu.VMEM((4, n, half), F32), pltpu.VMEM((4, n, half), BF16),
+            pltpu.VMEM((4, n, half), F32), pltpu.VMEM((n, d), BF16),
             pltpu.VMEM((4, 2 * n, half), BF16), pltpu.VMEM((4, 2 * n, half), BF16),
             pltpu.VMEM((2 * n, half), BF16),
-            pltpu.SemaphoreType.DMA((20,)),
+            pltpu.VMEM((2, d, 2 * half), BF16), pltpu.VMEM((4, d, half), BF16),
+            pltpu.VMEM((TOKEN_ROWS, d), F32), pltpu.VMEM((TOKEN_ROWS, d), F32),
+            pltpu.VMEM((chunks, TOKEN_ROWS, d), BF16), pltpu.VMEM((chunks, TOKEN_ROWS, d), BF16),
+            pltpu.VMEM((chunks, TOKEN_ROWS, d), F32), pltpu.VMEM((chunks, TOKEN_ROWS, d), BF16),
+            pltpu.VMEM((chunks, d, TOKEN_ROWS), BF16),
+            pltpu.SemaphoreType.DMA((24 + 5 * chunks,)),
             pltpu.SemaphoreType.DMA((40,)), pltpu.SemaphoreType.DMA((40,)),
         ],
         compiler_params=params_of(collective_id=5, has_side_effects=True),
@@ -541,46 +589,6 @@
         (via, far + (1 - core) * width, width),
     ):
         out[:, pl.ds(pl.multiple_of(first, width), count)] = dot(left, ref[...])
-
-
-def glu_body(
-    act, source, value_own, value_direct, value_via, gate_own, gate_direct, gate_via, gains,
-    value_ref, sig_ref, residual_ref, n2_ref, n2t_ref, values, gates,
-):
-    project_all(act[...], value_own, value_direct, value_via, values)
-    project_all(act[...], gate_own, gate_direct, gate_via, gates)
-    value = values[...]
-    sig = 1.0 / (1.0 + jnp.exp(-gates[...]))
-    value_ref[...] = value.astype(BF16)
-    sig_ref[...] = sig.astype(BF16)
-    residual = source[...].astype(F32) + (value * sig).astype(BF16).astype(F32)
-    residual_ref[...] = residual
-    n2 = norm_forward(residual, gains[2:3, :], gains[3:4, :])[0].astype(BF16)
-    n2_ref[...] = n2
-    n2t_ref[...] = n2.T
-
-
-def glu_kernel(act, source, weights, gains):
-    n, d = act.shape
-    rows = pl.BlockSpec((TOKEN_ROWS, d), lambda i: (i, 0))
-
-    def whole(a):
-        return pl.BlockSpec(a.shape, lambda i: (0, 0), pipeline_mode=pl.Buffered(1))
-
-    return pl.pallas_call(
-        glu_body,
-        grid=(n // TOKEN_ROWS,),
-        in_specs=[rows, rows] + [whole(w) for w in weights] + [whole(gains)],
-        out_specs=[rows] * 4 + [pl.BlockSpec((d, TOKEN_ROWS), lambda i: (0, i))],
-        out_shape=[
-            jax.ShapeDtypeStruct((n, d), BF16), jax.ShapeDtypeStruct((n, d), BF16),
-            jax.ShapeDtypeStruct((n, d), F32), jax.ShapeDtypeStruct((n, d), BF16),
-            jax.ShapeDtypeStruct((d, n), BF16),
-        ],
-        scratch_shapes=[pltpu.VMEM((TOKEN_ROWS, d), F32)] * 2,
-        compiler_params=params_of(),
-        name="glu_kernel",
-    )(act, source, *weights, gains)
 
 
 def glu_back_body(
@@ -1195,11 +1203,69 @@
 BACK_ROUNDS = {1: ("in", "out"), 3: ("glu", "in"), "norm": ("out", "in", "glu")}
 
 
+def last_body(
+    counts, residual, far, own, in_all, out_all, glu_all, small,
+    output, in_total, out_total, value_total, gate_total, *rest, modes
+):
+    core, side = lax.axis_index("core"), lax.axis_index("tensor")
+    used = (side < counts[0]).astype(F32)
+    output[...] = (used * (residual[...] + (far[...] + own[...]))).astype(BF16)
+    out_total[...] = out_all[...].astype(F32)
+    width = in_all.shape[2]
+    half = glu_all.shape[2] // 2
+    for i in range(2):
+        in_total[:, i * width : (i + 1) * width] = in_all[i].astype(F32)
+        value_total[:, i * half : (i + 1) * half] = glu_all[i, :, :half].astype(F32)
+        gate_total[:, i * half : (i + 1) * half] = glu_all[i, :, half:].astype(F32)
+
+    @pl.when(pl.program_id(0) == 0)
+    def _():
+        count = small.shape[2]
+        top = 4 * modes
+        spans = [(i * modes, modes) for i in range(4)] + [(top + i, 1) for i in (0, 8, 9, 10, 11, 12)]
+        for ref, (first, rows) in zip(rest, spans):
+            for i, which in ((-2, core), (-1, 1 - core)):
+                at = pl.ds(pl.multiple_of(which * count, count), count)
+                ref[:, at] = small[small.shape[0] + i, first : first + rows, :]
+
+
+def last_kernel(counts, residual, far, own, in_all, out_all, glu_all, small):
+    n, d = residual.shape
+    steps = 8
+    modes = (small.shape[1] - 16) // 4
+    units, cols, count = in_all.shape[2], glu_all.shape[2], 2 * small.shape[2]
+    shape = jax.ShapeDtypeStruct
+
+    def rows(count, width):
+        return pl.BlockSpec((count // steps, width), lambda i: (i, 0))
+
+    def pair(width):
+        return pl.BlockSpec((2, d // steps, width), lambda i: (0, i, 0))
+
+    def whole(shape):
+        return pl.BlockSpec(shape, lambda i: (0,) * len(shape))
+
+    sizes = [(modes, count)] * 4 + [(1, count)] * 6
+    return pl.pallas_call(
+        functools.partial(last_body, modes=modes),
+        grid=(steps,),
+        in_specs=[
+            pl.BlockSpec(memory_space=pltpu.SMEM), rows(n, d), rows(n, d), rows(n, d),
+            pair(units), rows(2 * units, d), pair(cols), whole(small.shape),
+        ],
+        out_specs=[rows(n, d), rows(d, 2 * units), rows(2 * units, d), rows(d, cols), rows(d, cols)]
+        + [whole(size) for size in sizes],
+        out_shape=[
+            shape((n, d), BF16), shape((d, 2 * units), F32), shape((2 * units, d), F32),
+            shape((d, cols), F32), shape((d, cols), F32),
+        ]
+        + [shape(size, F32) for size in sizes],
+        compiler_params=params_of(),
+        name="last_kernel",
+    )(counts, residual, far, own, in_all, out_all, glu_all, small)
+
+
 SWAP = ((0, 1), (1, 0))
-
-
-def over_core(values):
-    return lax.ppermute(values, "core", SWAP)
 
 
 def over_tensor(values):
@@ -1209,52 +1275,6 @@
 def over_pair(values, flip):
     size = lax.axis_size("pair")
     return lax.ppermute(values, "pair", [(p, p ^ flip) for p in range(size)])
-
-
-def place_in(group):
-    first, count = group
-    return (lax.axis_index("pair") // (1 << first)) % (1 << count)
-
-
-def flips_of(group):
-    first, count = group
-    return [j << first for j in range(1, 1 << count)]
-
-
-def pair_bits():
-    return log2_of(lax.axis_size("pair"))
-
-
-def by_bits(values):
-    bits = pair_bits()
-    return values.reshape(*[2] * bits, values.shape[0] >> bits, values.shape[1])
-
-
-def split_over(total, bit):
-    axis = 0 if bit == 0 else pair_bits() - bit
-    return part(total, place_in((bit, 1)), axis), part(total, 1 - place_in((bit, 1)), axis).astype(BF16)
-
-
-def gathered(keep, come, group, axis):
-    me = place_in(group)
-    parts = [keep] + come
-    bit = 1
-    while bit < len(parts):
-        swapped = (me & bit) != 0
-        parts = [jnp.where(swapped, parts[k ^ bit], parts[k]) for k in range(len(parts))]
-        bit *= 2
-    return jnp.concatenate(parts, axis=axis)
-
-
-def ordered(index, mine, other, axis):
-    first = jnp.where(index == 0, mine, other)
-    second = jnp.where(index == 0, other, mine)
-    return jnp.concatenate([first, second], axis=axis)
-
-
-def part(values, index, axis):
-    half = values.shape[axis] // 2
-    return lax.dynamic_slice_in_dim(values, index * half, half, axis)
 
 
 def together(*values):
@@ -1266,7 +1286,6 @@
     w_value, w_gate, ln2_gain, ln2_bias, w_in, w_out, cotangent,
 ):
     _, length, width = inputs.shape
-    core, side = lax.axis_index("core"), lax.axis_index("tensor")
     source = inputs.reshape(length, width)
     gains = jnp.stack([ln1_gain, ln1_bias, ln2_gain, ln2_bias]).astype(F32)
     table = transform_table(length)
@@ -1274,13 +1293,13 @@
     inv = jnp.asarray(np.ascontiguousarray((table.T / length).astype(ml_dtypes.bfloat16)))
     (
         packed, log_dts, skip, grad_low, normed1, mixed, act, spectrum, kernel_spectrum,
+        value_proj, gate_sig, residual, normed2, normed2_t,
         value_direct, value_via, gate_direct, gate_via, in_direct, in_via, out_direct, out_via,
     ) = front_kernel(
         source, cotangent.reshape(length, width), counts, gains, log_dt[None], skip_gain[None],
         log_a.T, freq.T, c_real.T, c_imag.T, fwd, inv, w_value, w_gate, w_in, w_out,
     )
     glu_weights = (w_value, value_direct, value_via, w_gate, gate_direct, gate_via)
-    value_proj, gate_sig, residual, normed2, normed2_t = glu_kernel(act, source, glu_weights, gains)
     units = in_direct.shape[1]
     far_ffn, far_normed2, there_box, there_keep, there_out = ffn_kernel(
         normed2, normed2_t, grad_low, (in_via, in_direct), (out_via, out_direct), units, False
@@ -1308,35 +1327,29 @@
         here_out, out_come, out_z, here_glu.reshape(by_block), there_glu.reshape(by_block),
         skip, gains, gain_second_grad, bias_second_grad, packed, log_dts,
     )
-    used_flag = (side < counts[0]).astype(F32)
-    output = (used_flag * (residual + (far_ffn + own_ffn))).astype(BF16).reshape(inputs.shape)
-    input_grad = input_grad.reshape(inputs.shape)
-    small = ordered(core, small[-2], small[-1], 1)
-    out_total = out_all.reshape(-1, width).astype(F32)
-    in_all = in_all.reshape(2, width, -1)
-    in_total = jnp.concatenate([in_all[0], in_all[1]], axis=1).astype(F32)
-    glu_all = glu_all.reshape(2, width, -1)
-    cut = glu_all.shape[2] // 2
-    value_total = jnp.concatenate([glu_all[0, :, :cut], glu_all[1, :, :cut]], axis=1).astype(F32)
-    gate_total = jnp.concatenate([glu_all[0, :, cut:], glu_all[1, :, cut:]], axis=1).astype(F32)
-
-    modes = log_a.shape[1]
-    top = 4 * modes
+    (
+        output, in_total, out_total, value_total, gate_total,
+        log_a_grad, freq_grad, real_grad, imag_grad, *vectors,
+    ) = last_kernel(
+        counts, residual, far_ffn, own_ffn, in_all.reshape(2, width, -1), out_all.reshape(-1, width),
+        glu_all.reshape(2, width, -1), small,
+    )
+    log_dt_grad, skip_grad, gain1, bias1, gain2, bias2 = (v.reshape(-1) for v in vectors)
     return (
-        output,
-        input_grad,
-        small[top + 9],
-        small[top + 10],
-        small[top],
-        small[:modes].T,
-        small[modes : 2 * modes].T,
-        small[2 * modes : 3 * modes].T,
-        small[3 * modes : 4 * modes].T,
-        small[top + 8],
+        output.reshape(inputs.shape),
+        input_grad.reshape(inputs.shape),
+        gain1,
+        bias1,
+        log_dt_grad,
+        log_a_grad.T,
+        freq_grad.T,
+        real_grad.T,
+        imag_grad.T,
+        skip_grad,
         value_total,
         gate_total,
-        small[top + 11],
-        small[top + 12],
+        gain2,
+        bias2,
         in_total,
         out_total,
     )

time: 366 us -> 345 us (0.943)
  other arithmetic: 18.5 us -> 0.63 us
  local copies, waits for them, and re-layouts: 12.8 us -> 5.39 us
  Pallas kernels: 323 us -> 327 us
    convert_element_type x3 -> x0, other arithmetic: 12.6 us -> none  [the longest x1 5.28 us: shards(): in_total = jnp.concatenate([in_all[0], in_all[1]], axis=1).astype(F32)]
    pallas_call x1, Pallas kernels: 12.5 us -> 17.6 us  [last_kernel(): pl.pallas_call(functools.partial(last_body, modes=modes), grid=(steps,),...]
    unnamed x17 -> x7, local copies, waits for them, and re-layouts: 7.74 us -> 2.65 us
  transfers between devices with their start and end apart: 2 -> 2, of which waited for: 1 -> 1; matrix products, arithmetic and copies ran while one was open for 0% -> 0% of each run, Pallas kernels for 11% -> 12%
where the time goes in v5:
time: 345 us; the launch traced here: 343 us
  Pallas kernels  327 us (95%)
  local copies, waits for them, and re-layouts  5.39 us (2%)
  waiting for transfers between devices  4.82 us (1%)
    pallas_call x1, Pallas kernels, back_kernel(): pl.pallas_call(functools.partial(back_body, bits=bits), in_specs=[hbm] *...  126 us
    pallas_call x2, Pallas kernels, ffn_kernel(): pl.pallas_call(ffn_body, grid=(2 * half,), in_specs=[whole(n2), whole(n2t...  81.6 us
    pallas_call x1, Pallas kernels, front_kernel(): pl.pallas_call(functools.partial(front_body, bits=bits), in_specs=[vmem]...  67.7 us
    pallas_call x1, Pallas kernels, glu_back_kernel(): pl.pallas_call(functools.partial(glu_back_body, bits=bits), grid=(chunks...  34.7 us
    pallas_call x1, Pallas kernels, last_kernel(): pl.pallas_call(functools.partial(last_body, modes=modes), grid=(steps,),...  17.6 us
  transfers between devices with their start and end apart: 2, of which 1 were waited for; matrix products, arithmetic and copies ran while one was open for 0% of the time, Pallas kernels for 12%

profile of v5, /device:TPU:0, one launch (start us, length us, event | category | flops | bytes accessed | tf_op | source)
XLA Modules:
  0.0 342.6 jit_solution(12501498066035758344)
XLA Ops:
  1.3 0.7 stack.15
  2.0 0.7 stack.16
  2.7 0.7 stack.17
  3.4 0.7 stack.18
  4.0 0.6 maximum_convert_fusion.gains
  4.7 67.7 %front_kernel.1 = (f32[2,128,256]{2,1,0:T(8,128)}, f32[2,1,256]{2,1,0:T(1,128)}, f32[1,1024]{1,0:T(1,128)}, bf16[1024,1024]{1,0:T(8,128)(2,1)}, bf16[1024,1024]{...) custom-call(bf16[1024,1024]{1,0:T(8,128)(2,1)} %bitcast.32, ...), custom_call_target="tpu_custom_call" | custom-call | tf_op jit(solution)/shard_map/front_kernel/pallas_call | solution.py:517
  72.4 40.7 %ffn_kernel.2 = (f32[1024,1024]{1,0:T(8,128)}, f32[1024,1024]{1,0:T(8,128)}, bf16[512,1024]{1,0:T(8,128)(2,1)}, bf16[512,1024]{1,0:T(8,128)(2,1)}, bf16[1024,1024]{1,0:T(8,128)(2,1)}) custom-call(bf16[1024,1024]{1,0:T(8,128)(2,1)} %get-tuple-element.98.n2, bf16[1024,1024]{1,0:T(8,128)(2,1)} %get-tuple-element.89.n2t, ...), custom_call_target="tpu_custom_call" | custom-call | tf_op jit(solution)/shard_map/ffn_kernel/pallas_call | solution.py:824
  113.1 1.6 collective-permute-start
  114.6 0.9 collective-permute-start.1
  115.6 40.9 %ffn_kernel.3 = (f32[1024,1024]{1,0:T(8,128)}, f32[1024,1024]{1,0:T(8,128)}, bf16[512,1024]{1,0:T(8,128)(2,1)}, f32[512,1024]{1,0:T(8,128)}, f32[1024,1024]{1,0:T(8,128)}) custom-call(bf16[1024,1024]{1,0:T(8,128)(2,1)} %get-tuple-element.98.n2, bf16[1024,1024]{1,0:T(8,128)(2,1)} %get-tuple-element.89.n2t, bf16[1024,1024]{1,0:T(8,128)(2,1)} %get-tuple-element.90.gl.cot, ...), custom_call_target="tpu_custom_call" | custom-call | tf_op jit(solution)/shard_map/ffn_kernel/pallas_call | solution.py:824
  156.5 0.0 collective-permute-done.1.there_come
  156.5 0.0 copy-start.2
  156.5 4.8 %collective-permute-done = bf16[1024,1024]{1,0:T(8,128)(2,1)S(1)} collective-permute-done((bf16[1024,1024]{1,0:T(8,128)(2,1)}, bf16[1024,1024]{1,0:T(8,128)(2,1)S(1)}, u32[]{:S(2)}, u32[]{:S(2)}) %collective-permute-start) | collective-permute-done | bytes 2097184 | tf_op jit(solution)/shard_map/ppermute | solution.py:1272
  161.4 0.0 copy-start
  161.4 0.0 copy-done.2
  161.4 1.3 copy-done
  162.7 34.7 %glu_back_kernel.1 = (f32[1024,1024]{1,0:T(8,128)}, f32[1024,1024]{1,0:T(8,128)}, f32[1,1024]{1,0:T(1,128)}, f32[1,1024]{1,0:T(1,128)}, bf16[1024,512]{1,0:T(8,1...) custom-call(f32[1024,1024]{1,0:T(8,128)} %get-tuple-element.107.g_fa, ...), custom_call_target="tpu_custom_call" | custom-call | tf_op jit(solution)/shard_map/glu_back_kernel/pallas_call | solution.py:724
  197.4 125.8 %back_kernel.1 = (bf16[1024,1024]{1,0:T(8,128)(2,1)}, bf16[2,8,128,1024]{3,2,1,0:T(8,128)(2,1)}, bf16[2,8,128,1024]{3,2,1,0:T(8,128)(2,1)}, bf16[2,8,128,512]{3,2,1,0:T(8,128)(2,1)}, f32[5,144,256]{2,1,0:T(8,128)}) custom-call(f32[1024,1024]{1,0:T(8,128)} %get-tuple-element.121.ga_hbm, f32[4,1024,256]{2,1,0:T(8,128)} %get-tuple-element.122.mixed_hbm, ...), custom_call_target="tpu_custom_call" | custom-call | tf_op jit(solution)/shard_map/back_kernel/pallas_call | solution.py:1155
  323.2 0.0 copy-start.1
  323.2 17.6 %last_kernel.1 = (bf16[1024,1024]{1,0:T(8,128)(2,1)}, f32[1024,2048]{1,0:T(8,128)}, f32[2048,1024]{1,0:T(8,128)}, f32[1024,512]{1,0:T(8,128)}, f32[1024,512]{1,0...) custom-call(s32[1]{0:T(128)S(6)} %copy.36.counts, ...), custom_call_target="tpu_custom_call" | custom-call | tf_op jit(solution)/shard_map/last_kernel/pallas_call | solution.py:1249
  340.8 0.0 copy-done.1
  340.9 1.3 copy.37
Async XLA Ops:
  113.1 48.3 %collective-permute-start = (bf16[1024,1024]{1,0:T(8,128)(2,1)}, bf16[1024,1024]{1,0:T(8,128)(2,1)S(1)}, u32[]{:S(2)}, u32[]{:S(2)}) collective-permute-start(bf16[1024,1024]{1,0:T(8,128)(2,1)} %get-tuple-element.104), channel_id=1, source_target_pairs={{0,1},{1,0},{2,3},{3,2},{4,5},{5,4},{6,7},{7,6},{8,9},{9,8},{10,11... | collective-permute-start | bytes 6291464 | tf_op jit(solution)/shard_map/ppermute | solution.py:1272
  114.6 41.9 %collective-permute-start.1 = (bf16[512,1024]{1,0:T(8,128)(2,1)}, bf16[512,1024]{1,0:T(8,128)(2,1)S(1)}, u32[]{:S(2)}, u32[]{:S(2)}) collective-permute-start(bf16[512,1024]{1,0:T(8,128)(2,1)} %get-tuple-element.105), channel_id=1, source_target_pairs={{0,4},{4,0},{8,12},{12,8},{16,20},{20,16},{24,28},{28,24},{1,5},{5... | collective-permute-start | bytes 3145736 | tf_op jit(solution)/shard_map/ppermute | solution.py:1277
  156.5 4.8 %copy-start.2 = (bf16[512,1024]{1,0:T(8,128)(2,1)}, bf16[512,1024]{1,0:T(8,128)(2,1)S(1)}, u32[]{:S(2)}) copy-start(bf16[512,1024]{1,0:T(8,128)(2,1)S(1)} %collective-permute-done.1.there_come) | copy-start | bytes 3145732
  161.4 1.3 copy-start
  323.2 17.6 %copy-start.1 = (bf16[1024,1024]{1,0:T(8,128)(2,1)S(1)}, bf16[1024,1024]{1,0:T(8,128)(2,1)}, u32[]{:S(2)}) copy-start(bf16[1024,1024]{1,0:T(8,128)(2,1)} %get-tuple-element.143) | copy-start | bytes 6291460

commit v6 on v5

--- a/solution.py
+++ b/solution.py
@@ -33,14 +33,6 @@
     def __init__(self, pairs, send, recv):
         self.pairs, self.send, self.recv = pairs, send, recv
         self.other = {"core": 1 - lax.axis_index("core")}
-
-    def greet(self):
-        pl.semaphore_signal(
-            pltpu.get_barrier_semaphore(), inc=1, device_id=self.other, device_id_type=MESH
-        )
-
-    def meet(self):
-        pl.semaphore_wait(pltpu.get_barrier_semaphore(), 1)
 
     def copies(self, slot):
         return [
@@ -592,7 +584,7 @@
 
 
 def glu_back_body(
-    g_far, g_own, residual, cot, value, sig, act, value_own, value_direct, value_via,
+    g_sum, residual, cot, value, sig, act, value_own, value_direct, value_via,
     gate_own, gate_direct, gate_via, gains,
     there_keep, there_come, in_box, here_out, out_come,
     resid_ref, ga_ref, gain_ref, bias_ref, there_ref, here_ref, in_x, in_y, out_z,
@@ -643,7 +635,7 @@
     def _():
         standard, inv_std = norm_forward(residual[...], 1.0, 0.0)[1:]
         part, gain_grad, bias_grad = norm_backward(
-            g_far[...] + g_own[...], standard, inv_std, gains[2:3, :]
+            g_sum[...], standard, inv_std, gains[2:3, :]
         )
         new = step == 0
         gain_ref[...] = jnp.where(new, 0.0, gain_ref[...]) + gain_grad[None]
@@ -704,7 +696,7 @@
 
 
 def glu_back_kernel(
-    g_far, g_own, residual, cot, value, sig, act, weights, gains,
+    g_sum, residual, cot, value, sig, act, weights, gains,
     there_keep, there_come, in_box, here_out, out_come,
 ):
     bits = log2_of(lax.axis_size("pair"))
@@ -724,7 +716,7 @@
     return pl.pallas_call(
         functools.partial(glu_back_body, bits=bits),
         grid=(chunks + 4,),
-        in_specs=[rows] * 6 + [whole(act)] + [whole(w) for w in weights] + [whole(gains)] + [hbm] * 5,
+        in_specs=[rows] * 5 + [whole(act)] + [whole(w) for w in weights] + [whole(gains)] + [hbm] * 5,
         out_specs=[rows, rows, vector, vector, weight, weight] + [hbm] * 3,
         scratch_shapes=[pltpu.VMEM((4, n, width), BF16)] * 2
         + [pltpu.VMEM((2, d, 2 * width), BF16)] * 2
@@ -741,17 +733,35 @@
         ],
         compiler_params=params_of(collective_id=2, has_side_effects=True),
         name="glu_back_kernel",
-    )(g_far, g_own, residual, cot, value, sig, act, *weights, gains, *extra)
-
-
-def ffn_body(
-    n2, n2t, gl, ia, ib, oa, ob, ffn, gn2, box_ref, keep_ref, out_ref,
-    wi, wo, h, gp, total, in_mine, out_mine, in_theirs, out_theirs, send, recv,
-):
+    )(g_sum, residual, cot, value, sig, act, *weights, gains, *extra)
+
+
+def ffn_body(*refs, own):
+    n2, n2t, gl, ia, ib, oa, ob, before, *refs = refs
+    if own:
+        counts, gn2_before, *refs = refs
+    first_out, gn2, box_ref, keep_ref, out_ref, *refs = refs
+    if own:
+        ffn, *refs = refs
+    else:
+        ffn = first_out
+    wi, wo, h, gp, total, in_mine, out_mine, in_theirs, out_theirs, local, send, recv = refs
     step, half = pl.program_id(0), in_mine.shape[0]
     first = step < half
     cores = CoreExchange([(in_mine, in_theirs), (out_mine, out_theirs)], send, recv)
-    pl.when(step == 0)(cores.greet)
+    barrier = pltpu.get_barrier_semaphore()
+
+    def before_loads():
+        pairs = [(before, ffn)] + ([(gn2_before, gn2)] if own else [])
+        return [pltpu.make_async_copy(src, dst, local.at[i]) for i, (src, dst) in enumerate(pairs)]
+
+    @pl.when(step == 0)
+    def _():
+        pl.semaphore_signal(barrier, inc=1, device_id=cores.other, device_id_type=MESH)
+        for copy in before_loads():
+            copy.start()
+        if not own:
+            gn2[...] = jnp.zeros_like(gn2)
 
     @pl.when(first)
     def _():
@@ -763,25 +773,28 @@
         wi[...] = ib[...]
         wo[...] = ob[...]
 
-    @pl.when(step == 0)
-    def _():
-        ffn[...] = jnp.zeros_like(ffn)
-        gn2[...] = jnp.zeros_like(gn2)
-
     w1, w2 = wi[...], wo[...]
     for r in range(n2.shape[0] // TOKEN_ROWS):
         at = pl.ds(r * TOKEN_ROWS, TOKEN_ROWS)
         act, slope = gelu_both(dot(n2[at, :], w1))
-        hidden = act.astype(BF16)
-        grad_pre = (contract_cols(gl[at, :], w2) * slope).astype(BF16)
-        h[at, :] = hidden
-        gp[at, :] = grad_pre
-        ffn[at, :] += dot(hidden, w2)
-        gn2[at, :] += contract_cols(grad_pre, w1)
+        h[at, :] = act.astype(BF16)
+        gp[at, :] = (contract_cols(gl[at, :], w2) * slope).astype(BF16)
+
+    @pl.when(step == 0)
+    def _():
+        for copy in before_loads():
+            copy.wait()
+
+    for r in range(n2.shape[0] // TOKEN_ROWS):
+        at = pl.ds(r * TOKEN_ROWS, TOKEN_ROWS)
+        ffn[at, :] += dot(h[at, :], w2)
+        gn2[at, :] += contract_cols(gp[at, :], w1)
     out_grad = contract_rows(h[...], gl[...])
     in_grad = dot(n2t[...], gp[...])
 
-    pl.when(step == 0)(cores.meet)
+    @pl.when(step == 0)
+    def _():
+        pl.semaphore_wait(barrier, 1)
 
     @pl.when(first)
     def _():
@@ -801,28 +814,37 @@
 
     @pl.when(step == 2 * half - 1)
     def _():
+        if own:
+            used = (lax.axis_index("tensor") < counts[0]).astype(F32)
+            first_out[...] = (used * ffn[...]).astype(BF16)
         cores.sent(half)
 
 
-def ffn_kernel(n2, n2t, gl, ins, outs, units, own):
+def ffn_kernel(n2, n2t, gl, ins, outs, units, before, own=()):
     n, d = n2.shape
     half = units // FFN_TILE
+    owned = bool(own)
+    hbm = pl.BlockSpec(memory_space=pl.ANY)
 
     def whole(a):
         return pl.BlockSpec(a.shape, lambda s: (0, 0), pipeline_mode=pl.Buffered(1))
 
     def fst(s):
         at = jnp.minimum(s, half - 1)
-        return at + (1 - lax.axis_index("core")) * half if own else at
+        return at + (1 - lax.axis_index("core")) * half if owned else at
 
     def snd(s):
         at = jnp.maximum(s - half, 0)
-        return at + lax.axis_index("core") * half if own else at
+        return at + lax.axis_index("core") * half if owned else at
+
+    def late(s):
+        return jnp.maximum(s - half, 0)
 
     total = pl.BlockSpec((n, d), lambda s: (0, 0))
-    dtype = F32 if own else BF16
+    dtype = F32 if owned else BF16
+    shape = jax.ShapeDtypeStruct
     return pl.pallas_call(
-        ffn_body,
+        functools.partial(ffn_body, own=owned),
         grid=(2 * half,),
         in_specs=[
             whole(n2), whole(n2t), whole(gl),
@@ -830,28 +852,31 @@
             pl.BlockSpec((d, FFN_TILE), lambda s: (0, snd(s))),
             pl.BlockSpec((FFN_TILE, d), lambda s: (fst(s), 0)),
             pl.BlockSpec((FFN_TILE, d), lambda s: (snd(s), 0)),
-        ],
+            hbm,
+        ]
+        + ([pl.BlockSpec(memory_space=pltpu.SMEM), hbm] if owned else []),
         out_specs=[
             total, total,
-            pl.BlockSpec((d // 2, FFN_TILE), lambda s: (0, jnp.maximum(s - half, 0))),
-            pl.BlockSpec((d // 2, FFN_TILE), lambda s: (0, jnp.maximum(s - half, 0))),
-            pl.BlockSpec((FFN_TILE, d), lambda s: (jnp.maximum(s - half, 0), 0)),
+            pl.BlockSpec((d // 2, FFN_TILE), lambda s: (0, late(s))),
+            pl.BlockSpec((d // 2, FFN_TILE), lambda s: (0, late(s))),
+            pl.BlockSpec((FFN_TILE, d), lambda s: (late(s), 0)),
         ],
-        scratch_shapes=[
+        scratch_shapes=([pltpu.VMEM((n, d), F32)] if owned else [])
+        + [
             pltpu.VMEM((d, FFN_TILE), BF16), pltpu.VMEM((FFN_TILE, d), BF16),
             pltpu.VMEM((n, FFN_TILE), BF16), pltpu.VMEM((n, FFN_TILE), BF16),
             pltpu.VMEM((d, FFN_TILE), F32),
         ]
         + [pltpu.VMEM((half, d, FFN_TILE), BF16), pltpu.VMEM((half, FFN_TILE, d), BF16)] * 2
+        + [pltpu.SemaphoreType.DMA((2,))]
         + exchange_sems(2, half),
         out_shape=[
-            jax.ShapeDtypeStruct((n, d), F32), jax.ShapeDtypeStruct((n, d), F32),
-            jax.ShapeDtypeStruct((d // 2, units), BF16), jax.ShapeDtypeStruct((d // 2, units), dtype),
-            jax.ShapeDtypeStruct((units, d), dtype),
+            shape((n, d), BF16 if owned else F32), shape((n, d), F32),
+            shape((d // 2, units), BF16), shape((d // 2, units), dtype), shape((units, d), dtype),
         ],
-        compiler_params=params_of(collective_id=int(own), has_side_effects=True),
+        compiler_params=params_of(collective_id=int(owned), has_side_effects=True),
         name="ffn_kernel",
-    )(n2, n2t, gl, *ins, *outs)
+    )(n2, n2t, gl, *ins, *outs, before, *own)
 
 
 def norm_forward(values, norm_gain, norm_bias):
@@ -1204,12 +1229,9 @@
 
 
 def last_body(
-    counts, residual, far, own, in_all, out_all, glu_all, small,
-    output, in_total, out_total, value_total, gate_total, *rest, modes
+    in_all, out_all, glu_all, small, in_total, out_total, value_total, gate_total, *rest, modes
 ):
-    core, side = lax.axis_index("core"), lax.axis_index("tensor")
-    used = (side < counts[0]).astype(F32)
-    output[...] = (used * (residual[...] + (far[...] + own[...]))).astype(BF16)
+    core = lax.axis_index("core")
     out_total[...] = out_all[...].astype(F32)
     width = in_all.shape[2]
     half = glu_all.shape[2] // 2
@@ -1229,8 +1251,8 @@
                 ref[:, at] = small[small.shape[0] + i, first : first + rows, :]
 
 
-def last_kernel(counts, residual, far, own, in_all, out_all, glu_all, small):
-    n, d = residual.shape
+def last_kernel(in_all, out_all, glu_all, small):
+    d = in_all.shape[1]
     steps = 8
     modes = (small.shape[1] - 16) // 4
     units, cols, count = in_all.shape[2], glu_all.shape[2], 2 * small.shape[2]
@@ -1250,19 +1272,18 @@
         functools.partial(last_body, modes=modes),
         grid=(steps,),
         in_specs=[
-            pl.BlockSpec(memory_space=pltpu.SMEM), rows(n, d), rows(n, d), rows(n, d),
             pair(units), rows(2 * units, d), pair(cols), whole(small.shape),
         ],
-        out_specs=[rows(n, d), rows(d, 2 * units), rows(2 * units, d), rows(d, cols), rows(d, cols)]
+        out_specs=[rows(d, 2 * units), rows(2 * units, d), rows(d, cols), rows(d, cols)]
         + [whole(size) for size in sizes],
         out_shape=[
-            shape((n, d), BF16), shape((d, 2 * units), F32), shape((2 * units, d), F32),
+            shape((d, 2 * units), F32), shape((2 * units, d), F32),
             shape((d, cols), F32), shape((d, cols), F32),
         ]
         + [shape(size, F32) for size in sizes],
         compiler_params=params_of(),
         name="last_kernel",
-    )(counts, residual, far, own, in_all, out_all, glu_all, small)
+    )(in_all, out_all, glu_all, small)
 
 
 SWAP = ((0, 1), (1, 0))
@@ -1302,13 +1323,16 @@
     glu_weights = (w_value, value_direct, value_via, w_gate, gate_direct, gate_via)
     units = in_direct.shape[1]
     far_ffn, far_normed2, there_box, there_keep, there_out = ffn_kernel(
-        normed2, normed2_t, grad_low, (in_via, in_direct), (out_via, out_direct), units, False
+        normed2, normed2_t, grad_low, (in_via, in_direct), (out_via, out_direct), units, residual
     )
     normed2, there_out, there_box = together(normed2, there_out, there_box)
     out_come, there_come = over_tensor(there_out), over_pair(there_box, 1)
-    own_sums = ffn_kernel(normed2, normed2_t, grad_low, (w_in, w_in), (w_out, w_out), units, True)
+    own_sums = ffn_kernel(
+        normed2, normed2_t, grad_low, (w_in, w_in), (w_out, w_out), units, far_ffn,
+        (counts, far_normed2),
+    )
     own_sums, out_come, there_come = together(own_sums, out_come, there_come)
-    own_ffn, own_normed2, in_box, in_keep, here_out = own_sums
+    output, grad_normed2, in_box, in_keep, here_out = own_sums
     blocks = lax.axis_size("pair")
     split = (blocks // 2, 2, width // blocks, width)
     here_out, out_come = here_out.reshape(split), out_come.reshape(split)
@@ -1316,7 +1340,7 @@
         grad_residual, grad_act, gain_second_grad, bias_second_grad, there_glu, here_glu,
         in_x, in_y, out_z,
     ) = glu_back_kernel(
-        far_normed2, own_normed2, residual, grad_low, value_proj, gate_sig, act, glu_weights, gains,
+        grad_normed2, residual, grad_low, value_proj, gate_sig, act, glu_weights, gains,
         there_keep, there_come, in_box, here_out, out_come,
     )
     halved = (blocks // 2, width // blocks, width)
@@ -1328,11 +1352,10 @@
         skip, gains, gain_second_grad, bias_second_grad, packed, log_dts,
     )
     (
-        output, in_total, out_total, value_total, gate_total,
+        in_total, out_total, value_total, gate_total,
         log_a_grad, freq_grad, real_grad, imag_grad, *vectors,
     ) = last_kernel(
-        counts, residual, far_ffn, own_ffn, in_all.reshape(2, width, -1), out_all.reshape(-1, width),
-        glu_all.reshape(2, width, -1), small,
+        in_all.reshape(2, width, -1), out_all.reshape(-1, width), glu_all.reshape(2, width, -1), small
     )
     log_dt_grad, skip_grad, gain1, bias1, gain2, bias2 = (v.reshape(-1) for v in vectors)
     return (

time: 345 us -> 343 us (level)
  Pallas kernels: 327 us -> 322 us
    pallas_call x1, Pallas kernels: 17.6 us -> 12.5 us  [last_kernel(): pl.pallas_call(functools.partial(last_body, modes=modes), grid=(steps,),...]
where the time goes in v6:
time: 343 us; the launch traced here: 339 us
  Pallas kernels  322 us (94%)
  local copies, waits for them, and re-layouts  7.73 us (2%)
  waiting for transfers between devices  4.18 us (1%)
    pallas_call x1, Pallas kernels, back_kernel(): pl.pallas_call(functools.partial(back_body, bits=bits), in_specs=[hbm] *...  125 us
    pallas_call x2, Pallas kernels, ffn_kernel(): pl.pallas_call(functools.partial(ffn_body, own=owned), grid=(2 * half,),...  82.7 us
    pallas_call x1, Pallas kernels, front_kernel(): pl.pallas_call(functools.partial(front_body, bits=bits), in_specs=[vmem]...  67.7 us
    pallas_call x1, Pallas kernels, glu_back_kernel(): pl.pallas_call(functools.partial(glu_back_body, bits=bits), grid=(chunks...  34.4 us
    pallas_call x1, Pallas kernels, last_kernel(): pl.pallas_call(functools.partial(last_body, modes=modes), grid=(steps,),...  12.5 us
  transfers between devices with their start and end apart: 2, of which 1 were waited for; matrix products, arithmetic and copies ran while one was open for 0% of the time, Pallas kernels for 12%

profile of v6, /device:TPU:0, one launch (start us, length us, event | category | flops | bytes accessed | tf_op | source)
XLA Modules:
  0.0 338.9 jit_solution(16431331703532307510)
XLA Ops:
  1.3 0.7 stack.15
  2.0 0.7 stack.16
  2.7 0.7 stack.17
  3.4 0.7 stack.18
  4.0 0.6 maximum_convert_fusion.gains
  4.7 67.7 %front_kernel.1 = (f32[2,128,256]{2,1,0:T(8,128)}, f32[2,1,256]{2,1,0:T(1,128)}, f32[1,1024]{1,0:T(1,128)}, bf16[1024,1024]{1,0:T(8,128)(2,1)}, bf16[1024,1024]{...) custom-call(bf16[1024,1024]{1,0:T(8,128)(2,1)} %bitcast.32, ...), custom_call_target="tpu_custom_call" | custom-call | tf_op jit(solution)/shard_map/front_kernel/pallas_call | solution.py:509
  72.4 41.2 %ffn_kernel.2 = (f32[1024,1024]{1,0:T(8,128)}, f32[1024,1024]{1,0:T(8,128)}, bf16[512,1024]{1,0:T(8,128)(2,1)}, bf16[512,1024]{1,0:T(8,128)(2,1)}, bf16[1024,1024]{1,0:T(8,128)(2,1)}) custom-call(bf16[1024,1024]{1,0:T(8,128)(2,1)} %get-tuple-element.96.refs_0_, bf16[1024,1024]{1,0:T(8,128)(2,1)} %get-tuple-element.87.refs_1_, ...), custom_call_target="tpu_custom_call" | custom-call | tf_op jit(solution)/shard_map/ffn_kernel/pallas_call | solution.py:846
  113.5 1.6 collective-permute-start
  115.1 0.9 collective-permute-start.1
  116.0 41.6 %ffn_kernel.3 = (bf16[1024,1024]{1,0:T(8,128)(2,1)}, f32[1024,1024]{1,0:T(8,128)}, bf16[512,1024]{1,0:T(8,128)(2,1)}, f32[512,1024]{1,0:T(8,128)}, f32[1024,1024]{1,0:T(8,128)}) custom-call(bf16[1024,1024]{1,0:T(8,128)(2,1)} %get-tuple-element.96.refs_0_, bf16[1024,1024]{1,0:T(8,128)(2,1)} %get-tuple-element.87.refs_1_, ...), custom_call_target="tpu_custom_call" | custom-call | tf_op jit(solution)/shard_map/ffn_kernel/pallas_call | solution.py:846
  157.6 0.0 collective-permute-done.1.there_come
  157.6 0.0 copy-start.3
  157.7 4.2 %collective-permute-done = bf16[1024,1024]{1,0:T(8,128)(2,1)S(1)} collective-permute-done((bf16[1024,1024]{1,0:T(8,128)(2,1)}, bf16[1024,1024]{1,0:T(8,128)(2,1)S(1)}, u32[]{:S(2)}, u32[]{:S(2)}) %collective-permute-start) | collective-permute-done | bytes 2097184 | tf_op jit(solution)/shard_map/ppermute | solution.py:1293
  161.8 0.0 copy-start
  161.8 0.0 copy-done.3
  161.8 1.3 copy-done
  163.2 34.4 %glu_back_kernel.1 = (f32[1024,1024]{1,0:T(8,128)}, f32[1024,1024]{1,0:T(8,128)}, f32[1,1024]{1,0:T(1,128)}, f32[1,1024]{1,0:T(1,128)}, bf16[1024,512]{1,0:T(8,1...) custom-call(f32[1024,1024]{1,0:T(8,128)} %get-tuple-element.107.g_su, ...), custom_call_target="tpu_custom_call" | custom-call | tf_op jit(solution)/shard_map/glu_back_kernel/pallas_call | solution.py:716
  197.6 124.6 %back_kernel.1 = (bf16[1024,1024]{1,0:T(8,128)(2,1)}, bf16[2,8,128,1024]{3,2,1,0:T(8,128)(2,1)}, bf16[2,8,128,1024]{3,2,1,0:T(8,128)(2,1)}, bf16[2,8,128,512]{3,2,1,0:T(8,128)(2,1)}, f32[5,144,256]{2,1,0:T(8,128)}) custom-call(f32[1024,1024]{1,0:T(8,128)} %get-tuple-element.120.ga_hbm, f32[4,1024,256]{2,1,0:T(8,128)} %get-tuple-element.121.mixed_hbm, ...), custom_call_target="tpu_custom_call" | custom-call | tf_op jit(solution)/shard_map/back_kernel/pallas_call | solution.py:1180
  322.2 0.0 copy-start.1
  322.2 12.5 %last_kernel.1 = (f32[1024,2048]{1,0:T(8,128)}, f32[2048,1024]{1,0:T(8,128)}, f32[1024,512]{1,0:T(8,128)}, f32[1024,512]{1,0:T(8,128)}, f32[32,512]{1,0:T(8,128)...) custom-call(bf16[2,1024,1024]{2,1,0:T(8,128)(2,1)} %bitcast.36, ...), custom_call_target="tpu_custom_call" | custom-call | tf_op jit(solution)/shard_map/last_kernel/pallas_call | solution.py:1271
  334.8 0.0 copy-done.1
  334.8 0.0 copy-start.2
  334.8 1.3 copy.38
  336.1 1.0 copy-done.2
  337.1 1.3 copy.39
Async XLA Ops:
  113.5 48.3 %collective-permute-start = (bf16[1024,1024]{1,0:T(8,128)(2,1)}, bf16[1024,1024]{1,0:T(8,128)(2,1)S(1)}, u32[]{:S(2)}, u32[]{:S(2)}) collective-permute-start(bf16[1024,1024]{1,0:T(8,128)(2,1)} %get-tuple-element.104), channel_id=1, source_target_pairs={{0,1},{1,0},{2,3},{3,2},{4,5},{5,4},{6,7},{7,6},{8,9},{9,8},{10,11... | collective-permute-start | bytes 6291464 | tf_op jit(solution)/shard_map/ppermute | solution.py:1293
  115.1 42.5 %collective-permute-start.1 = (bf16[512,1024]{1,0:T(8,128)(2,1)}, bf16[512,1024]{1,0:T(8,128)(2,1)S(1)}, u32[]{:S(2)}, u32[]{:S(2)}) collective-permute-start(bf16[512,1024]{1,0:T(8,128)(2,1)} %get-tuple-element.105), channel_id=1, source_target_pairs={{0,4},{4,0},{8,12},{12,8},{16,20},{20,16},{24,28},{28,24},{1,5},{5... | collective-permute-start | bytes 3145736 | tf_op jit(solution)/shard_map/ppermute | solution.py:1298
  157.6 4.2 %copy-start.3 = (bf16[512,1024]{1,0:T(8,128)(2,1)}, bf16[512,1024]{1,0:T(8,128)(2,1)S(1)}, u32[]{:S(2)}) copy-start(bf16[512,1024]{1,0:T(8,128)(2,1)S(1)} %collective-permute-done.1.there_come) | copy-start | bytes 3145732
  161.8 1.3 copy-start
  322.2 12.6 %copy-start.1 = (bf16[1024,1024]{1,0:T(8,128)(2,1)S(1)}, bf16[1024,1024]{1,0:T(8,128)(2,1)}, u32[]{:S(2)}) copy-start(bf16[1024,1024]{1,0:T(8,128)(2,1)} %get-tuple-element.106) | copy-start | bytes 6291460
  334.8 2.3 copy-start.2

commit v7 on v6

--- a/solution.py
+++ b/solution.py
@@ -265,8 +265,9 @@
     sq = v * v
     th = jnp.tanh(v * (GELU_A + (GELU_A * GELU_B) * sq))
     rise = 0.5 + 0.5 * th
-    slope = rise + v * (0.5 - 0.5 * th * th) * (GELU_A + (3.0 * GELU_A * GELU_B) * sq)
-    return v * rise, slope
+    act = v * rise
+    slope = rise + act * (1.0 - rise) * (2.0 * GELU_A + (6.0 * GELU_A * GELU_B) * sq)
+    return act, slope
 
 
 def gelu(v):

time: 343 us -> 343 us (level)
  no operation moved by 1% of the time
where the time goes in v7:
time: 343 us; the launch traced here: 339 us
  Pallas kernels  323 us (94%)
  local copies, waits for them, and re-layouts  7.73 us (2%)
  waiting for transfers between devices  3.81 us (1%)
    pallas_call x1, Pallas kernels, back_kernel(): pl.pallas_call(functools.partial(back_body, bits=bits), in_specs=[hbm] *...  125 us
    pallas_call x2, Pallas kernels, ffn_kernel(): pl.pallas_call(functools.partial(ffn_body, own=owned), grid=(2 * half,),...  83.6 us
    pallas_call x1, Pallas kernels, front_kernel(): pl.pallas_call(functools.partial(front_body, bits=bits), in_specs=[vmem]...  67.7 us
    pallas_call x1, Pallas kernels, glu_back_kernel(): pl.pallas_call(functools.partial(glu_back_body, bits=bits), grid=(chunks...  34.4 us
    pallas_call x1, Pallas kernels, last_kernel(): pl.pallas_call(functools.partial(last_body, modes=modes), grid=(steps,),...  12.5 us
  transfers between devices with their start and end apart: 2, of which 1 were waited for; matrix products, arithmetic and copies ran while one was open for 0% of the time, Pallas kernels for 12%

profile of v7, /device:TPU:0, one launch (start us, length us, event | category | flops | bytes accessed | tf_op | source)
XLA Modules:
  0.0 339.5 jit_solution(13474350441054725003)
XLA Ops:
  1.3 0.7 stack.15
  2.0 0.7 stack.16
  2.7 0.7 stack.17
  3.4 0.7 stack.18
  4.0 0.6 maximum_convert_fusion.gains
  4.7 67.7 %front_kernel.1 = (f32[2,128,256]{2,1,0:T(8,128)}, f32[2,1,256]{2,1,0:T(1,128)}, f32[1,1024]{1,0:T(1,128)}, bf16[1024,1024]{1,0:T(8,128)(2,1)}, bf16[1024,1024]{...) custom-call(bf16[1024,1024]{1,0:T(8,128)(2,1)} %bitcast.32, ...), custom_call_target="tpu_custom_call" | custom-call | tf_op jit(solution)/shard_map/front_kernel/pallas_call | solution.py:510
  72.4 41.6 %ffn_kernel.2 = (f32[1024,1024]{1,0:T(8,128)}, f32[1024,1024]{1,0:T(8,128)}, bf16[512,1024]{1,0:T(8,128)(2,1)}, bf16[512,1024]{1,0:T(8,128)(2,1)}, bf16[1024,1024]{1,0:T(8,128)(2,1)}) custom-call(bf16[1024,1024]{1,0:T(8,128)(2,1)} %get-tuple-element.96.refs_0_, bf16[1024,1024]{1,0:T(8,128)(2,1)} %get-tuple-element.87.refs_1_, ...), custom_call_target="tpu_custom_call" | custom-call | tf_op jit(solution)/shard_map/ffn_kernel/pallas_call | solution.py:847
  114.0 1.6 collective-permute-start
  115.6 0.9 collective-permute-start.1
  116.5 41.9 %ffn_kernel.3 = (bf16[1024,1024]{1,0:T(8,128)(2,1)}, f32[1024,1024]{1,0:T(8,128)}, bf16[512,1024]{1,0:T(8,128)(2,1)}, f32[512,1024]{1,0:T(8,128)}, f32[1024,1024]{1,0:T(8,128)}) custom-call(bf16[1024,1024]{1,0:T(8,128)(2,1)} %get-tuple-element.96.refs_0_, bf16[1024,1024]{1,0:T(8,128)(2,1)} %get-tuple-element.87.refs_1_, ...), custom_call_target="tpu_custom_call" | custom-call | tf_op jit(solution)/shard_map/ffn_kernel/pallas_call | solution.py:847
  158.5 0.0 collective-permute-done.1.there_come
  158.5 0.0 copy-start.3
  158.5 3.8 %collective-permute-done = bf16[1024,1024]{1,0:T(8,128)(2,1)S(1)} collective-permute-done((bf16[1024,1024]{1,0:T(8,128)(2,1)}, bf16[1024,1024]{1,0:T(8,128)(2,1)S(1)}, u32[]{:S(2)}, u32[]{:S(2)}) %collective-permute-start) | collective-permute-done | bytes 2097184 | tf_op jit(solution)/shard_map/ppermute | solution.py:1294
  162.3 0.0 copy-start
  162.3 0.0 copy-done.3
  162.3 1.3 copy-done
  163.6 34.4 %glu_back_kernel.1 = (f32[1024,1024]{1,0:T(8,128)}, f32[1024,1024]{1,0:T(8,128)}, f32[1,1024]{1,0:T(1,128)}, f32[1,1024]{1,0:T(1,128)}, bf16[1024,512]{1,0:T(8,1...) custom-call(f32[1024,1024]{1,0:T(8,128)} %get-tuple-element.107.g_su, ...), custom_call_target="tpu_custom_call" | custom-call | tf_op jit(solution)/shard_map/glu_back_kernel/pallas_call | solution.py:717
  198.1 124.8 %back_kernel.1 = (bf16[1024,1024]{1,0:T(8,128)(2,1)}, bf16[2,8,128,1024]{3,2,1,0:T(8,128)(2,1)}, bf16[2,8,128,1024]{3,2,1,0:T(8,128)(2,1)}, bf16[2,8,128,512]{3,2,1,0:T(8,128)(2,1)}, f32[5,144,256]{2,1,0:T(8,128)}) custom-call(f32[1024,1024]{1,0:T(8,128)} %get-tuple-element.120.ga_hbm, f32[4,1024,256]{2,1,0:T(8,128)} %get-tuple-element.121.mixed_hbm, ...), custom_call_target="tpu_custom_call" | custom-call | tf_op jit(solution)/shard_map/back_kernel/pallas_call | solution.py:1181
  322.8 0.0 copy-start.1
  322.8 12.5 %last_kernel.1 = (f32[1024,2048]{1,0:T(8,128)}, f32[2048,1024]{1,0:T(8,128)}, f32[1024,512]{1,0:T(8,128)}, f32[1024,512]{1,0:T(8,128)}, f32[32,512]{1,0:T(8,128)...) custom-call(bf16[2,1024,1024]{2,1,0:T(8,128)(2,1)} %bitcast.36, ...), custom_call_target="tpu_custom_call" | custom-call | tf_op jit(solution)/shard_map/last_kernel/pallas_call | solution.py:1272
  335.4 0.0 copy-done.1
  335.4 0.0 copy-start.2
  335.4 1.3 copy.38
  336.7 1.0 copy-done.2
  337.7 1.3 copy.39
Async XLA Ops:
  114.0 48.3 %collective-permute-start = (bf16[1024,1024]{1,0:T(8,128)(2,1)}, bf16[1024,1024]{1,0:T(8,128)(2,1)S(1)}, u32[]{:S(2)}, u32[]{:S(2)}) collective-permute-start(bf16[1024,1024]{1,0:T(8,128)(2,1)} %get-tuple-element.104), channel_id=1, source_target_pairs={{0,1},{1,0},{2,3},{3,2},{4,5},{5,4},{6,7},{7,6},{8,9},{9,8},{10,11... | collective-permute-start | bytes 6291464 | tf_op jit(solution)/shard_map/ppermute | solution.py:1294
  115.6 42.9 %collective-permute-start.1 = (bf16[512,1024]{1,0:T(8,128)(2,1)}, bf16[512,1024]{1,0:T(8,128)(2,1)S(1)}, u32[]{:S(2)}, u32[]{:S(2)}) collective-permute-start(bf16[512,1024]{1,0:T(8,128)(2,1)} %get-tuple-element.105), channel_id=1, source_target_pairs={{0,4},{4,0},{8,12},{12,8},{16,20},{20,16},{24,28},{28,24},{1,5},{5... | collective-permute-start | bytes 3145736 | tf_op jit(solution)/shard_map/ppermute | solution.py:1299
  158.5 3.8 %copy-start.3 = (bf16[512,1024]{1,0:T(8,128)(2,1)}, bf16[512,1024]{1,0:T(8,128)(2,1)S(1)}, u32[]{:S(2)}) copy-start(bf16[512,1024]{1,0:T(8,128)(2,1)S(1)} %collective-permute-done.1.there_come) | copy-start | bytes 3145732
  162.3 1.3 copy-start
  322.8 12.6 %copy-start.1 = (bf16[1024,1024]{1,0:T(8,128)(2,1)S(1)}, bf16[1024,1024]{1,0:T(8,128)(2,1)}, u32[]{:S(2)}) copy-start(bf16[1024,1024]{1,0:T(8,128)(2,1)} %get-tuple-element.106) | copy-start | bytes 6291460
  335.4 2.3 copy-start.2
